TPU v7x, 256 devices: a whole 4x4x8 slice. The times are simulated.
256 devices in a mesh: dp: 64 (over z, x, core), tensor: 4 (over y).
Axes of the slice: x: 4, y: 4, z: 8, core: 2. Of those that a mesh axis runs over, the one named last changes fastest.
Arguments:
- inputs: bfloat16 [65536, 6144], P('dp'), may hold values from -6 to 6
- pre_act: bfloat16 [65536, 1024], P('dp', 'tensor'), may hold values from -6 to 6
- grad_hidden: bfloat16 [65536, 1024], P('dp', 'tensor'), may hold values from -6 to 6
- master: float32 [6144, 1024], P('dp', 'tensor'), may hold values from -0.1875 to 0.1875
- moment_one: float32 [6144, 1024], P('dp', 'tensor'), may hold values from -6 to 6
- moment_two: float32 [6144, 1024], P('dp', 'tensor'), may hold values from 1 to 262144
Outputs:
- grad_input: bfloat16 [65536, 6144], P('dp', 'tensor')
- new_master: float32 [6144, 1024], P('dp', 'tensor')
- new_one: float32 [6144, 1024], P('dp', 'tensor')
- new_two: float32 [6144, 1024], P('dp', 'tensor')
- new_weights: bfloat16 [6144, 1024], P(None, 'tensor')
All inputs are finite; a program needn't handle non-finite values.
Results may differ from a plain program's by a relative error of at most 0.013.
Values may be sent and summed in bfloat16 or wider, within the bound.
No kernel may reach another device: no remote copies, remote signals or barrier semaphores. Data moves between devices by JAX's collectives and lax.ppermute only.
A program may use at most 128 MiB of HBM per device.

v0:
```python
import math

import jax
import jax.numpy as jnp
from jax import lax
from jax.sharding import PartitionSpec as P

QBLOCK = 256
ADAM_STEP = 10


def gelu_slope(value):
    cdf = 0.5 * (1.0 + jax.scipy.special.erf(value / math.sqrt(2.0)))
    pdf = jnp.exp(-0.5 * value * value) / math.sqrt(2.0 * math.pi)
    return cdf + value * pdf


def encode(term):
    rows, cols = term.shape
    blocks = term.reshape(rows, cols // QBLOCK, QBLOCK)
    scale = (jnp.max(jnp.abs(blocks), axis=2) + 1e-06) / 127.0
    codes = jnp.clip(blocks / scale[:, :, None], -127.0, 127.0).astype(jnp.bfloat16)
    return (codes.reshape(rows, cols), scale)


def decode(codes, scale):
    rows, cols = codes.shape
    blocks = codes.astype(jnp.float32).reshape(rows, cols // QBLOCK, QBLOCK)
    return (blocks * scale[:, :, None]).reshape(rows, cols)


def local(inputs, pre_act, grad_hidden, master, moment_one, moment_two):
    act_grad = (grad_hidden.astype(jnp.float32) * gelu_slope(pre_act.astype(jnp.float32))).astype(
        jnp.bfloat16
    )
    weights = master.astype(jnp.bfloat16)
    terms = jnp.einsum(
        "th,dh->td",
        act_grad,
        lax.all_gather(weights, "dp", axis=0, tiled=True),
        preferred_element_type=jnp.float32,
    )
    grad_input = lax.psum_scatter(
        terms.astype(jnp.bfloat16), "tensor", scatter_dimension=1, tiled=True
    )
    term = jnp.einsum("tr,th->rh", inputs, act_grad, preferred_element_type=jnp.float32)
    codes, scale = encode(term)
    grad = lax.psum_scatter(decode(codes, scale), "dp", scatter_dimension=0, tiled=True)
    new_one = 0.9 * moment_one + 0.1 * grad
    new_two = 0.999 * moment_two + 0.001 * grad * grad
    corr_one = 1.0 - 0.9**ADAM_STEP
    corr_two = 1.0 - 0.999**ADAM_STEP
    update = new_one / corr_one / (jnp.sqrt(new_two / corr_two) + 1e-08) + 0.01 * master
    new_master = master - 0.01 * update
    new_weights = lax.all_gather(new_master.astype(jnp.bfloat16), "dp", axis=0, tiled=True)
    return (grad_input, new_master, new_one, new_two, new_weights)


def solution(mesh):
    in_specs = (
        P("dp", None),
        P("dp", "tensor"),
        P("dp", "tensor"),
        P("dp", "tensor"),
        P("dp", "tensor"),
        P("dp", "tensor"),
    )
    out_specs = (
        P("dp", "tensor"),
        P("dp", "tensor"),
        P("dp", "tensor"),
        P("dp", "tensor"),
        P(None, "tensor"),
    )
    return jax.shard_map(local, mesh=mesh, in_specs=in_specs, out_specs=out_specs, check_vma=False)
```

profile of v0, /device:TPU:1, one launch (start us, length us, event | category | flops | bytes accessed | tf_op | source)
XLA Modules:
  0.0 464.7 jit_solution(8532754055390767680)
XLA Ops:
  7.2 0.0 reduce-scatter.7.cloned.1.call-start
  7.2 7.5 %abs_reduce_fusion = (f32[6144]{0:T(1024)S(1)}, f32[256,6144]{1,0:T(8,128)S(1)}) fusion(bf16[1024,6144]{1,0:T(8,128)(2,1)} %param.6, bf16[1024,256]{1,0:T(8,128)(2,1)} %param.7, bf16[1024,256]{1,0:T(8,128)(2,1)} %param.8), kind=kOutput, calls=%fused_computation.3 | convolution fusion | flops 3227510784 | bytes 19947520 | tf_op jit(solution)/shard_map/tr,th->rh/dot_general | solution.py:46
  14.7 3.6 multiply_bitcast_fusion
  18.3 6.6 %copy.30 = f32[6144,256]{1,0:T(8,128)} copy(f32[6144,256]{0,1:T(8,128)} %multiply_bitcast_fusion) | data formatting | bytes 12582912
  24.9 0.0 copy-start.2
  24.9 0.0 copy-start.3
  24.9 0.0 copy-start.4
  24.9 0.0 copy-start
  24.9 0.0 copy-start.1
  24.9 0.0 reduce-scatter.7.cloned.1.call-update
  24.9 0.0 all-gather.3.cloned.1.call-start
  25.0 146.7 %reduce-scatter.7.cloned.1.call-done = f32[96,256]{1,0:T(8,128)} async-done(((f32[6144,256]{1,0:T(8,128)}), f32[96,256]{1,0:T(8,128)}) %reduce-scatter.7.cloned.1.call-update) | async-done | bytes 98320 | tf_op jit(solution)/shard_map/reduce_scatter | solution.py:48
  171.7 0.0 copy-done.2
  171.7 0.0 copy-done.3
  171.7 0.0 copy-done.4
  171.7 1.7 fusion.12
  173.3 0.0 all-gather.3.cloned.1.call-update
  173.4 0.0 all-gather.5.cloned.1.call-start
  173.4 0.7 all-gather.5.cloned.1.call-update
  174.1 0.0 reduce-scatter.5.cloned.1.call-start
  174.1 83.3 %all-gather.3.cloned.1.call-done = bf16[6144,256]{1,0:T(8,128)(2,1)} async-done(((bf16[96,256]{1,0:T(8,128)(2,1)}), bf16[6144,256]{1,0:T(8,128)(2,1)}) %all-gather.3.cloned.1.call-update) | async-done | bytes 3145744 | tf_op jit(solution)/shard_map/all_gather | solution.py:40
  257.4 0.0 copy-done
  257.4 0.0 copy-done.1
  257.4 8.4 %convolution_convert_fusion = bf16[1024,6144]{1,0:T(8,128)(2,1)} fusion(bf16[6144,256]{1,0:T(8,128)(2,1)} %all-gather.3.cloned.1.call-done, bf16[1024,256]{1,0:T(8,128)(2,1)S(1)} %copy-done, bf16[1024,256]{1,0:T(8,128)(2,1)S(1)} %copy-done.1), kind=kOutput, calls=%fused_computation | convolution fusion | flops 3230662656 | bytes 16777216 | tf_op jit(solution)/shard_map/th,dh->td/dot_general | solution.py:37
  265.8 0.0 reduce-scatter.5.cloned.1.call-update
  265.9 71.1 %all-gather.5.cloned.1.call-done = bf16[6144,256]{1,0:T(8,128)(2,1)} async-done(((bf16[96,256]{1,0:T(8,128)(2,1)}), bf16[6144,256]{1,0:T(8,128)(2,1)}) %all-gather.5.cloned.1.call-update) | async-done | bytes 3145744 | tf_op jit(solution)/shard_map/all_gather | solution.py:55
  336.9 117.5 %reduce-scatter.5.cloned.1.call-done = bf16[1024,1536]{1,0:T(8,128)(2,1)} async-done(((bf16[1024,6144]{1,0:T(8,128)(2,1)}), bf16[1024,1536]{1,0:T(8,128)(2,1)}) %reduce-scatter.5.cloned.1.call-update) | async-done | bytes 3145744 | tf_op jit(solution)/shard_map/reduce_scatter | solution.py:43
  454.4 3.8 copy.33
  (1 shorter events, 0.0 us)
Async XLA Ops:
  7.2 164.5 %reduce-scatter.7.cloned.1.call-start = ((), (), s32[]{:S(2)}) async-start(), calls=%async_computation.5 | async-start | bytes 6389760 | tf_op jit(solution)/shard_map/reduce_scatter | solution.py:48
  24.9 146.8 %copy-start.2 = (f32[96,256]{1,0:T(8,128)S(1)}, f32[96,256]{1,0:T(8,128)}, u32[]{:S(2)}) copy-start(f32[96,256]{1,0:T(8,128)} %param.9) | copy-start | bytes 294916
  24.9 146.8 %copy-start.3 = (f32[96,256]{1,0:T(8,128)S(1)}, f32[96,256]{1,0:T(8,128)}, u32[]{:S(2)}) copy-start(f32[96,256]{1,0:T(8,128)} %param.10) | copy-start | bytes 294916
  24.9 146.8 %copy-start.4 = (f32[96,256]{1,0:T(8,128)S(1)}, f32[96,256]{1,0:T(8,128)}, u32[]{:S(2)}) copy-start(f32[96,256]{1,0:T(8,128)} %param.11) | copy-start | bytes 294916
  24.9 232.5 %copy-start = (bf16[1024,256]{1,0:T(8,128)(2,1)S(1)}, bf16[1024,256]{1,0:T(8,128)(2,1)}, u32[]{:S(2)}) copy-start(bf16[1024,256]{1,0:T(8,128)(2,1)} %param.7) | copy-start | bytes 1572868
  24.9 232.5 %copy-start.1 = (bf16[1024,256]{1,0:T(8,128)(2,1)S(1)}, bf16[1024,256]{1,0:T(8,128)(2,1)}, u32[]{:S(2)}) copy-start(bf16[1024,256]{1,0:T(8,128)(2,1)} %param.8) | copy-start | bytes 1572868
  24.9 232.5 %all-gather.3.cloned.1.call-start = ((), (), s32[]{:S(2)}) async-start(), calls=%async_computation.2 | async-start | bytes 3194880 | tf_op jit(solution)/shard_map/all_gather | solution.py:40
  173.4 163.6 %all-gather.5.cloned.1.call-start = ((), (), s32[]{:S(2)}) async-start(), calls=%async_computation.4 | async-start | bytes 3194880 | tf_op jit(solution)/shard_map/all_gather | solution.py:55
  174.1 280.3 %reduce-scatter.5.cloned.1.call-start = ((), (), s32[]{:S(2)}) async-start(), calls=%async_computation.3 | async-start | bytes 15728640 | tf_op jit(solution)/shard_map/reduce_scatter | solution.py:43
Sparse Core Ops, SparseCore 0:
  25.0 146.5 reduce-scatter.6
  175.4 81.9 all-gather.2
  261.1 75.7 all-gather.4
  340.1 114.1 reduce-scatter.4
where the time goes:
time: 465 us
  waiting for transfers between devices  419 us (90%)
  matrix products  15.9 us (3%)
  between operations  13.8 us (3%)
  local copies, waits for them, and re-layouts  10.4 us (2%)
  other arithmetic  5.24 us (1%)
    reduce_scatter x1, waiting for transfers between devices, local(): lax.psum_scatter(decode(codes, scale), 'dp', scatter_dimension=0, tiled=T...  147 us
    reduce_scatter x1, waiting for transfers between devices, local(): lax.psum_scatter(terms.astype(jnp.bfloat16), 'tensor', scatter_dimension=...  117 us
    all_gather x1, waiting for transfers between devices, local(): lax.all_gather(weights, 'dp', axis=0, tiled=True)  83.3 us
    all_gather x1, waiting for transfers between devices, local(): lax.all_gather(new_master.astype(jnp.bfloat16), 'dp', axis=0, tiled=True)  71.1 us
    unnamed x12, local copies, waits for them, and re-layouts  10.4 us
  transfers between devices with their start and end apart: 4, of which 4 were waited for; matrix products, arithmetic and copies ran while one was open for 2% of the time, Pallas kernels for 0%

commit v1 on v0

v1 whole, which is shorter than its diff:
```python
import math

import jax
import jax.numpy as jnp
from jax import lax
from jax.experimental import pallas as pl
from jax.experimental.pallas import tpu as pltpu
from jax.sharding import PartitionSpec as P

ADAM_STEP = 10
NZ, NX, NC, NT = 8, 4, 2, 4
NDP = NZ * NX * NC
TOK = 1024
HID = 256
D = 6144
OWN = D // NDP
ZROWS = D // NZ
HALF = NZ * OWN

BF16 = jnp.bfloat16
F32 = jnp.float32


def dp_index(z, x, c):
    return (z * NX + x) * NC + c


POINTS = [(z, x, c) for z in range(NZ) for x in range(NX) for c in range(NC)]
CORE_SWAP = [(dp_index(z, x, c), dp_index(z, x, 1 - c)) for z, x, c in POINTS]
Z_GROUPS = [[dp_index(z, x, c) for z in range(NZ)] for x in range(NX) for c in range(NC)]
X_GROUPS = [[dp_index(z, x, c) for x in range(NX)] for z in range(NZ) for c in range(NC)]
PLANE = NDP // NT


def x_shift(s):
    return [(dp_index(z, x, c), dp_index(z, (x + s) % NX, c)) for z, x, c in POINTS]


def weight_route():
    pairs = []
    for r in range(NDP):
        for t in range(NT):
            k, j = divmod(r, PLANE)
            c, z = divmod(j, NZ)
            pairs.append((r * NT + t, dp_index(z, t, c) * NT + k))
    return pairs


def gelu_slope(value):
    cdf = 0.5 * (1.0 + jax.scipy.special.erf(value / math.sqrt(2.0)))
    pdf = jnp.exp(-0.5 * value * value) / math.sqrt(2.0 * math.pi)
    return cdf + value * pdf


def term_kernel(place, in_ref, act_ref, keep_ref, send_ref, held):
    x, c = place[0], place[1]
    term = lax.dot_general(
        in_ref[...], act_ref[...], (((0,), (0,)), ((), ())), preferred_element_type=F32
    )
    scale = (jnp.max(jnp.abs(term), axis=1, keepdims=True) + 1e-06) / 127.0
    codes = jnp.clip(term / scale, -127.0, 127.0).astype(BF16)
    held[...] = (codes.astype(F32) * scale).astype(BF16)
    for s in range(NX):
        base = lax.rem(x + s, NX) * (NC * OWN)
        mine = pl.multiple_of(base + c * OWN, OWN)
        other = pl.multiple_of(base + (1 - c) * OWN, OWN)
        keep_ref[s, 0] = held[pl.ds(mine, OWN), :]
        send_ref[s, 0] = held[pl.ds(other, OWN), :]


def make_terms(place, inputs, act_grad):
    out = jax.ShapeDtypeStruct((NX, NZ, OWN, HID), BF16)
    out_spec = pl.BlockSpec((NX, 1, OWN, HID), lambda i, place: (0, i, 0, 0))
    return pl.pallas_call(
        term_kernel,
        grid_spec=pltpu.PrefetchScalarGridSpec(
            num_scalar_prefetch=1,
            grid=(NZ,),
            in_specs=[
                pl.BlockSpec((TOK, ZROWS), lambda i, place: (0, i)),
                pl.BlockSpec((TOK, HID), lambda i, place: (0, 0)),
            ],
            out_specs=[out_spec, out_spec],
            scratch_shapes=[pltpu.VMEM((ZROWS, HID), BF16)],
        ),
        out_shape=[out, out],
        compiler_params=pltpu.CompilerParams(vmem_limit_bytes=40 * 2**20),
        cost_estimate=pl.CostEstimate(
            flops=2 * TOK * D * HID, bytes_accessed=2 * D * (TOK + HID), transcendentals=0
        ),
        name="terms",
    )(place, inputs, act_grad)


GI_ROWS = 256
GI_COLS = D // NT


def input_kernel(place, act_ref, mine_ref, other_ref, out_ref):
    c = place[1]
    for ref, core in ((mine_ref, c), (other_ref, 1 - c)):
        total = jnp.zeros((GI_ROWS, HALF), F32)
        for t in range(NT):
            total += lax.dot_general(
                act_ref[t], ref[t], (((1,), (1,)), ((), ())), preferred_element_type=F32
            )
        out_ref[:, pl.ds(pl.multiple_of(core * HALF, HALF), HALF)] = total.astype(BF16)


def make_grad_input(place, act_all, mine, other):
    whole = pl.BlockSpec((NT, HALF, HID), lambda i, place: (0, 0, 0))
    return pl.pallas_call(
        input_kernel,
        grid_spec=pltpu.PrefetchScalarGridSpec(
            num_scalar_prefetch=1,
            grid=(TOK // GI_ROWS,),
            in_specs=[
                pl.BlockSpec((NT, GI_ROWS, HID), lambda i, place: (0, i, 0)),
                whole,
                whole,
            ],
            out_specs=pl.BlockSpec((GI_ROWS, GI_COLS), lambda i, place: (i, 0)),
        ),
        out_shape=jax.ShapeDtypeStruct((TOK, GI_COLS), BF16),
        compiler_params=pltpu.CompilerParams(vmem_limit_bytes=40 * 2**20),
        cost_estimate=pl.CostEstimate(
            flops=2 * TOK * GI_COLS * HID * NT,
            bytes_accessed=2 * (TOK * HID * NT + GI_COLS * HID * NT + TOK * GI_COLS),
            transcendentals=0,
        ),
        name="grad_input",
    )(place, act_all, mine, other)


def place_kernel(place, *refs):
    pieces, out_ref, sems = refs[: 2 * NX], refs[2 * NX], refs[2 * NX + 1]
    x, c = place[0], place[1]
    copies = []
    for s in range(NX):
        from_x = lax.rem(x + NX - s, NX)
        for side, core in ((0, c), (1, 1 - c)):
            copy = pltpu.make_async_copy(
                pieces[2 * s + side], out_ref.at[:, from_x, core], sems.at[2 * s + side]
            )
            copy.start()
            copies.append(copy)
    for copy in copies:
        copy.wait()


def make_weights(place, pieces):
    anywhere = pl.BlockSpec(memory_space=pl.ANY)
    out = pl.pallas_call(
        place_kernel,
        in_specs=[pl.BlockSpec(memory_space=pltpu.SMEM)] + [anywhere] * (2 * NX),
        out_specs=anywhere,
        out_shape=jax.ShapeDtypeStruct((NZ, NX, NC, OWN, HID), BF16),
        scratch_shapes=[pltpu.SemaphoreType.DMA((2 * NX,))],
        name="place",
    )(place, *pieces)
    return out.reshape(D, HID)


def local(inputs, pre_act, grad_hidden, master, moment_one, moment_two):
    rank = lax.axis_index("dp")
    place = jnp.stack([lax.rem(lax.div(rank, NC), NX), lax.rem(rank, NC)]).astype(jnp.int32)

    act_grad = (grad_hidden.astype(F32) * gelu_slope(pre_act.astype(F32))).astype(BF16)
    act_all = lax.all_gather(act_grad, "tensor", axis=0)
    w_own = lax.ppermute(master.astype(BF16), ("dp", "tensor"), weight_route())

    keep, send = make_terms(place, inputs, act_grad)
    recv = lax.ppermute(send, "dp", CORE_SWAP)
    sums = [(keep[s].astype(F32) + recv[s].astype(F32)).astype(BF16) for s in range(NX)]
    parts = [lax.ppermute(sums[s], "dp", x_shift(s)) for s in range(1, NX)]

    w_own, _ = lax.optimization_barrier((w_own, sums[NX - 1]))
    w_z = lax.all_to_all(
        jnp.broadcast_to(w_own[None], (NZ, OWN, HID)),
        "dp",
        split_axis=0,
        concat_axis=0,
        axis_index_groups=Z_GROUPS,
        tiled=True,
    )
    w_mine = lax.all_gather(w_z.reshape(HALF, HID), "dp", axis=0, axis_index_groups=X_GROUPS)

    total = sums[0].astype(F32)
    for part in parts:
        total += part.astype(F32)
    blocks = lax.all_to_all(
        total.astype(BF16),
        "dp",
        split_axis=0,
        concat_axis=0,
        axis_index_groups=Z_GROUPS,
        tiled=True,
    )
    grad = jnp.sum(blocks.astype(F32), axis=0)

    new_one = 0.9 * moment_one + 0.1 * grad
    new_two = 0.999 * moment_two + 0.001 * grad * grad
    corr_one = 1.0 - 0.9**ADAM_STEP
    corr_two = 1.0 - 0.999**ADAM_STEP
    update = new_one / corr_one / (jnp.sqrt(new_two / corr_two) + 1e-08) + 0.01 * master
    new_master = master - 0.01 * update

    n_z = lax.all_to_all(
        jnp.broadcast_to(new_master.astype(BF16)[None], (NZ, OWN, HID)),
        "dp",
        split_axis=0,
        concat_axis=0,
        axis_index_groups=Z_GROUPS,
        tiled=True,
    )
    mine = [n_z] + [lax.ppermute(n_z, "dp", x_shift(s)) for s in range(1, NX)]
    other = [lax.ppermute(piece, "dp", CORE_SWAP) for piece in mine]
    new_weights = make_weights(place, [p for pair in zip(mine, other) for p in pair])

    w_other = lax.ppermute(w_mine, "dp", CORE_SWAP)
    grad_input = make_grad_input(place, act_all, w_mine, w_other)
    return (grad_input, new_master, new_one, new_two, new_weights)


def solution(mesh):
    shard = P("dp", "tensor")
    return jax.shard_map(
        local,
        mesh=mesh,
        in_specs=(P("dp", None), shard, shard, shard, shard, shard),
        out_specs=(shard, shard, shard, shard, P(None, "tensor")),
        check_vma=False,
    )
```

time: 465 us -> 282 us (0.61)
  waiting for transfers between devices: 419 us -> 60.8 us
  Pallas kernels: 0 us -> 113 us
  blocking collectives: 0 us -> 62.3 us
  starting transfers between devices: 0.16 us -> 25.2 us
  matrix products: 15.9 us -> 0 us
  local copies, waits for them, and re-layouts: 10.4 us -> 2.67 us
    reduce_scatter x2 -> x0, waiting for transfers between devices: 264 us -> none  [the longest x1 147 us: local(): lax.psum_scatter(decode(codes, scale), 'dp', scatter_dimension=0, tiled=T...]
    all_gather x2, waiting for transfers between devices: 154 us -> 27.4 us  [the longest x1 27.4 us: local(): lax.all_gather(w_z.reshape(HALF, HID), 'dp', axis=0, axis_index_groups=X_...]
    pallas_call x0 -> x3, Pallas kernels: none -> 113 us  [the longest x1 97.1 us: make_weights(): pl.pallas_call(place_kernel, in_specs=[pl.BlockSpec(memory_space=pltpu.SM...]
    all_to_all x0 -> x3, blocking collectives: none -> 62.3 us  [the longest x1 21.7 us: local(): lax.all_to_all(jnp.broadcast_to(new_master.astype(BF16)[None], (NZ, OWN,...]
    ppermute x0 -> x13, waiting for transfers between devices: none -> 32.7 us  [the longest x3 19.8 us: local(): parts = [lax.ppermute(sums[s], 'dp', x_shift(s)) for s in range(1, NX)]]
    ppermute x0 -> x13, starting transfers between devices: none -> 25.2 us  [the longest x4 11.4 us: local(): other = [lax.ppermute(piece, 'dp', CORE_SWAP) for piece in mine]]
    dot_general x2 -> x0, matrix products: 15.9 us -> none  [the longest x1 8.43 us: local(): jnp.einsum('th,dh->td', act_grad, lax.all_gather(weights, 'dp', axis=0, t...]
    unnamed x12 -> x30, local copies, waits for them, and re-layouts: 10.4 us -> 2.62 us
  transfers between devices with their start and end apart: 4 -> 15, of which waited for: 4 -> 9; matrix products, arithmetic and copies ran while one was open for 2% -> 0% of each run, Pallas kernels for 0% -> 34%
where the time goes in v1:
time: 282 us
  Pallas kernels  113 us (40%)
  blocking collectives  62.3 us (22%)
  waiting for transfers between devices  60.8 us (22%)
  starting transfers between devices  25.2 us (9%)
  between operations  14.2 us (5%)
  other arithmetic  3.23 us (1%)
    pallas_call x1, Pallas kernels, make_weights(): pl.pallas_call(place_kernel, in_specs=[pl.BlockSpec(memory_space=pltpu.SM...  97.1 us
    all_gather x1, waiting for transfers between devices, local(): lax.all_gather(w_z.reshape(HALF, HID), 'dp', axis=0, axis_index_groups=X_...  27.4 us
    all_to_all x1, blocking collectives, local(): lax.all_to_all(jnp.broadcast_to(new_master.astype(BF16)[None], (NZ, OWN,...  21.7 us
    all_to_all x1, blocking collectives, local(): lax.all_to_all(total.astype(BF16), 'dp', split_axis=0, concat_axis=0, axi...  21.5 us
    ppermute x3, waiting for transfers between devices, local(): parts = [lax.ppermute(sums[s], 'dp', x_shift(s)) for s in range(1, NX)]  19.8 us
    all_to_all x1, blocking collectives, local(): lax.all_to_all(jnp.broadcast_to(w_own[None], (NZ, OWN, HID)), 'dp', split...  19.1 us
    ppermute x4, starting transfers between devices, local(): other = [lax.ppermute(piece, 'dp', CORE_SWAP) for piece in mine]  11.4 us
    pallas_call x1, Pallas kernels, make_terms(): pl.pallas_call(term_kernel, grid_spec=pltpu.PrefetchScalarGridSpec(num_sc...  10.5 us
  transfers between devices with their start and end apart: 15, of which 9 were waited for; matrix products, arithmetic and copies ran while one was open for 0% of the time, Pallas kernels for 34%

profile of v1, /device:TPU:1, one launch (start us, length us, event | category | flops | bytes accessed | tf_op | source)
XLA Modules:
  0.0 281.8 jit_solution(1567510114187409870)
XLA Ops:
  7.2 0.0 all-gather.4.cloned.1.call-start
  7.2 0.1 pad_add_fusion.place
  7.3 1.7 fusion.7.act_ref
  9.0 0.0 copy-start
  9.0 10.5 %terms.1 = (bf16[4,8,96,256]{3,2,1,0:T(8,128)(2,1)S(1)}, bf16[4,8,96,256]{3,2,1,0:T(8,128)(2,1)S(1)}) custom-call(s32[2]{0:T(128)S(1)} %pad_add_fusion.place, bf16[1024,6144]{1,0:T(8,128)(2,1)} %in_ref.1, bf16[1024,256]{1,0:T(8,128)(2,1)S(1)} %fusion.7.act_ref), custom_call_target="tpu_custom_call" | custom-call | flops 3221225472 | bytes 15728640 | tf_op jit(solution)/shard_map/terms/pallas_call | solution.py:74
  19.6 3.3 %collective-permute-start.1 = (bf16[4,8,96,256]{3,2,1,0:T(8,128)(2,1)S(1)}, bf16[4,8,96,256]{3,2,1,0:T(8,128)(2,1)S(1)}, u32[]{:S(2)}, u32[]{:S(2)}) collective-permute-start(bf16[4,8,96,256]{3,2,1,0:T(8,128)(2,1)S(1)} %get-tuple-element.9), channel_id=1, source_target_pairs={{0,4},{4,0},{8,12},{12,8},{16,20},{20,16},{24,28},{28,24},{32,36},... | collective-permute-start | bytes 4718600 | tf_op jit(solution)/shard_map/ppermute | solution.py:173
  22.9 3.0 %collective-permute-done.1 = bf16[4,8,96,256]{3,2,1,0:T(8,128)(2,1)S(1)} collective-permute-done((bf16[4,8,96,256]{3,2,1,0:T(8,128)(2,1)S(1)}, bf16[4,8,96,256]{3,2,1,0:T(8,128)(2,1)S(1)}, u32[]{:S(2)}, u32[]{:S(2)}) %collective-permute-start.1) | collective-permute-done | bytes 1572896 | tf_op jit(solution)/shard_map/ppermute | solution.py:173
  25.9 0.4 fusion.13
  26.3 0.8 collective-permute-start.5
  27.1 0.5 collective-permute-start.4
  27.7 0.6 collective-permute-start.3
  28.3 8.4 %collective-permute-done.5 = bf16[8,96,256]{2,1,0:T(8,128)(2,1)S(1)} collective-permute-done((bf16[8,96,256]{2,1,0:T(8,128)(2,1)S(1)}, bf16[8,96,256]{2,1,0:T(8,128)(2,1)S(1)}, u32[]{:S(2)}, u32[]{:S(2)}) %collective-permute-start.5) | collective-permute-done | bytes 393248 | tf_op jit(solution)/shard_map/ppermute | solution.py:175
  36.7 2.0 collective-permute-done.4
  38.7 9.4 %collective-permute-done.3 = bf16[8,96,256]{2,1,0:T(8,128)(2,1)S(1)} collective-permute-done((bf16[8,96,256]{2,1,0:T(8,128)(2,1)S(1)}, bf16[8,96,256]{2,1,0:T(8,128)(2,1)S(1)}, u32[]{:S(2)}, u32[]{:S(2)}) %collective-permute-start.3) | collective-permute-done | bytes 393248 | tf_op jit(solution)/shard_map/ppermute | solution.py:175
  48.1 0.3 fusion.10
  48.4 21.5 %all_to_all.15 = bf16[8,96,256]{2,1,0:T(8,128)(2,1)S(1)} all-to-all(bf16[8,96,256]{2,1,0:T(8,128)(2,1)S(1)} %fusion.10), channel_id=1, replica_groups={{0,32,64,96,128,160,192,224},{4,36,68,100,132,164,196,228},{8,40,72,104..., dimensions={0} | all-to-all | bytes 786432 | tf_op jit(solution)/shard_map/all_to_all | solution.py:191
  69.9 0.1 convert_reduce_fusion
  69.9 0.8 fusion.16
  70.7 4.2 %collective-permute-start = (bf16[96,256]{1,0:T(8,128)(2,1)S(1)}, bf16[96,256]{1,0:T(8,128)(2,1)S(1)}, u32[]{:S(2)}, u32[]{:S(2)}) collective-permute-start(bf16[96,256]{1,0:T(8,128)(2,1)S(1)} %get-tuple-element.18), channel_id=1, source_target_pairs={{0,0},{1,8},{2,16},{3,24},{4,32},{5,40},{6,48},{7,56},{8,64},{9,72... | collective-permute-start | bytes 147464 | tf_op jit(solution)/shard_map/ppermute | solution.py:170
  74.9 1.8 collective-permute-done
  76.7 19.1 %all_to_all.16 = bf16[8,96,256]{2,1,0:T(8,128)(2,1)} all-to-all(bf16[8,96,256]{2,1,0:T(8,128)(2,1)S(1)} %broadcast_in_dim.4), channel_id=1, replica_groups={{0,32,64,96,128,160,192,224},{4,36,68,100,132,164,196,228},{8,40,72,104..., dimensions={0} | all-to-all | bytes 786432 | tf_op jit(solution)/shard_map/all_to_all | solution.py:178
  95.8 0.0 all-gather.4.cloned.1.call-update
  95.8 0.0 all-gather.6.cloned.1.call-start
  95.8 0.7 all-gather.6.cloned.1.call-update
  96.5 27.4 %all-gather.4.cloned.1.call-done.mine_ref = bf16[4,768,256]{2,1,0:T(8,128)(2,1)} async-done(((bf16[1,768,256]{2,1,0:T(8,128)(2,1)}), bf16[4,768,256]{2,1,0:T(8,128)(2,1)}) %all-gather.4.cloned.1.call-update) | async-done | bytes 1572880 | tf_op jit(solution)/shard_map/all_gather | solution.py:186
  123.9 0.7 collective-permute-start.2
  124.6 21.7 %all_to_all.17.refs_0_ = bf16[8,96,256]{2,1,0:T(8,128)(2,1)S(1)} all-to-all(bf16[8,96,256]{2,1,0:T(8,128)(2,1)S(1)} %broadcast_in_dim.5), channel_id=1, replica_groups={{0,32,64,96,128,160,192,224},{4,36,68,100,132,164,196,228},{8,40,72,104..., dimensions={0} | all-to-all | bytes 786432 | tf_op jit(solution)/shard_map/all_to_all | solution.py:208
  146.3 0.2 collective-permute-start.7
  146.5 2.4 collective-permute-start.9
  148.9 1.1 collective-permute-start.11
  149.9 1.3 collective-permute-start.6
  151.2 6.8 %collective-permute-done.7.refs_2_ = bf16[8,96,256]{2,1,0:T(8,128)(2,1)S(1)} collective-permute-done((bf16[8,96,256]{2,1,0:T(8,128)(2,1)S(1)}, bf16[8,96,256]{2,1,0:T(8,128)(2,1)S(1)}, u32[]{:S(2)}, u32[]{:S(2)}) %collective-permute-start.7) | collective-permute-done | bytes 393248 | tf_op jit(solution)/shard_map/ppermute | solution.py:216
  158.0 9.5 %collective-permute-start.8 = (bf16[8,96,256]{2,1,0:T(8,128)(2,1)S(1)}, bf16[8,96,256]{2,1,0:T(8,128)(2,1)S(1)}, u32[]{:S(2)}, u32[]{:S(2)}) collective-permute-start(bf16[8,96,256]{2,1,0:T(8,128)(2,1)S(1)} %collective-permute-done.7.refs_2_), channel_id=1, source_target_pairs={{0,4},{4,0},{8,12},{12,8},{16,20},{20,16},{24,28},{28,24},{32,36},... | collective-permute-start | bytes 1179656 | tf_op jit(solution)/shard_map/ppermute | solution.py:217
  167.5 0.0 collective-permute-done.9.refs_4_
  167.5 0.1 collective-permute-start.10
  167.6 0.0 collective-permute-done.11.refs_6_
  167.6 0.5 collective-permute-start.12
  168.1 0.0 collective-permute-done.6.refs_1_
  168.1 0.7 collective-permute-done.8.refs_3_
  168.8 0.6 collective-permute-done.10.refs_5_
  169.4 0.2 copy-done.10
  169.6 0.8 copy-done.11
  170.4 0.0 collective-permute-done.12.refs_7_
  170.4 97.1 %place.1 = bf16[8,4,2,96,256]{4,3,2,1,0:T(8,128)(2,1)} custom-call(s32[2]{0:T(128)} %copy-done.1, bf16[8,96,256]{2,1,0:T(8,128)(2,1)} %copy-done.5, bf16[8,96,256]{2,1,0:T(8,128)(2,1)} %copy-done.9, bf16[8,96,256]{2,1,0:T(8,128)(2,1)} %copy-done.6, bf16[8,96,256]{2,1,0:T(8,128)(2,1)} %copy-done.10, bf16[8,96,256]{2,1,0:T(8,128)(2,1)} %copy-done.7, ...), custom_call_target="tpu_custom_call" | custom-call | tf_op jit(solution)/shard_map/place/pallas_call | solution.py:153
  267.5 0.0 all-gather.6.cloned.1.call-done
  267.6 0.0 collective-permute-done.2.other_ref
  267.6 1.6 copy-done.3
  269.2 5.8 %grad_input.1 = bf16[1024,1536]{1,0:T(8,128)(2,1)} custom-call(s32[2]{0:T(128)S(1)} %copy-done.2, bf16[4,1024,256]{2,1,0:T(8,128)(2,1)S(1)} %bitcast.16, bf16[4,768,256]{2,1,0:T(8,128)(2,1)S(1)} %copy-done.4, bf16[4,768,256]{2,1,0:T(8,128)(2,1)S(1)} %collective-permute-done.2.other_ref), custom_call_target="tpu_custom_call" | custom-call | flops 3221225472 | bytes 8388608 | tf_op jit(solution)/shard_map/grad_input/pallas_call | solution.py:112
  (28 shorter events, 0.1 us)
Async XLA Ops:
  7.2 116.7 %all-gather.4.cloned.1.call-start = ((), (), s32[]{:S(2)}) async-start(), calls=%async_computation.3 | async-start | bytes 1966080 | tf_op jit(solution)/shard_map/all_gather | solution.py:186
  7.3 12.2 %copy-start.1 = (s32[2]{0:T(128)}, s32[2]{0:T(128)S(1)}, u32[]{:S(2)}) copy-start(s32[2]{0:T(128)S(1)} %pad_add_fusion.place) | copy-start | bytes 28
  9.0 10.5 %copy-start = (bf16[1024,256]{1,0:T(8,128)(2,1)}, bf16[1024,256]{1,0:T(8,128)(2,1)S(1)}, u32[]{:S(2)}) copy-start(bf16[1024,256]{1,0:T(8,128)(2,1)S(1)} %fusion.7.act_ref) | copy-start | bytes 1572868
  19.6 6.4 %collective-permute-start.1 = (bf16[4,8,96,256]{3,2,1,0:T(8,128)(2,1)S(1)}, bf16[4,8,96,256]{3,2,1,0:T(8,128)(2,1)S(1)}, u32[]{:S(2)}, u32[]{:S(2)}) collective-permute-start(bf16[4,8,96,256]{3,2,1,0:T(8,128)(2,1)S(1)} %get-tuple-element.9), channel_id=1, source_target_pairs={{0,4},{4,0},{8,12},{12,8},{16,20},{20,16},{24,28},{28,24},{32,36},... | collective-permute-start | bytes 4718600 | tf_op jit(solution)/shard_map/ppermute | solution.py:173
  26.3 10.4 %collective-permute-start.5 = (bf16[8,96,256]{2,1,0:T(8,128)(2,1)S(1)}, bf16[8,96,256]{2,1,0:T(8,128)(2,1)S(1)}, u32[]{:S(2)}, u32[]{:S(2)}) collective-permute-start(bf16[8,96,256]{2,1,0:T(8,128)(2,1)S(1)} %get-tuple-element.17), channel_id=1, source_target_pairs={{0,24},{4,28},{8,0},{12,4},{16,8},{20,12},{24,16},{28,20},{32,56},... | collective-permute-start | bytes 1179656 | tf_op jit(solution)/shard_map/ppermute | solution.py:175
  27.1 11.6 %collective-permute-start.4 = (bf16[8,96,256]{2,1,0:T(8,128)(2,1)S(1)}, bf16[8,96,256]{2,1,0:T(8,128)(2,1)S(1)}, u32[]{:S(2)}, u32[]{:S(2)}) collective-permute-start(bf16[8,96,256]{2,1,0:T(8,128)(2,1)S(1)} %get-tuple-element.16), channel_id=1, source_target_pairs={{0,16},{4,20},{8,24},{12,28},{16,0},{20,4},{24,8},{28,12},{32,48},... | collective-permute-start | bytes 1179656 | tf_op jit(solution)/shard_map/ppermute | solution.py:175
  27.7 42.3 %copy-start.12 = (f32[96,256]{1,0:T(8,128)S(1)}, f32[96,256]{1,0:T(8,128)}, u32[]{:S(2)}) copy-start(f32[96,256]{1,0:T(8,128)} %param.9) | copy-start | bytes 294916
  27.7 42.3 %copy-start.13 = (f32[96,256]{1,0:T(8,128)S(1)}, f32[96,256]{1,0:T(8,128)}, u32[]{:S(2)}) copy-start(f32[96,256]{1,0:T(8,128)} %param.10) | copy-start | bytes 294916
  27.7 42.3 %copy-start.14 = (f32[96,256]{1,0:T(8,128)S(1)}, f32[96,256]{1,0:T(8,128)}, u32[]{:S(2)}) copy-start(f32[96,256]{1,0:T(8,128)} %param.11) | copy-start | bytes 294916
  27.7 20.4 %collective-permute-start.3 = (bf16[8,96,256]{2,1,0:T(8,128)(2,1)S(1)}, bf16[8,96,256]{2,1,0:T(8,128)(2,1)S(1)}, u32[]{:S(2)}, u32[]{:S(2)}) collective-permute-start(bf16[8,96,256]{2,1,0:T(8,128)(2,1)S(1)} %get-tuple-element.15), channel_id=1, source_target_pairs={{0,8},{4,12},{8,16},{12,20},{16,24},{20,28},{24,0},{28,4},{32,40},... | collective-permute-start | bytes 1179656 | tf_op jit(solution)/shard_map/ppermute | solution.py:175
  70.7 6.0 %collective-permute-start = (bf16[96,256]{1,0:T(8,128)(2,1)S(1)}, bf16[96,256]{1,0:T(8,128)(2,1)S(1)}, u32[]{:S(2)}, u32[]{:S(2)}) collective-permute-start(bf16[96,256]{1,0:T(8,128)(2,1)S(1)} %get-tuple-element.18), channel_id=1, source_target_pairs={{0,0},{1,8},{2,16},{3,24},{4,32},{5,40},{6,48},{7,56},{8,64},{9,72... | collective-permute-start | bytes 147464 | tf_op jit(solution)/shard_map/ppermute | solution.py:170
  95.8 171.8 %all-gather.6.cloned.1.call-start = ((), (), s32[]{:S(2)}) async-start(), calls=%async_computation.4 | async-start | bytes 2621440 | tf_op jit(solution)/shard_map/all_gather | solution.py:169
  123.9 143.7 %collective-permute-start.2 = (bf16[4,768,256]{2,1,0:T(8,128)(2,1)}, bf16[4,768,256]{2,1,0:T(8,128)(2,1)S(1)}, u32[]{:S(2)}, u32[]{:S(2)}) collective-permute-start(bf16[4,768,256]{2,1,0:T(8,128)(2,1)} %all-gather.4.cloned.1.call-done.mine_ref), channel_id=1, source_target_pairs={{0,4},{4,0},{8,12},{12,8},{16,20},{20,16},{24,28},{28,24},{32,36},... | collective-permute-start | bytes 4718600 | tf_op jit(solution)/shard_map/ppermute | solution.py:220
  146.3 24.1 %copy-start.5 = (bf16[8,96,256]{2,1,0:T(8,128)(2,1)}, bf16[8,96,256]{2,1,0:T(8,128)(2,1)S(1)}, u32[]{:S(2)}) copy-start(bf16[8,96,256]{2,1,0:T(8,128)(2,1)S(1)} %all_to_all.17.refs_0_) | copy-start | bytes 1179652
  146.3 121.3 %copy-start.2 = (s32[2]{0:T(128)S(1)}, s32[2]{0:T(128)}, u32[]{:S(2)}) copy-start(s32[2]{0:T(128)} %copy-done.1) | copy-start | bytes 28
  146.3 121.3 %copy-start.4 = (bf16[4,768,256]{2,1,0:T(8,128)(2,1)S(1)}, bf16[4,768,256]{2,1,0:T(8,128)(2,1)}, u32[]{:S(2)}) copy-start(bf16[4,768,256]{2,1,0:T(8,128)(2,1)} %all-gather.4.cloned.1.call-done.mine_ref) | copy-start | bytes 4718596
  146.3 11.7 %collective-permute-start.7 = (bf16[8,96,256]{2,1,0:T(8,128)(2,1)S(1)}, bf16[8,96,256]{2,1,0:T(8,128)(2,1)S(1)}, u32[]{:S(2)}, u32[]{:S(2)}) collective-permute-start(bf16[8,96,256]{2,1,0:T(8,128)(2,1)S(1)} %all_to_all.17.refs_0_), channel_id=1, source_target_pairs={{0,8},{4,12},{8,16},{12,20},{16,24},{20,28},{24,0},{28,4},{32,40},... | collective-permute-start | bytes 1179656 | tf_op jit(solution)/shard_map/ppermute | solution.py:216
  146.5 21.0 %collective-permute-start.9 = (bf16[8,96,256]{2,1,0:T(8,128)(2,1)S(1)}, bf16[8,96,256]{2,1,0:T(8,128)(2,1)S(1)}, u32[]{:S(2)}, u32[]{:S(2)}) collective-permute-start(bf16[8,96,256]{2,1,0:T(8,128)(2,1)S(1)} %all_to_all.17.refs_0_), channel_id=1, source_target_pairs={{0,16},{4,20},{8,24},{12,28},{16,0},{20,4},{24,8},{28,12},{32,48},... | collective-permute-start | bytes 1179656 | tf_op jit(solution)/shard_map/ppermute | solution.py:216
  148.9 18.7 %collective-permute-start.11 = (bf16[8,96,256]{2,1,0:T(8,128)(2,1)S(1)}, bf16[8,96,256]{2,1,0:T(8,128)(2,1)S(1)}, u32[]{:S(2)}, u32[]{:S(2)}) collective-permute-start(bf16[8,96,256]{2,1,0:T(8,128)(2,1)S(1)} %all_to_all.17.refs_0_), channel_id=1, source_target_pairs={{0,24},{4,28},{8,0},{12,4},{16,8},{20,12},{24,16},{28,20},{32,56},... | collective-permute-start | bytes 1179656 | tf_op jit(solution)/shard_map/ppermute | solution.py:216
  149.9 18.2 %collective-permute-start.6 = (bf16[8,96,256]{2,1,0:T(8,128)(2,1)S(1)}, bf16[8,96,256]{2,1,0:T(8,128)(2,1)S(1)}, u32[]{:S(2)}, u32[]{:S(2)}) collective-permute-start(bf16[8,96,256]{2,1,0:T(8,128)(2,1)S(1)} %all_to_all.17.refs_0_), channel_id=1, source_target_pairs={{0,4},{4,0},{8,12},{12,8},{16,20},{20,16},{24,28},{28,24},{32,36},... | collective-permute-start | bytes 1179656 | tf_op jit(solution)/shard_map/ppermute | solution.py:217
  158.0 10.1 %copy-start.6 = (bf16[8,96,256]{2,1,0:T(8,128)(2,1)}, bf16[8,96,256]{2,1,0:T(8,128)(2,1)S(1)}, u32[]{:S(2)}) copy-start(bf16[8,96,256]{2,1,0:T(8,128)(2,1)S(1)} %collective-permute-done.7.refs_2_) | copy-start | bytes 1179652
  158.0 10.9 %collective-permute-start.8 = (bf16[8,96,256]{2,1,0:T(8,128)(2,1)S(1)}, bf16[8,96,256]{2,1,0:T(8,128)(2,1)S(1)}, u32[]{:S(2)}, u32[]{:S(2)}) collective-permute-start(bf16[8,96,256]{2,1,0:T(8,128)(2,1)S(1)} %collective-permute-done.7.refs_2_), channel_id=1, source_target_pairs={{0,4},{4,0},{8,12},{12,8},{16,20},{20,16},{24,28},{28,24},{32,36},... | collective-permute-start | bytes 1179656 | tf_op jit(solution)/shard_map/ppermute | solution.py:217
  167.5 1.3 copy-start.7
  167.5 1.9 collective-permute-start.10
  167.6 1.8 copy-start.8
  167.6 2.8 collective-permute-start.12
  168.1 1.3 copy-start.9
  168.8 0.8 copy-start.10
  169.6 0.8 copy-start.11
  267.6 1.6 copy-start.3
Sparse Core Ops, SparseCore 0:
  95.9 27.9 all-gather.3
  126.3 33.5 all-gather.5

commit v2 on v1

v2 whole, which is shorter than its diff:
```python
import math

import jax
import jax.numpy as jnp
from jax import lax
from jax.experimental import pallas as pl
from jax.experimental.pallas import tpu as pltpu
from jax.sharding import PartitionSpec as P

ADAM_STEP = 10
NZ, NX, NC, NT = 8, 4, 2, 4
NDP = NZ * NX * NC
TOK = 1024
HID = 256
D = 6144
OWN = D // NDP
ZROWS = D // NZ
HALF = NZ * OWN

BF16 = jnp.bfloat16
F32 = jnp.float32


def dp_index(z, x, c):
    return (z * NX + x) * NC + c


POINTS = [(z, x, c) for z in range(NZ) for x in range(NX) for c in range(NC)]
CORE_SWAP = [(dp_index(z, x, c), dp_index(z, x, 1 - c)) for z, x, c in POINTS]
Z_GROUPS = [[dp_index(z, x, c) for z in range(NZ)] for x in range(NX) for c in range(NC)]
X_GROUPS = [[dp_index(z, x, c) for x in range(NX)] for z in range(NZ) for c in range(NC)]
PLANE = NDP // NT


def x_shift(s):
    return [(dp_index(z, x, c), dp_index(z, (x + s) % NX, c)) for z, x, c in POINTS]


def z_shift(s):
    return [(dp_index(z, x, c), dp_index((z + s) % NZ, x, c)) for z, x, c in POINTS]


def y_shift(s):
    return [(t, (t + s) % NT) for t in range(NT)]


def weight_route():
    pairs = []
    for r in range(NDP):
        for t in range(NT):
            k, j = divmod(r, PLANE)
            c, z = divmod(j, NZ)
            pairs.append((r * NT + t, dp_index(z, (t - k) % NX, c) * NT + k))
    return pairs


def gelu_slope(value):
    cdf = 0.5 * (1.0 + lax.erf(value * (1.0 / math.sqrt(2.0))))
    pdf = jnp.exp(-0.5 * value * value) * (1.0 / math.sqrt(2.0 * math.pi))
    return cdf + value * pdf


def term_kernel(
    place, pre_hbm, cot_hbm, in_ref, keep_ref, send_ref, act_ref, pre_ref, cot_ref, held, made, sems
):
    x, c = place[0], place[1]

    def fetch(i):
        columns = pl.ds(pl.multiple_of(i * ZROWS, ZROWS), ZROWS)
        return pltpu.make_async_copy(in_ref.at[:, columns], held.at[i], sems.at[i])

    pre_copy = pltpu.make_async_copy(pre_hbm, pre_ref, sems.at[NZ])
    cot_copy = pltpu.make_async_copy(cot_hbm, cot_ref, sems.at[NZ + 1])
    pre_copy.start()
    cot_copy.start()
    for i in range(NZ):
        fetch(i).start()
    pre_copy.wait()
    cot_copy.wait()
    slope = gelu_slope(pre_ref[...].astype(F32))
    act_ref[...] = (cot_ref[...].astype(F32) * slope).astype(BF16)

    @pl.loop(0, NZ)
    def _(i):
        fetch(i).wait()
        term = lax.dot_general(
            held[i], act_ref[...], (((0,), (0,)), ((), ())), preferred_element_type=F32
        )
        scale = (jnp.max(jnp.abs(term), axis=1, keepdims=True) + 1e-06) / 127.0
        codes = jnp.clip(term * (1.0 / scale), -127.0, 127.0).astype(BF16)
        made[...] = (codes.astype(F32) * scale).astype(BF16)
        for s in range(NX):
            base = lax.rem(x + s, NX) * (NC * OWN)
            mine = pl.multiple_of(base + c * OWN, OWN)
            other = pl.multiple_of(base + (1 - c) * OWN, OWN)
            keep_ref[s, i] = made[pl.ds(mine, OWN), :]
            send_ref[s, i] = made[pl.ds(other, OWN), :]


def make_terms(place, pre_act, grad_hidden, inputs):
    out = jax.ShapeDtypeStruct((NX, NZ, OWN, HID), BF16)
    vmem = pl.BlockSpec(memory_space=pltpu.VMEM)
    return pl.pallas_call(
        term_kernel,
        in_specs=[
            pl.BlockSpec(memory_space=pltpu.SMEM),
            pl.BlockSpec(memory_space=pltpu.HBM),
            pl.BlockSpec(memory_space=pltpu.HBM),
            pl.BlockSpec(memory_space=pltpu.HBM),
        ],
        out_specs=[vmem, vmem, vmem],
        out_shape=[out, out, jax.ShapeDtypeStruct((TOK, HID), BF16)],
        scratch_shapes=[
            pltpu.VMEM((TOK, HID), BF16),
            pltpu.VMEM((TOK, HID), BF16),
            pltpu.VMEM((NZ, TOK, ZROWS), BF16),
            pltpu.VMEM((ZROWS, HID), BF16),
            pltpu.SemaphoreType.DMA((NZ + 2,)),
        ],
        compiler_params=pltpu.CompilerParams(vmem_limit_bytes=40 * 2**20),
        cost_estimate=pl.CostEstimate(
            flops=2 * TOK * D * HID, bytes_accessed=2 * D * (TOK + HID), transcendentals=0
        ),
        name="terms",
    )(place, pre_act, grad_hidden, inputs)


GI_ROWS = 256
GI_COLS = D // NT


def input_kernel(place, *refs):
    x, c, z = place[0], place[1], place[2]
    act_refs, mine_refs, other_refs = refs[:NT], refs[NT : NT + NX], refs[NT + NX : NT + 2 * NX]
    out_ref, acts, weights = refs[NT + 2 * NX :]

    @pl.when(pl.program_id(0) == 0)
    def _():
        for s in range(NX):
            for i in range(NZ):
                j = lax.rem(z + NZ - i, NZ)
                weights[s, i * OWN : (i + 1) * OWN] = mine_refs[s][j]
                weights[NX + s, i * OWN : (i + 1) * OWN] = other_refs[s][j]

    for j in range(NT):
        acts[j] = act_refs[j][...]
    for side, core in ((0, c), (1, 1 - c)):
        total = jnp.zeros((GI_ROWS, HALF), F32)
        for s in range(NX):
            total += lax.dot_general(
                acts[lax.rem(s + NT - x, NT)],
                weights[side * NX + s],
                (((1,), (1,)), ((), ())),
                preferred_element_type=F32,
            )
        out_ref[:, pl.ds(pl.multiple_of(core * HALF, HALF), HALF)] = total.astype(BF16)


def make_grad_input(place, act_all, mine, other):
    whole = pl.BlockSpec((NZ, OWN, HID), lambda i, place: (0, 0, 0))
    return pl.pallas_call(
        input_kernel,
        grid_spec=pltpu.PrefetchScalarGridSpec(
            num_scalar_prefetch=1,
            grid=(TOK // GI_ROWS,),
            in_specs=[pl.BlockSpec((GI_ROWS, HID), lambda i, place: (i, 0))] * NT
            + [whole] * (2 * NX),
            out_specs=pl.BlockSpec((GI_ROWS, GI_COLS), lambda i, place: (i, 0)),
            scratch_shapes=[
                pltpu.VMEM((NT, GI_ROWS, HID), BF16),
                pltpu.VMEM((2 * NX, HALF, HID), BF16),
            ],
        ),
        out_shape=jax.ShapeDtypeStruct((TOK, GI_COLS), BF16),
        compiler_params=pltpu.CompilerParams(vmem_limit_bytes=40 * 2**20),
        cost_estimate=pl.CostEstimate(
            flops=2 * TOK * GI_COLS * HID * NT,
            bytes_accessed=2 * (TOK * HID * NT + GI_COLS * HID * NT + TOK * GI_COLS),
            transcendentals=0,
        ),
        name="grad_input",
    )(place, *act_all, *mine, *other)


def place_kernel(place, *refs):
    pieces, out_ref, sems = refs[: 2 * NX], refs[2 * NX], refs[2 * NX + 1]
    x, c = place[0], place[1]
    copies = []
    for s in range(NX):
        from_x = lax.rem(x + NX - s, NX)
        for side, core in ((0, c), (1, 1 - c)):
            copy = pltpu.make_async_copy(
                pieces[2 * s + side], out_ref.at[:, from_x, core], sems.at[2 * s + side]
            )
            copy.start()
            copies.append(copy)
    for copy in copies:
        copy.wait()


def make_weights(place, pieces):
    anywhere = pl.BlockSpec(memory_space=pl.ANY)
    out = pl.pallas_call(
        place_kernel,
        in_specs=[pl.BlockSpec(memory_space=pltpu.SMEM)]
        + [pl.BlockSpec(memory_space=pltpu.VMEM)] * (2 * NX),
        out_specs=anywhere,
        out_shape=jax.ShapeDtypeStruct((NZ, NX, NC, OWN, HID), BF16),
        scratch_shapes=[pltpu.SemaphoreType.DMA((2 * NX,))],
        compiler_params=pltpu.CompilerParams(vmem_limit_bytes=40 * 2**20),
        name="place",
    )(place, *pieces)
    return out.reshape(D, HID)


def swap_all_z(block):
    return lax.all_to_all(
        block, "dp", split_axis=0, concat_axis=0, axis_index_groups=Z_GROUPS, tiled=True
    )


def tie(*arrays):
    return lax.optimization_barrier(arrays)


def local(inputs, pre_act, grad_hidden, master, moment_one, moment_two):
    rank = lax.axis_index("dp")
    at_z, at_x = lax.div(rank, NX * NC), lax.rem(lax.div(rank, NC), NX)
    place = jnp.stack([at_x, lax.rem(rank, NC), at_z]).astype(jnp.int32)

    w_own = lax.ppermute(master.astype(BF16), ("dp", "tensor"), weight_route())
    keep, send, act_grad = make_terms(place, pre_act, grad_hidden, inputs)
    send, w_own = tie(send, w_own)

    recv = lax.ppermute(send, "dp", CORE_SWAP)
    sums = [(keep[s].astype(F32) + recv[s].astype(F32)).astype(BF16) for s in range(NX)]
    w_own, *sums = tie(w_own, *sums)
    parts = [lax.ppermute(sums[s], "dp", x_shift(s)) for s in range(1, NX)]
    w_z = [w_own] + [lax.ppermute(w_own, "dp", z_shift(s)) for s in range(1, NZ)]
    *parts, w_mine = tie(*parts, jnp.stack(w_z))
    total = sums[0].astype(F32)
    for part in parts:
        total += part.astype(F32)

    acts = [act_grad] + [lax.ppermute(act_grad, "tensor", y_shift(s)) for s in range(1, NT)]
    w_mine = [w_mine] + [lax.ppermute(w_mine, "dp", x_shift(s)) for s in range(1, NX)]
    blocks = swap_all_z(total.astype(BF16))
    blocks, acts[1], acts[3], w_mine[1], w_mine[3] = tie(
        blocks, acts[1], acts[3], w_mine[1], w_mine[3]
    )
    grad = jnp.sum(blocks.astype(F32), axis=0)

    new_one = 0.9 * moment_one + 0.1 * grad
    new_two = 0.999 * moment_two + 0.001 * grad * grad
    corr_one = 1.0 - 0.9**ADAM_STEP
    corr_two = 1.0 - 0.999**ADAM_STEP
    update = new_one / corr_one / (jnp.sqrt(new_two / corr_two) + 1e-08) + 0.01 * master
    new_master = master - 0.01 * update

    n_z = swap_all_z(jnp.broadcast_to(new_master.astype(BF16)[None], (NZ, OWN, HID)))
    n_z, acts[2], w_mine[2] = tie(n_z, acts[2], w_mine[2])
    w_other = [lax.ppermute(piece, "dp", CORE_SWAP) for piece in w_mine]
    mine = [n_z] + [lax.ppermute(n_z, "dp", x_shift(s)) for s in range(1, NX)]
    grad_input = make_grad_input(place, acts, w_mine, w_other)
    grad_input, *mine[1:] = tie(grad_input, *mine[1:])
    other = [lax.ppermute(piece, "dp", CORE_SWAP) for piece in mine]
    new_weights = make_weights(place, [p for pair in zip(mine, other) for p in pair])
    return (grad_input, new_master, new_one, new_two, new_weights)


def solution(mesh):
    shard = P("dp", "tensor")
    return jax.shard_map(
        local,
        mesh=mesh,
        in_specs=(P("dp", None), shard, shard, shard, shard, shard),
        out_specs=(shard, shard, shard, shard, P(None, "tensor")),
        check_vma=False,
    )
```

time: 282 us -> 132 us (0.47)
  Pallas kernels: 113 us -> 17.9 us
  blocking collectives: 62.3 us -> 0 us
  starting transfers between devices: 25.2 us -> 62.4 us
  waiting for transfers between devices: 60.8 us -> 43.9 us
  between operations: 14.2 us -> 0.99 us
    pallas_call x1, Pallas kernels: 97.1 us -> 2.27 us  [make_weights(): pl.pallas_call(place_kernel, in_specs=[pl.BlockSpec(memory_space=pltpu.SM...]
    all_to_all x3 -> x0, blocking collectives: 62.3 us -> none  [the longest x1 21.7 us: local(): lax.all_to_all(jnp.broadcast_to(new_master.astype(BF16)[None], (NZ, OWN,...]
    ppermute x1 -> x17, starting transfers between devices: 0.67 us -> 36.4 us  [the longest x7 18.9 us: local(): lax.ppermute(w_own, 'dp', z_shift(s))]
    all_gather x2 -> x0, waiting for transfers between devices: 27.4 us -> none  [the longest x1 27.4 us: local(): lax.all_gather(w_z.reshape(HALF, HID), 'dp', axis=0, axis_index_groups=X_...]
    ppermute x1 -> x17, waiting for transfers between devices: 0.01 us -> 13.4 us  [the longest x3 11.2 us: local(): lax.ppermute(act_grad, 'tensor', y_shift(s))]
    all_to_all x0 -> x2, starting transfers between devices: none -> 9.74 us  [swap_all_z(): lax.all_to_all(block, 'dp', split_axis=0, concat_axis=0, axis_index_group...]
    ppermute x4, starting transfers between devices: 11.4 us -> 2.11 us  [local(): other = [lax.ppermute(piece, 'dp', CORE_SWAP) for piece in mine]]
    ppermute x3, waiting for transfers between devices: 19.8 us -> 15.7 us  [local(): parts = [lax.ppermute(sums[s], 'dp', x_shift(s)) for s in range(1, NX)]]
  transfers between devices with their start and end apart: 15 -> 31, of which waited for: 9 -> 13; matrix products, arithmetic and copies ran while one was open for 0% -> 0% of each run, Pallas kernels for 34% -> 12%
where the time goes in v2:
time: 132 us; the launch traced here: 131 us
  starting transfers between devices  62.4 us (47%)
  waiting for transfers between devices  43.9 us (33%)
  Pallas kernels  17.9 us (14%)
  other arithmetic  3.31 us (3%)
  local copies, waits for them, and re-layouts  2.91 us (2%)
    ppermute x7, starting transfers between devices, local(): lax.ppermute(w_own, 'dp', z_shift(s))  18.9 us
    ppermute x3, waiting for transfers between devices, local(): parts = [lax.ppermute(sums[s], 'dp', x_shift(s)) for s in range(1, NX)]  15.7 us
    ppermute x3, waiting for transfers between devices, local(): lax.ppermute(act_grad, 'tensor', y_shift(s))  11.2 us
    all_to_all x2, starting transfers between devices, swap_all_z(): lax.all_to_all(block, 'dp', split_axis=0, concat_axis=0, axis_index_group...  9.74 us
    ppermute x3, waiting for transfers between devices, local(): mine = [n_z] + [lax.ppermute(n_z, 'dp', x_shift(s)) for s in range(1, NX)]  9.44 us
    pallas_call x1, Pallas kernels, make_terms(): pl.pallas_call(term_kernel, in_specs=[pl.BlockSpec(memory_space=pltpu.SME...  8.19 us
    ppermute x4, starting transfers between devices, local(): w_other = [lax.ppermute(piece, 'dp', CORE_SWAP) for piece in w_mine]  7.52 us
    pallas_call x1, Pallas kernels, make_grad_input(): pl.pallas_call(input_kernel, grid_spec=pltpu.PrefetchScalarGridSpec(num_s...  7.43 us
  transfers between devices with their start and end apart: 31, of which 13 were waited for; matrix products, arithmetic and copies ran while one was open for 0% of the time, Pallas kernels for 12%

profile of v2, /device:TPU:1, one launch (start us, length us, event | category | flops | bytes accessed | tf_op | source)
XLA Modules:
  0.0 131.4 jit_solution(14087209900784087887)
XLA Ops:
  0.6 0.9 convert_element_type.80
  1.5 4.9 %collective-permute-start = (bf16[96,256]{1,0:T(8,128)(2,1)S(1)}, bf16[96,256]{1,0:T(8,128)(2,1)S(1)}, u32[]{:S(2)}, u32[]{:S(2)}) collective-permute-start(bf16[96,256]{1,0:T(8,128)(2,1)S(1)} %convert_element_type.80), channel_id=1, source_target_pairs={{0,0},{1,8},{2,16},{3,24},{4,32},{5,40},{6,48},{7,56},{8,64},{9,72... | collective-permute-start | bytes 147464 | tf_op jit(solution)/shard_map/ppermute | solution.py:231
  6.6 1.0 copy-done
  7.6 1.0 copy-done.1
  8.6 8.2 %terms.1 = (bf16[4,8,96,256]{3,2,1,0:T(8,128)(2,1)S(1)}, bf16[4,8,96,256]{3,2,1,0:T(8,128)(2,1)S(1)}, bf16[1024,256]{1,0:T(8,128)(2,1)S(1)}) custom-call(s32[3]{0:T(128)S(1)} %pad_add_fusion.place, bf16[1024,256]{1,0:T(8,128)(2,1)S(1)} %copy-done, bf16[1024,256]{1,0:T(8,128)(2,1)S(1)} %copy-done.1, bf16[1024,6144]{1,0:T(8,128)(2,1)} %in_ref.1), custom_call_target="tpu_custom_call" | custom-call | flops 3221225472 | bytes 15728640 | tf_op jit(solution)/shard_map/terms/pallas_call | solution.py:103
  16.8 0.1 collective-permute-start.1
  16.9 3.4 %collective-permute-done.1 = bf16[4,8,96,256]{3,2,1,0:T(8,128)(2,1)S(1)} collective-permute-done((bf16[4,8,96,256]{3,2,1,0:T(8,128)(2,1)S(1)}, bf16[4,8,96,256]{3,2,1,0:T(8,128)(2,1)S(1)}, u32[]{:S(2)}, u32[]{:S(2)}) %collective-permute-start.1) | collective-permute-done | bytes 1572896 | tf_op jit(solution)/shard_map/ppermute | solution.py:235
  20.3 0.6 fusion.3
  20.9 0.1 collective-permute-start.5
  21.0 5.0 %collective-permute-start.6 = (bf16[96,256]{1,0:T(8,128)(2,1)S(1)}, bf16[96,256]{1,0:T(8,128)(2,1)S(1)}, u32[]{:S(2)}, u32[]{:S(2)}) collective-permute-start(bf16[96,256]{1,0:T(8,128)(2,1)S(1)} %collective-permute-done), channel_id=1, source_target_pairs={{0,64},{4,68},{8,72},{12,76},{16,80},{20,84},{24,88},{28,92},{32,9... | collective-permute-start | bytes 147464 | tf_op jit(solution)/shard_map/ppermute | solution.py:239
  26.0 5.0 %collective-permute-start.7 = (bf16[96,256]{1,0:T(8,128)(2,1)S(1)}, bf16[96,256]{1,0:T(8,128)(2,1)S(1)}, u32[]{:S(2)}, u32[]{:S(2)}) collective-permute-start(bf16[96,256]{1,0:T(8,128)(2,1)S(1)} %collective-permute-done), channel_id=1, source_target_pairs={{0,96},{4,100},{8,104},{12,108},{16,112},{20,116},{24,120},{28,124... | collective-permute-start | bytes 147464 | tf_op jit(solution)/shard_map/ppermute | solution.py:239
  31.1 4.4 %collective-permute-start.9 = (bf16[96,256]{1,0:T(8,128)(2,1)S(1)}, bf16[96,256]{1,0:T(8,128)(2,1)S(1)}, u32[]{:S(2)}, u32[]{:S(2)}) collective-permute-start(bf16[96,256]{1,0:T(8,128)(2,1)S(1)} %collective-permute-done), channel_id=1, source_target_pairs={{0,160},{4,164},{8,168},{12,172},{16,176},{20,180},{24,184},{28,18... | collective-permute-start | bytes 147464 | tf_op jit(solution)/shard_map/ppermute | solution.py:239
  35.4 3.5 %collective-permute-start.10 = (bf16[96,256]{1,0:T(8,128)(2,1)S(1)}, bf16[96,256]{1,0:T(8,128)(2,1)S(1)}, u32[]{:S(2)}, u32[]{:S(2)}) collective-permute-start(bf16[96,256]{1,0:T(8,128)(2,1)S(1)} %collective-permute-done), channel_id=1, source_target_pairs={{0,192},{4,196},{8,200},{12,204},{16,208},{20,212},{24,216},{28,22... | collective-permute-start | bytes 147464 | tf_op jit(solution)/shard_map/ppermute | solution.py:239
  39.0 0.9 collective-permute-start.11
  39.9 0.7 collective-permute-start.2
  40.6 3.7 %collective-permute-start.3 = (bf16[8,96,256]{2,1,0:T(8,128)(2,1)S(1)}, bf16[8,96,256]{2,1,0:T(8,128)(2,1)S(1)}, u32[]{:S(2)}, u32[]{:S(2)}) collective-permute-start(bf16[8,96,256]{2,1,0:T(8,128)(2,1)S(1)} %get-tuple-element.38), channel_id=1, source_target_pairs={{0,16},{4,20},{8,24},{12,28},{16,0},{20,4},{24,8},{28,12},{32,48},... | collective-permute-start | bytes 1179656 | tf_op jit(solution)/shard_map/ppermute | solution.py:238
  44.4 0.5 collective-permute-done.11
  44.9 5.4 %collective-permute-done.2 = bf16[8,96,256]{2,1,0:T(8,128)(2,1)S(1)} collective-permute-done((bf16[8,96,256]{2,1,0:T(8,128)(2,1)S(1)}, bf16[8,96,256]{2,1,0:T(8,128)(2,1)S(1)}, u32[]{:S(2)}, u32[]{:S(2)}) %collective-permute-start.2) | collective-permute-done | bytes 393248 | tf_op jit(solution)/shard_map/ppermute | solution.py:238
  50.3 9.3 %collective-permute-done.3 = bf16[8,96,256]{2,1,0:T(8,128)(2,1)S(1)} collective-permute-done((bf16[8,96,256]{2,1,0:T(8,128)(2,1)S(1)}, bf16[8,96,256]{2,1,0:T(8,128)(2,1)S(1)}, u32[]{:S(2)}, u32[]{:S(2)}) %collective-permute-start.3) | collective-permute-done | bytes 393248 | tf_op jit(solution)/shard_map/ppermute | solution.py:238
  59.6 1.0 collective-permute-done.4
  60.7 1.0 add_convert_fusion
  61.6 3.5 %all-to-all-start = ((bf16[8,96,256]{2,1,0:T(8,128)(2,1)}), bf16[8,96,256]{2,1,0:T(8,128)(2,1)S(1)}, u32[]{:S(2)}, u32[]{:S(2)}) async-start(bf16[8,96,256]{2,1,0:T(8,128)(2,1)} %add_convert_fusion), calls=%async_computation | async-start | bytes 786432 | tf_op jit(solution)/shard_map/all_to_all | solution.py:217
  65.2 2.8 %collective-permute-start.13 = (bf16[1024,256]{1,0:T(8,128)(2,1)S(1)}, bf16[1024,256]{1,0:T(8,128)(2,1)S(1)}, u32[]{:S(2)}, u32[]{:S(2)}) collective-permute-start(bf16[1024,256]{1,0:T(8,128)(2,1)S(1)} %get-tuple-element.31.refs_0_), channel_id=1, source_target_pairs={{0,3},{1,0},{2,1},{3,2},{4,7},{5,4},{6,5},{7,6},{8,11},{9,8},{10,9... | collective-permute-start | bytes 1572872 | tf_op jit(solution)/shard_map/ppermute | solution.py:245
  68.0 2.2 %collective-permute-start.14 = (bf16[8,96,256]{2,1,0:T(8,128)(2,1)S(1)}, bf16[8,96,256]{2,1,0:T(8,128)(2,1)S(1)}, u32[]{:S(2)}, u32[]{:S(2)}) collective-permute-start(bf16[8,96,256]{2,1,0:T(8,128)(2,1)S(1)} %bitcast_dynamic-update-slice_fusion.refs_4_), channel_id=1, source_target_pairs={{0,8},{4,12},{8,16},{12,20},{16,24},{20,28},{24,0},{28,4},{32,40},... | collective-permute-start | bytes 1179656 | tf_op jit(solution)/shard_map/ppermute | solution.py:246
  70.2 1.3 collective-permute-start.15
  71.4 6.5 %collective-permute-done.12.refs_1_ = bf16[1024,256]{1,0:T(8,128)(2,1)S(1)} collective-permute-done((bf16[1024,256]{1,0:T(8,128)(2,1)S(1)}, bf16[1024,256]{1,0:T(8,128)(2,1)S(1)}, u32[]{:S(2)}, u32[]{:S(2)}) %collective-permute-start.12) | collective-permute-done | bytes 524320 | tf_op jit(solution)/shard_map/ppermute | solution.py:245
  78.0 0.9 collective-permute-done.14.refs_5_
  78.9 0.6 collective-permute-done.15.refs_7_
  79.6 0.7 fusion.5
  80.4 0.8 broadcast_in_dim.2
  81.2 6.3 %all-to-all-start.1 = ((bf16[8,96,256]{2,1,0:T(8,128)(2,1)}), bf16[8,96,256]{2,1,0:T(8,128)(2,1)S(1)}, u32[]{:S(2)}, u32[]{:S(2)}) async-start(bf16[8,96,256]{2,1,0:T(8,128)(2,1)} %broadcast_in_dim.2), calls=%async_computation.1 | async-start | bytes 786432 | tf_op jit(solution)/shard_map/all_to_all | solution.py:217
  87.5 1.1 collective-permute-start.16
  88.5 2.6 %collective-permute-start.17 = (bf16[8,96,256]{2,1,0:T(8,128)(2,1)S(1)}, bf16[8,96,256]{2,1,0:T(8,128)(2,1)}, u32[]{:S(2)}, u32[]{:S(2)}) collective-permute-start(bf16[8,96,256]{2,1,0:T(8,128)(2,1)S(1)} %bitcast_dynamic-update-slice_fusion.refs_4_), channel_id=1, source_target_pairs={{0,16},{4,20},{8,24},{12,28},{16,0},{20,4},{24,8},{28,12},{32,48},... | collective-permute-start | bytes 1179656 | tf_op jit(solution)/shard_map/ppermute | solution.py:246
  91.1 3.4 %collective-permute-start.18 = (bf16[8,96,256]{2,1,0:T(8,128)(2,1)S(1)}, bf16[8,96,256]{2,1,0:T(8,128)(2,1)}, u32[]{:S(2)}, u32[]{:S(2)}) collective-permute-start(bf16[8,96,256]{2,1,0:T(8,128)(2,1)S(1)} %bitcast_dynamic-update-slice_fusion.refs_4_), channel_id=1, source_target_pairs={{0,4},{4,0},{8,12},{12,8},{16,20},{20,16},{24,28},{28,24},{32,36},... | collective-permute-start | bytes 1179656 | tf_op jit(solution)/shard_map/ppermute | solution.py:262
  94.4 0.5 collective-permute-start.21
  95.0 4.7 %collective-permute-done.16.refs_2_ = bf16[1024,256]{1,0:T(8,128)(2,1)S(1)} collective-permute-done((bf16[1024,256]{1,0:T(8,128)(2,1)S(1)}, bf16[1024,256]{1,0:T(8,128)(2,1)S(1)}, u32[]{:S(2)}, u32[]{:S(2)}) %collective-permute-start.16) | collective-permute-done | bytes 524320 | tf_op jit(solution)/shard_map/ppermute | solution.py:245
  99.7 3.6 %collective-permute-start.20 = (bf16[8,96,256]{2,1,0:T(8,128)(2,1)}, bf16[8,96,256]{2,1,0:T(8,128)(2,1)S(1)}, u32[]{:S(2)}, u32[]{:S(2)}) collective-permute-start(bf16[8,96,256]{2,1,0:T(8,128)(2,1)} %collective-permute-done.17.refs_6_), channel_id=1, source_target_pairs={{0,4},{4,0},{8,12},{12,8},{16,20},{20,16},{24,28},{28,24},{32,36},... | collective-permute-start | bytes 1179656 | tf_op jit(solution)/shard_map/ppermute | solution.py:262
  103.3 2.1 %collective-permute-start.22 = (bf16[8,96,256]{2,1,0:T(8,128)(2,1)S(1)}, bf16[8,96,256]{2,1,0:T(8,128)(2,1)S(1)}, u32[]{:S(2)}, u32[]{:S(2)}) collective-permute-start(bf16[8,96,256]{2,1,0:T(8,128)(2,1)S(1)} %all-to-all-done.1.refs_0_), channel_id=1, source_target_pairs={{0,8},{4,12},{8,16},{12,20},{16,24},{20,28},{24,0},{28,4},{32,40},... | collective-permute-start | bytes 1179656 | tf_op jit(solution)/shard_map/ppermute | solution.py:263
  105.5 2.5 %collective-permute-start.23 = (bf16[8,96,256]{2,1,0:T(8,128)(2,1)S(1)}, bf16[8,96,256]{2,1,0:T(8,128)(2,1)S(1)}, u32[]{:S(2)}, u32[]{:S(2)}) collective-permute-start(bf16[8,96,256]{2,1,0:T(8,128)(2,1)S(1)} %all-to-all-done.1.refs_0_), channel_id=1, source_target_pairs={{0,16},{4,20},{8,24},{12,28},{16,0},{20,4},{24,8},{28,12},{32,48},... | collective-permute-start | bytes 1179656 | tf_op jit(solution)/shard_map/ppermute | solution.py:263
  108.0 0.7 collective-permute-start.25
  108.7 7.4 %grad_input.1 = bf16[1024,1536]{1,0:T(8,128)(2,1)} custom-call(s32[3]{0:T(128)S(1)} %pad_add_fusion.place, bf16[1024,256]{1,0:T(8,128)(2,1)S(1)} %get-tuple-element.31.refs_0_, bf16[1024,256]{1,0:T(8,128)(2,1)S(1)} %collective-permute-done.12.refs_1_, bf16[1024,256]{1,0:T(8,128)(2,1)S(1)} %collective-permute-done.16.refs_2_, ...), custom_call_target="tpu_custom_call" | custom-call | flops 3221225472 | bytes 8388608 | tf_op jit(solution)/shard_map/grad_input/pallas_call | solution.py:161
  116.2 9.4 %collective-permute-done.23.refs_4_ = bf16[8,96,256]{2,1,0:T(8,128)(2,1)S(1)} collective-permute-done((bf16[8,96,256]{2,1,0:T(8,128)(2,1)S(1)}, bf16[8,96,256]{2,1,0:T(8,128)(2,1)S(1)}, u32[]{:S(2)}, u32[]{:S(2)}) %collective-permute-start.23) | collective-permute-done | bytes 393248 | tf_op jit(solution)/shard_map/ppermute | solution.py:263
  125.6 0.9 collective-permute-start.26
  126.5 0.5 collective-permute-start.28
  127.0 0.8 collective-permute-done.26.refs_3_
  127.8 0.6 collective-permute-done.27.refs_5_
  128.4 0.6 collective-permute-done.28.refs_7_
  129.0 2.3 %place.1 = bf16[8,4,2,96,256]{4,3,2,1,0:T(8,128)(2,1)} custom-call(s32[3]{0:T(128)S(1)} %pad_add_fusion.place, bf16[8,96,256]{2,1,0:T(8,128)(2,1)S(1)} %all-to-all-done.1.refs_0_, bf16[8,96,256]{2,1,0:T(8,128)(2,1)S(1)} %collective-permute-done.25.refs_1_, bf16[8,96,256]{2,1,0:T(8,128)(2,1)S(1)} %collective-permute-done.22.refs_2_, ...), custom_call_target="tpu_custom_call" | custom-call | tf_op jit(solution)/shard_map/place/pallas_call | solution.py:203
  (42 shorter events, 0.5 us)
Async XLA Ops:
  1.5 15.3 %collective-permute-start = (bf16[96,256]{1,0:T(8,128)(2,1)S(1)}, bf16[96,256]{1,0:T(8,128)(2,1)S(1)}, u32[]{:S(2)}, u32[]{:S(2)}) collective-permute-start(bf16[96,256]{1,0:T(8,128)(2,1)S(1)} %convert_element_type.80), channel_id=1, source_target_pairs={{0,0},{1,8},{2,16},{3,24},{4,32},{5,40},{6,48},{7,56},{8,64},{9,72... | collective-permute-start | bytes 147464 | tf_op jit(solution)/shard_map/ppermute | solution.py:231
  6.6 1.0 copy-start
  7.6 1.0 copy-start.1
  16.8 3.5 %collective-permute-start.1 = (bf16[4,8,96,256]{3,2,1,0:T(8,128)(2,1)S(1)}, bf16[4,8,96,256]{3,2,1,0:T(8,128)(2,1)S(1)}, u32[]{:S(2)}, u32[]{:S(2)}) collective-permute-start(bf16[4,8,96,256]{3,2,1,0:T(8,128)(2,1)S(1)} %get-tuple-element.35), channel_id=1, source_target_pairs={{0,4},{4,0},{8,12},{12,8},{16,20},{20,16},{24,28},{28,24},{32,36},... | collective-permute-start | bytes 4718600 | tf_op jit(solution)/shard_map/ppermute | solution.py:235
  20.9 14.5 %collective-permute-start.5 = (bf16[96,256]{1,0:T(8,128)(2,1)S(1)}, bf16[96,256]{1,0:T(8,128)(2,1)S(1)}, u32[]{:S(2)}, u32[]{:S(2)}) collective-permute-start(bf16[96,256]{1,0:T(8,128)(2,1)S(1)} %collective-permute-done), channel_id=1, source_target_pairs={{0,32},{4,36},{8,40},{12,44},{16,48},{20,52},{24,56},{28,60},{32,6... | collective-permute-start | bytes 147464 | tf_op jit(solution)/shard_map/ppermute | solution.py:239
  21.0 17.9 %collective-permute-start.6 = (bf16[96,256]{1,0:T(8,128)(2,1)S(1)}, bf16[96,256]{1,0:T(8,128)(2,1)S(1)}, u32[]{:S(2)}, u32[]{:S(2)}) collective-permute-start(bf16[96,256]{1,0:T(8,128)(2,1)S(1)} %collective-permute-done), channel_id=1, source_target_pairs={{0,64},{4,68},{8,72},{12,76},{16,80},{20,84},{24,88},{28,92},{32,9... | collective-permute-start | bytes 147464 | tf_op jit(solution)/shard_map/ppermute | solution.py:239
  26.0 13.9 %collective-permute-start.7 = (bf16[96,256]{1,0:T(8,128)(2,1)S(1)}, bf16[96,256]{1,0:T(8,128)(2,1)S(1)}, u32[]{:S(2)}, u32[]{:S(2)}) collective-permute-start(bf16[96,256]{1,0:T(8,128)(2,1)S(1)} %collective-permute-done), channel_id=1, source_target_pairs={{0,96},{4,100},{8,104},{12,108},{16,112},{20,116},{24,120},{28,124... | collective-permute-start | bytes 147464 | tf_op jit(solution)/shard_map/ppermute | solution.py:239
  31.0 9.6 %collective-permute-start.8 = (bf16[96,256]{1,0:T(8,128)(2,1)S(1)}, bf16[96,256]{1,0:T(8,128)(2,1)S(1)}, u32[]{:S(2)}, u32[]{:S(2)}) collective-permute-start(bf16[96,256]{1,0:T(8,128)(2,1)S(1)} %collective-permute-done), channel_id=1, source_target_pairs={{0,128},{4,132},{8,136},{12,140},{16,144},{20,148},{24,152},{28,15... | collective-permute-start | bytes 147464 | tf_op jit(solution)/shard_map/ppermute | solution.py:239
  31.1 13.2 %collective-permute-start.9 = (bf16[96,256]{1,0:T(8,128)(2,1)S(1)}, bf16[96,256]{1,0:T(8,128)(2,1)S(1)}, u32[]{:S(2)}, u32[]{:S(2)}) collective-permute-start(bf16[96,256]{1,0:T(8,128)(2,1)S(1)} %collective-permute-done), channel_id=1, source_target_pairs={{0,160},{4,164},{8,168},{12,172},{16,176},{20,180},{24,184},{28,18... | collective-permute-start | bytes 147464 | tf_op jit(solution)/shard_map/ppermute | solution.py:239
  35.4 8.9 %collective-permute-start.10 = (bf16[96,256]{1,0:T(8,128)(2,1)S(1)}, bf16[96,256]{1,0:T(8,128)(2,1)S(1)}, u32[]{:S(2)}, u32[]{:S(2)}) collective-permute-start(bf16[96,256]{1,0:T(8,128)(2,1)S(1)} %collective-permute-done), channel_id=1, source_target_pairs={{0,192},{4,196},{8,200},{12,204},{16,208},{20,212},{24,216},{28,22... | collective-permute-start | bytes 147464 | tf_op jit(solution)/shard_map/ppermute | solution.py:239
  39.0 6.0 %collective-permute-start.11 = (bf16[96,256]{1,0:T(8,128)(2,1)S(1)}, bf16[96,256]{1,0:T(8,128)(2,1)S(1)}, u32[]{:S(2)}, u32[]{:S(2)}) collective-permute-start(bf16[96,256]{1,0:T(8,128)(2,1)S(1)} %collective-permute-done), channel_id=1, source_target_pairs={{0,224},{4,228},{8,232},{12,236},{16,240},{20,244},{24,248},{28,25... | collective-permute-start | bytes 147464 | tf_op jit(solution)/shard_map/ppermute | solution.py:239
  39.9 10.4 %collective-permute-start.2 = (bf16[8,96,256]{2,1,0:T(8,128)(2,1)S(1)}, bf16[8,96,256]{2,1,0:T(8,128)(2,1)S(1)}, u32[]{:S(2)}, u32[]{:S(2)}) collective-permute-start(bf16[8,96,256]{2,1,0:T(8,128)(2,1)S(1)} %get-tuple-element.37), channel_id=1, source_target_pairs={{0,8},{4,12},{8,16},{12,20},{16,24},{20,28},{24,0},{28,4},{32,40},... | collective-permute-start | bytes 1179656 | tf_op jit(solution)/shard_map/ppermute | solution.py:238
  40.6 19.1 %collective-permute-start.3 = (bf16[8,96,256]{2,1,0:T(8,128)(2,1)S(1)}, bf16[8,96,256]{2,1,0:T(8,128)(2,1)S(1)}, u32[]{:S(2)}, u32[]{:S(2)}) collective-permute-start(bf16[8,96,256]{2,1,0:T(8,128)(2,1)S(1)} %get-tuple-element.38), channel_id=1, source_target_pairs={{0,16},{4,20},{8,24},{12,28},{16,0},{20,4},{24,8},{28,12},{32,48},... | collective-permute-start | bytes 1179656 | tf_op jit(solution)/shard_map/ppermute | solution.py:238
  44.3 16.4 %collective-permute-start.4 = (bf16[8,96,256]{2,1,0:T(8,128)(2,1)S(1)}, bf16[8,96,256]{2,1,0:T(8,128)(2,1)S(1)}, u32[]{:S(2)}, u32[]{:S(2)}) collective-permute-start(bf16[8,96,256]{2,1,0:T(8,128)(2,1)S(1)} %get-tuple-element.39), channel_id=1, source_target_pairs={{0,24},{4,28},{8,0},{12,4},{16,8},{20,12},{24,16},{28,20},{32,56},... | collective-permute-start | bytes 1179656 | tf_op jit(solution)/shard_map/ppermute | solution.py:238
  44.9 34.7 %copy-start.2 = (f32[96,256]{1,0:T(8,128)S(1)}, f32[96,256]{1,0:T(8,128)}, u32[]{:S(2)}) copy-start(f32[96,256]{1,0:T(8,128)} %param.9) | copy-start | bytes 294916
  44.9 34.7 %copy-start.3 = (f32[96,256]{1,0:T(8,128)S(1)}, f32[96,256]{1,0:T(8,128)}, u32[]{:S(2)}) copy-start(f32[96,256]{1,0:T(8,128)} %param.10) | copy-start | bytes 294916
  44.9 34.7 %copy-start.4 = (f32[96,256]{1,0:T(8,128)S(1)}, f32[96,256]{1,0:T(8,128)}, u32[]{:S(2)}) copy-start(f32[96,256]{1,0:T(8,128)} %param.11) | copy-start | bytes 294916
  61.6 17.9 %all-to-all-start = ((bf16[8,96,256]{2,1,0:T(8,128)(2,1)}), bf16[8,96,256]{2,1,0:T(8,128)(2,1)S(1)}, u32[]{:S(2)}, u32[]{:S(2)}) async-start(bf16[8,96,256]{2,1,0:T(8,128)(2,1)} %add_convert_fusion), calls=%async_computation | async-start | bytes 786432 | tf_op jit(solution)/shard_map/all_to_all | solution.py:217
  65.1 12.9 %collective-permute-start.12 = (bf16[1024,256]{1,0:T(8,128)(2,1)S(1)}, bf16[1024,256]{1,0:T(8,128)(2,1)S(1)}, u32[]{:S(2)}, u32[]{:S(2)}) collective-permute-start(bf16[1024,256]{1,0:T(8,128)(2,1)S(1)} %get-tuple-element.31.refs_0_), channel_id=1, source_target_pairs={{0,1},{1,2},{2,3},{3,0},{4,5},{5,6},{6,7},{7,4},{8,9},{9,10},{10,1... | collective-permute-start | bytes 1572872 | tf_op jit(solution)/shard_map/ppermute | solution.py:245
  65.2 12.8 %collective-permute-start.13 = (bf16[1024,256]{1,0:T(8,128)(2,1)S(1)}, bf16[1024,256]{1,0:T(8,128)(2,1)S(1)}, u32[]{:S(2)}, u32[]{:S(2)}) collective-permute-start(bf16[1024,256]{1,0:T(8,128)(2,1)S(1)} %get-tuple-element.31.refs_0_), channel_id=1, source_target_pairs={{0,3},{1,0},{2,1},{3,2},{4,7},{5,4},{6,5},{7,6},{8,11},{9,8},{10,9... | collective-permute-start | bytes 1572872 | tf_op jit(solution)/shard_map/ppermute | solution.py:245
  68.0 10.9 %collective-permute-start.14 = (bf16[8,96,256]{2,1,0:T(8,128)(2,1)S(1)}, bf16[8,96,256]{2,1,0:T(8,128)(2,1)S(1)}, u32[]{:S(2)}, u32[]{:S(2)}) collective-permute-start(bf16[8,96,256]{2,1,0:T(8,128)(2,1)S(1)} %bitcast_dynamic-update-slice_fusion.refs_4_), channel_id=1, source_target_pairs={{0,8},{4,12},{8,16},{12,20},{16,24},{20,28},{24,0},{28,4},{32,40},... | collective-permute-start | bytes 1179656 | tf_op jit(solution)/shard_map/ppermute | solution.py:246
  70.2 9.4 %collective-permute-start.15 = (bf16[8,96,256]{2,1,0:T(8,128)(2,1)S(1)}, bf16[8,96,256]{2,1,0:T(8,128)(2,1)}, u32[]{:S(2)}, u32[]{:S(2)}) collective-permute-start(bf16[8,96,256]{2,1,0:T(8,128)(2,1)S(1)} %bitcast_dynamic-update-slice_fusion.refs_4_), channel_id=1, source_target_pairs={{0,24},{4,28},{8,0},{12,4},{16,8},{20,12},{24,16},{28,20},{32,56},... | collective-permute-start | bytes 1179656 | tf_op jit(solution)/shard_map/ppermute | solution.py:246
  81.2 18.5 %all-to-all-start.1 = ((bf16[8,96,256]{2,1,0:T(8,128)(2,1)}), bf16[8,96,256]{2,1,0:T(8,128)(2,1)S(1)}, u32[]{:S(2)}, u32[]{:S(2)}) async-start(bf16[8,96,256]{2,1,0:T(8,128)(2,1)} %broadcast_in_dim.2), calls=%async_computation.1 | async-start | bytes 786432 | tf_op jit(solution)/shard_map/all_to_all | solution.py:217
  87.5 12.2 %collective-permute-start.16 = (bf16[1024,256]{1,0:T(8,128)(2,1)S(1)}, bf16[1024,256]{1,0:T(8,128)(2,1)S(1)}, u32[]{:S(2)}, u32[]{:S(2)}) collective-permute-start(bf16[1024,256]{1,0:T(8,128)(2,1)S(1)} %get-tuple-element.31.refs_0_), channel_id=1, source_target_pairs={{0,2},{1,3},{2,0},{3,1},{4,6},{5,7},{6,4},{7,5},{8,10},{9,11},{10,... | collective-permute-start | bytes 1572872 | tf_op jit(solution)/shard_map/ppermute | solution.py:245
  88.5 11.2 %collective-permute-start.17 = (bf16[8,96,256]{2,1,0:T(8,128)(2,1)S(1)}, bf16[8,96,256]{2,1,0:T(8,128)(2,1)}, u32[]{:S(2)}, u32[]{:S(2)}) collective-permute-start(bf16[8,96,256]{2,1,0:T(8,128)(2,1)S(1)} %bitcast_dynamic-update-slice_fusion.refs_4_), channel_id=1, source_target_pairs={{0,16},{4,20},{8,24},{12,28},{16,0},{20,4},{24,8},{28,12},{32,48},... | collective-permute-start | bytes 1179656 | tf_op jit(solution)/shard_map/ppermute | solution.py:246
  91.1 14.4 %collective-permute-start.18 = (bf16[8,96,256]{2,1,0:T(8,128)(2,1)S(1)}, bf16[8,96,256]{2,1,0:T(8,128)(2,1)}, u32[]{:S(2)}, u32[]{:S(2)}) collective-permute-start(bf16[8,96,256]{2,1,0:T(8,128)(2,1)S(1)} %bitcast_dynamic-update-slice_fusion.refs_4_), channel_id=1, source_target_pairs={{0,4},{4,0},{8,12},{12,8},{16,20},{20,16},{24,28},{28,24},{32,36},... | collective-permute-start | bytes 1179656 | tf_op jit(solution)/shard_map/ppermute | solution.py:262
  94.4 13.6 %collective-permute-start.19 = (bf16[8,96,256]{2,1,0:T(8,128)(2,1)S(1)}, bf16[8,96,256]{2,1,0:T(8,128)(2,1)}, u32[]{:S(2)}, u32[]{:S(2)}) collective-permute-start(bf16[8,96,256]{2,1,0:T(8,128)(2,1)S(1)} %collective-permute-done.14.refs_5_), channel_id=1, source_target_pairs={{0,4},{4,0},{8,12},{12,8},{16,20},{20,16},{24,28},{28,24},{32,36},... | collective-permute-start | bytes 1179656 | tf_op jit(solution)/shard_map/ppermute | solution.py:262
  94.4 13.6 %collective-permute-start.21 = (bf16[8,96,256]{2,1,0:T(8,128)(2,1)}, bf16[8,96,256]{2,1,0:T(8,128)(2,1)}, u32[]{:S(2)}, u32[]{:S(2)}) collective-permute-start(bf16[8,96,256]{2,1,0:T(8,128)(2,1)} %collective-permute-done.15.refs_7_), channel_id=1, source_target_pairs={{0,4},{4,0},{8,12},{12,8},{16,20},{20,16},{24,28},{28,24},{32,36},... | collective-permute-start | bytes 1179656 | tf_op jit(solution)/shard_map/ppermute | solution.py:262
  99.7 9.1 %collective-permute-start.20 = (bf16[8,96,256]{2,1,0:T(8,128)(2,1)}, bf16[8,96,256]{2,1,0:T(8,128)(2,1)S(1)}, u32[]{:S(2)}, u32[]{:S(2)}) collective-permute-start(bf16[8,96,256]{2,1,0:T(8,128)(2,1)} %collective-permute-done.17.refs_6_), channel_id=1, source_target_pairs={{0,4},{4,0},{8,12},{12,8},{16,20},{20,16},{24,28},{28,24},{32,36},... | collective-permute-start | bytes 1179656 | tf_op jit(solution)/shard_map/ppermute | solution.py:262
  103.3 12.9 %collective-permute-start.22 = (bf16[8,96,256]{2,1,0:T(8,128)(2,1)S(1)}, bf16[8,96,256]{2,1,0:T(8,128)(2,1)S(1)}, u32[]{:S(2)}, u32[]{:S(2)}) collective-permute-start(bf16[8,96,256]{2,1,0:T(8,128)(2,1)S(1)} %all-to-all-done.1.refs_0_), channel_id=1, source_target_pairs={{0,8},{4,12},{8,16},{12,20},{16,24},{20,28},{24,0},{28,4},{32,40},... | collective-permute-start | bytes 1179656 | tf_op jit(solution)/shard_map/ppermute | solution.py:263
  105.5 20.2 %collective-permute-start.23 = (bf16[8,96,256]{2,1,0:T(8,128)(2,1)S(1)}, bf16[8,96,256]{2,1,0:T(8,128)(2,1)S(1)}, u32[]{:S(2)}, u32[]{:S(2)}) collective-permute-start(bf16[8,96,256]{2,1,0:T(8,128)(2,1)S(1)} %all-to-all-done.1.refs_0_), channel_id=1, source_target_pairs={{0,16},{4,20},{8,24},{12,28},{16,0},{20,4},{24,8},{28,12},{32,48},... | collective-permute-start | bytes 1179656 | tf_op jit(solution)/shard_map/ppermute | solution.py:263
  108.0 17.6 %collective-permute-start.24 = (bf16[8,96,256]{2,1,0:T(8,128)(2,1)S(1)}, bf16[8,96,256]{2,1,0:T(8,128)(2,1)S(1)}, u32[]{:S(2)}, u32[]{:S(2)}) collective-permute-start(bf16[8,96,256]{2,1,0:T(8,128)(2,1)S(1)} %all-to-all-done.1.refs_0_), channel_id=1, source_target_pairs={{0,24},{4,28},{8,0},{12,4},{16,8},{20,12},{24,16},{28,20},{32,56},... | collective-permute-start | bytes 1179656 | tf_op jit(solution)/shard_map/ppermute | solution.py:263
  108.0 19.0 %collective-permute-start.25 = (bf16[8,96,256]{2,1,0:T(8,128)(2,1)S(1)}, bf16[8,96,256]{2,1,0:T(8,128)(2,1)S(1)}, u32[]{:S(2)}, u32[]{:S(2)}) collective-permute-start(bf16[8,96,256]{2,1,0:T(8,128)(2,1)S(1)} %all-to-all-done.1.refs_0_), channel_id=1, source_target_pairs={{0,4},{4,0},{8,12},{12,8},{16,20},{20,16},{24,28},{28,24},{32,36},... | collective-permute-start | bytes 1179656 | tf_op jit(solution)/shard_map/ppermute | solution.py:266
  125.6 2.2 %collective-permute-start.26 = (bf16[8,96,256]{2,1,0:T(8,128)(2,1)S(1)}, bf16[8,96,256]{2,1,0:T(8,128)(2,1)S(1)}, u32[]{:S(2)}, u32[]{:S(2)}) collective-permute-start(bf16[8,96,256]{2,1,0:T(8,128)(2,1)S(1)} %collective-permute-done.22.refs_2_), channel_id=1, source_target_pairs={{0,4},{4,0},{8,12},{12,8},{16,20},{20,16},{24,28},{28,24},{32,36},... | collective-permute-start | bytes 1179656 | tf_op jit(solution)/shard_map/ppermute | solution.py:266
  126.5 1.9 %collective-permute-start.27 = (bf16[8,96,256]{2,1,0:T(8,128)(2,1)S(1)}, bf16[8,96,256]{2,1,0:T(8,128)(2,1)S(1)}, u32[]{:S(2)}, u32[]{:S(2)}) collective-permute-start(bf16[8,96,256]{2,1,0:T(8,128)(2,1)S(1)} %collective-permute-done.23.refs_4_), channel_id=1, source_target_pairs={{0,4},{4,0},{8,12},{12,8},{16,20},{20,16},{24,28},{28,24},{32,36},... | collective-permute-start | bytes 1179656 | tf_op jit(solution)/shard_map/ppermute | solution.py:266
  126.5 2.5 %collective-permute-start.28 = (bf16[8,96,256]{2,1,0:T(8,128)(2,1)S(1)}, bf16[8,96,256]{2,1,0:T(8,128)(2,1)S(1)}, u32[]{:S(2)}, u32[]{:S(2)}) collective-permute-start(bf16[8,96,256]{2,1,0:T(8,128)(2,1)S(1)} %collective-permute-done.24.refs_6_), channel_id=1, source_target_pairs={{0,4},{4,0},{8,12},{12,8},{16,20},{20,16},{24,28},{28,24},{32,36},... | collective-permute-start | bytes 1179656 | tf_op jit(solution)/shard_map/ppermute | solution.py:266

commit v3 on v2

v3 whole, which is shorter than its diff:
```python
import math

import jax
import jax.numpy as jnp
from jax import lax
from jax.experimental import pallas as pl
from jax.experimental.pallas import tpu as pltpu
from jax.sharding import PartitionSpec as P

ADAM_STEP = 10
NZ, NX, NC, NT = 8, 4, 2, 4
NDP = NZ * NX * NC
TOK = 1024
HID = 256
D = 6144
OWN = D // NDP
ZROWS = D // NZ
NJ = NZ // 2
HALF = NZ * OWN

BF16 = jnp.bfloat16
F32 = jnp.float32


def dp_index(z, x, c):
    return (z * NX + x) * NC + c


POINTS = [(z, x, c) for z in range(NZ) for x in range(NX) for c in range(NC)]
CORE_SWAP = [(dp_index(z, x, c), dp_index(z, x, 1 - c)) for z, x, c in POINTS]
PLANE = NDP // NT


def x_shift(s):
    return [(dp_index(z, x, c), dp_index(z, (x + s) % NX, c)) for z, x, c in POINTS]


def z_shift(s):
    return [(dp_index(z, x, c), dp_index((z + s) % NZ, x, c)) for z, x, c in POINTS]


Z_SWAP = [(dp_index(z, x, c), dp_index(z ^ 1, x, c)) for z, x, c in POINTS]


Z_GROUPS = [[dp_index(z, x, c) for z in range(NZ)] for x in range(NX) for c in range(NC)]


def weight_route():
    pairs = []
    for r in range(NDP):
        for t in range(NT):
            k, j = divmod(r, PLANE)
            c, z = divmod(j, NZ)
            pairs.append((r * NT + t, dp_index(z, t, c) * NT + k))
    return pairs


def gelu_slope(value):
    cdf = 0.5 * (1.0 + lax.erf(value * (1.0 / math.sqrt(2.0))))
    pdf = jnp.exp(-0.5 * value * value) * (1.0 / math.sqrt(2.0 * math.pi))
    return cdf + value * pdf


def position():
    rank = lax.axis_index("dp")
    return lax.rem(lax.div(rank, NC), NX), lax.rem(rank, NC), lax.div(rank, NX * NC)


def z_of(z, side, j):
    base = z if side == 0 else z + 1 - 2 * lax.rem(z, 2)
    return lax.rem(base + 2 * j, NZ)


def term_kernel(pre_hbm, cot_hbm, in_ref, *refs):
    keeps, sends, act_ref = refs[0:2], refs[2:4], refs[4]
    pre_ref, cot_ref, held, made, sems = refs[5:]
    x, c, z = position()

    def fetch(side, j):
        columns = pl.ds(pl.multiple_of(z_of(z, side, j) * ZROWS, ZROWS), ZROWS)
        slot = side * NJ + j
        return pltpu.make_async_copy(in_ref.at[:, columns], held.at[slot], sems.at[slot])

    pre_copy = pltpu.make_async_copy(pre_hbm, pre_ref, sems.at[NZ])
    cot_copy = pltpu.make_async_copy(cot_hbm, cot_ref, sems.at[NZ + 1])
    pre_copy.start()
    cot_copy.start()
    for side in (1, 0):
        for j in range(NJ):
            fetch(side, j).start()
    pre_copy.wait()
    cot_copy.wait()
    slope = gelu_slope(pre_ref[...].astype(F32))
    act_ref[...] = (cot_ref[...].astype(F32) * slope).astype(BF16)

    for side in (1, 0):

        @pl.loop(0, NJ)
        def _(j):
            fetch(side, j).wait()
            term = lax.dot_general(
                held[side * NJ + j],
                act_ref[...],
                (((0,), (0,)), ((), ())),
                preferred_element_type=F32,
            )
            scale = (jnp.max(jnp.abs(term), axis=1, keepdims=True) + 1e-06) / 127.0
            codes = jnp.clip(term * (1.0 / scale), -127.0, 127.0).astype(BF16)
            made[...] = (codes.astype(F32) * scale).astype(BF16)
            for s in range(NX):
                base = lax.rem(x + s, NX) * (NC * OWN)
                mine = pl.multiple_of(base + c * OWN, OWN)
                other = pl.multiple_of(base + (1 - c) * OWN, OWN)
                keeps[side][s, j] = made[pl.ds(mine, OWN), :]
                sends[side][s, j] = made[pl.ds(other, OWN), :]


def make_terms(pre_act, grad_hidden, inputs):
    out = jax.ShapeDtypeStruct((NX, NJ, OWN, HID), BF16)
    vmem = pl.BlockSpec(memory_space=pltpu.VMEM)
    hbm = pl.BlockSpec(memory_space=pltpu.HBM)
    return pl.pallas_call(
        term_kernel,
        in_specs=[hbm, hbm, hbm],
        out_specs=[vmem] * 5,
        out_shape=[out] * 4 + [jax.ShapeDtypeStruct((TOK, HID), BF16)],
        scratch_shapes=[
            pltpu.VMEM((TOK, HID), BF16),
            pltpu.VMEM((TOK, HID), BF16),
            pltpu.VMEM((NZ, TOK, ZROWS), BF16),
            pltpu.VMEM((ZROWS, HID), BF16),
            pltpu.SemaphoreType.DMA((NZ + 2,)),
        ],
        compiler_params=pltpu.CompilerParams(vmem_limit_bytes=56 * 2**20),
        cost_estimate=pl.CostEstimate(
            flops=2 * TOK * D * HID, bytes_accessed=2 * D * (TOK + HID), transcendentals=0
        ),
        name="terms",
    )(pre_act, grad_hidden, inputs)


GI_ROWS = 256
GI_COLS = D // NT


def input_kernel(act_ref, *refs):
    mine_refs, other_refs, out_ref = refs[:NX], refs[NX : 2 * NX], refs[2 * NX]
    x, c, _ = position()
    for w_refs, core in ((mine_refs, c), (other_refs, 1 - c)):
        total = jnp.zeros((GI_ROWS, HALF), F32)
        for s in range(NX):
            total += lax.dot_general(
                act_ref[lax.rem(x + NX - s, NX)],
                w_refs[s][...],
                (((1,), (1,)), ((), ())),
                preferred_element_type=F32,
            )
        out_ref[:, pl.ds(pl.multiple_of(core * HALF, HALF), HALF)] = total.astype(BF16)


def make_grad_input(act_all, mine, other):
    whole = pl.BlockSpec((HALF, HID), lambda i: (0, 0))
    return pl.pallas_call(
        input_kernel,
        grid=(TOK // GI_ROWS,),
        in_specs=[pl.BlockSpec((NT, GI_ROWS, HID), lambda i: (0, i, 0))] + [whole] * (2 * NX),
        out_specs=pl.BlockSpec((GI_ROWS, GI_COLS), lambda i: (i, 0)),
        out_shape=jax.ShapeDtypeStruct((TOK, GI_COLS), BF16),
        compiler_params=pltpu.CompilerParams(vmem_limit_bytes=40 * 2**20),
        cost_estimate=pl.CostEstimate(
            flops=2 * TOK * GI_COLS * HID * NT,
            bytes_accessed=2 * (TOK * HID * NT + GI_COLS * HID * NT + TOK * GI_COLS),
            transcendentals=0,
        ),
        name="grad_input",
    )(act_all, *mine, *other)


def collect_kernel(*refs):
    pieces, out_ref = refs[:NJ], refs[NJ]
    _, _, z = position()
    for j in range(NJ):
        for side in range(2):
            out_ref[z_of(z, side, NJ - j)] = pieces[j][side]


def collect(pieces):
    return pl.pallas_call(
        collect_kernel,
        out_shape=jax.ShapeDtypeStruct((NZ, OWN, HID), BF16),
        name="collect",
    )(*pieces)


def place_kernel(*refs):
    pieces, out_ref, sems = refs[: 2 * NX], refs[2 * NX], refs[2 * NX + 1]
    x, c, _ = position()
    copies = []
    for s in range(NX):
        from_x = lax.rem(x + NX - s, NX)
        for side, core in ((0, c), (1, 1 - c)):
            copy = pltpu.make_async_copy(
                pieces[2 * s + side], out_ref.at[:, from_x, core], sems.at[2 * s + side]
            )
            copy.start()
            copies.append(copy)
    for copy in copies:
        copy.wait()


def make_weights(pieces):
    out = pl.pallas_call(
        place_kernel,
        in_specs=[pl.BlockSpec(memory_space=pltpu.VMEM)] * (2 * NX),
        out_specs=pl.BlockSpec(memory_space=pl.ANY),
        out_shape=jax.ShapeDtypeStruct((NZ, NX, NC, OWN, HID), BF16),
        scratch_shapes=[pltpu.SemaphoreType.DMA((2 * NX,))],
        compiler_params=pltpu.CompilerParams(vmem_limit_bytes=40 * 2**20),
        name="place",
    )(*pieces)
    return out.reshape(D, HID)


def tie(*arrays):
    return lax.optimization_barrier(arrays)


def spread_kernel(in_ref, after_ref, out_ref):
    for i in range(out_ref.shape[0]):
        out_ref[i] = in_ref[...]


def spread(block, count, after):
    return pl.pallas_call(
        spread_kernel,
        in_specs=[pl.BlockSpec(memory_space=pltpu.VMEM), pl.BlockSpec(memory_space=pl.ANY)],
        out_shape=jax.ShapeDtypeStruct((count,) + block.shape, block.dtype),
        cost_estimate=pl.CostEstimate(flops=10**10, bytes_accessed=0, transcendentals=0),
        compiler_params=pltpu.CompilerParams(vmem_limit_bytes=40 * 2**20),
        name="spread",
    )(block, after)


def swap_all(blocks, axis, groups=None):
    return lax.all_to_all(
        blocks, axis, split_axis=0, concat_axis=0, axis_index_groups=groups, tiled=True
    )


def local(inputs, pre_act, grad_hidden, master, moment_one, moment_two):
    w_own = lax.ppermute(master, ("dp", "tensor"), weight_route())
    *made, act_grad = make_terms(pre_act, grad_hidden, inputs)
    keeps, sends = made[:2], made[2:]
    sends[0], sends[1], w_own = tie(sends[0], sends[1], w_own)
    w_spread = spread(w_own.astype(BF16), NZ, sends[1])

    sums = [None, None]
    for side in (1, 0):
        recv = lax.ppermute(sends[side], "dp", CORE_SWAP)
        sums[side] = [
            (keeps[side][s].astype(F32) + recv[s].astype(F32)).astype(BF16) for s in range(NX)
        ]
    w_z = swap_all(w_spread, "dp", Z_GROUPS).reshape(HALF, HID)
    totals = [None, None]
    for side in (1, 0):
        total = sums[side][0].astype(F32)
        for s in range(1, NX):
            total += lax.ppermute(sums[side][s], "dp", x_shift(s)).astype(F32)
        totals[side] = total
    ahead = totals[1].astype(BF16)
    other = lax.ppermute(ahead, "dp", Z_SWAP)
    act_all = swap_all(spread(act_grad, NT, w_z), "tensor").reshape(NT, TOK, HID)
    total = (totals[0] + other.astype(F32)).astype(BF16)
    total, w_z = tie(total, w_z)

    w_z = spread(w_z, 1, total)[0]
    w_mine = [w_z] + [lax.ppermute(w_z, "dp", x_shift(s)) for s in range(1, NX)]
    grad = total[0].astype(F32)
    for j in range(1, NJ):
        grad += lax.ppermute(total[j], "dp", z_shift(2 * j)).astype(F32)

    new_one = 0.9 * moment_one + 0.1 * grad
    new_two = 0.999 * moment_two + 0.001 * grad * grad
    corr_one = 1.0 - 0.9**ADAM_STEP
    corr_two = 1.0 - 0.999**ADAM_STEP
    update = new_one / corr_one / (jnp.sqrt(new_two / corr_two) + 1e-08) + 0.01 * master
    new_master = master - 0.01 * update

    n_own = new_master.astype(BF16)
    n_pair = jnp.stack([n_own, lax.ppermute(n_own, "dp", Z_SWAP)])
    n_z = [n_pair] + [lax.ppermute(n_pair, "dp", z_shift(2 * j)) for j in range(1, NJ)]
    n_z[2], act_all = tie(n_z[2], act_all)
    n_z, *w_mine = tie(collect(n_z), *w_mine)
    mine = [n_z] + [lax.ppermute(n_z, "dp", x_shift(s)) for s in range(1, NX)]
    w_other = [lax.ppermute(piece, "dp", CORE_SWAP) for piece in w_mine]
    grad_input = make_grad_input(act_all, w_mine, w_other)
    grad_input, *mine[1:] = tie(grad_input, *mine[1:])
    pieces = []
    for piece in mine:
        pieces += [piece, lax.ppermute(piece, "dp", CORE_SWAP)]
    new_weights = make_weights(pieces)
    return (grad_input, new_master, new_one, new_two, new_weights)


def solution(mesh):
    shard = P("dp", "tensor")
    return jax.shard_map(
        local,
        mesh=mesh,
        in_specs=(P("dp", None), shard, shard, shard, shard, shard),
        out_specs=(shard, shard, shard, shard, P(None, "tensor")),
        check_vma=False,
    )
```

time: 132 us -> 120 us (0.909)
  waiting for transfers between devices: 43.9 us -> 28.4 us
  other arithmetic: 3.31 us -> 6.08 us
  Pallas kernels: 17.9 us -> 19.8 us
    ppermute x22 -> x24, waiting for transfers between devices: 34.5 us -> 15.6 us  [the longest x3 5.77 us: local(): lax.ppermute(n_pair, 'dp', z_shift(2 * j))]
    ppermute x3, waiting for transfers between devices: 9.44 us -> 12.8 us  [local(): mine = [n_z] + [lax.ppermute(n_z, 'dp', x_shift(s)) for s in range(1, NX)]]
    all_to_all x2, starting transfers between devices: 9.74 us -> 11.9 us  [swap_all(): lax.all_to_all(blocks, axis, split_axis=0, concat_axis=0, axis_index_grou...]
    convert_element_type x4 -> x5, other arithmetic: 3.18 us -> 5.17 us  [the longest x2 2.17 us: local(): (keeps[side][s].astype(F32) + recv[s].astype(F32)).astype(BF16)]
    ppermute x22 -> x24, starting transfers between devices: 40.4 us -> 38.5 us  [the longest x6 9.75 us: local(): total += lax.ppermute(sums[side][s], 'dp', x_shift(s)).astype(F32)]
    pallas_call x3 -> x7, Pallas kernels: 17.9 us -> 19.8 us  [the longest x1 9.22 us: make_terms(): pl.pallas_call(term_kernel, in_specs=[hbm, hbm, hbm], out_specs=[vmem] *...]
    ppermute x4, starting transfers between devices: 7.52 us -> 5.88 us  [local(): w_other = [lax.ppermute(piece, 'dp', CORE_SWAP) for piece in w_mine]]
  transfers between devices with their start and end apart: 31 -> 33, of which waited for: 13 -> 13; matrix products, arithmetic and copies ran while one was open for 0% -> 4% of each run, Pallas kernels for 12% -> 15%
where the time goes in v3:
time: 120 us
  starting transfers between devices  62.1 us (52%)
  waiting for transfers between devices  28.4 us (24%)
  Pallas kernels  19.8 us (16%)
  other arithmetic  6.08 us (5%)
  local copies, waits for them, and re-layouts  2.49 us (2%)
    ppermute x3, waiting for transfers between devices, local(): mine = [n_z] + [lax.ppermute(n_z, 'dp', x_shift(s)) for s in range(1, NX)]  12.8 us
    all_to_all x2, starting transfers between devices, swap_all(): lax.all_to_all(blocks, axis, split_axis=0, concat_axis=0, axis_index_grou...  11.9 us
    ppermute x6, starting transfers between devices, local(): total += lax.ppermute(sums[side][s], 'dp', x_shift(s)).astype(F32)  9.75 us
    pallas_call x1, Pallas kernels, make_terms(): pl.pallas_call(term_kernel, in_specs=[hbm, hbm, hbm], out_specs=[vmem] *...  9.22 us
    ppermute x3, starting transfers between devices, local(): grad += lax.ppermute(total[j], 'dp', z_shift(2 * j)).astype(F32)  8.7 us
    ppermute x3, starting transfers between devices, local(): lax.ppermute(n_pair, 'dp', z_shift(2 * j))  7.59 us
    pallas_call x1, Pallas kernels, make_grad_input(): pl.pallas_call(input_kernel, grid=(TOK // GI_ROWS,), in_specs=[pl.BlockSp...  6.09 us
    ppermute x3, starting transfers between devices, local(): mine = [n_z] + [lax.ppermute(n_z, 'dp', x_shift(s)) for s in range(1, NX)]  5.88 us
  transfers between devices with their start and end apart: 33, of which 13 were waited for; matrix products, arithmetic and copies ran while one was open for 4% of the time, Pallas kernels for 15%

profile of v3, /device:TPU:1, one launch (start us, length us, event | category | flops | bytes accessed | tf_op | source)
XLA Modules:
  0.0 119.9 jit_solution(14233739751547904293)
XLA Ops:
  0.6 0.9 convert.31
  1.5 4.9 %collective-permute-start = (bf16[96,256]{1,0:T(8,128)(2,1)S(1)}, bf16[96,256]{1,0:T(8,128)(2,1)S(1)}, u32[]{:S(2)}, u32[]{:S(2)}) collective-permute-start(bf16[96,256]{1,0:T(8,128)(2,1)S(1)} %convert.31), channel_id=1, source_target_pairs={{0,0},{1,8},{2,16},{3,24},{4,32},{5,40},{6,48},{7,56},{8,64},{9,72... | collective-permute-start | bytes 147464 | tf_op jit(solution)/shard_map/ppermute | solution.py:251
  6.5 9.2 %terms.1 = (bf16[4,4,96,256]{3,2,1,0:T(8,128)(2,1)}, bf16[4,4,96,256]{3,2,1,0:T(8,128)(2,1)}, bf16[4,4,96,256]{3,2,1,0:T(8,128)(2,1)}, bf16[4,4,96,256]{3,2,1,0:T(8,128)(2,1)}, bf16[1024,256]{1,0:T(8,128)(2,1)}) custom-call(bf16[1024,256]{1,0:T(8,128)(2,1)} %pre_hbm.1, bf16[1024,256]{1,0:T(8,128)(2,1)} %cot_hbm.1, bf16[1024,6144]{1,0:T(8,128)(2,1)} %in_ref.1), custom_call_target="tpu_custom_call" | custom-call | flops 3221225472 | bytes 15728640 | tf_op jit(solution)/shard_map/terms/pallas_call | solution.py:122
  16.3 1.1 copy-done.2
  17.4 0.8 spread.3
  18.2 8.3 %all-to-all-start = ((bf16[8,96,256]{2,1,0:T(8,128)(2,1)}), bf16[8,96,256]{2,1,0:T(8,128)(2,1)S(1)}, u32[]{:S(2)}, u32[]{:S(2)}) async-start(bf16[8,96,256]{2,1,0:T(8,128)(2,1)} %spread.3), calls=%async_computation | async-start | bytes 786432 | tf_op jit(solution)/shard_map/all_to_all | solution.py:245
  26.7 2.2 %collective-permute-start.6 = (bf16[4,96,256]{2,1,0:T(8,128)(2,1)S(1)}, bf16[4,96,256]{2,1,0:T(8,128)(2,1)S(1)}, u32[]{:S(2)}, u32[]{:S(2)}) collective-permute-start(bf16[4,96,256]{2,1,0:T(8,128)(2,1)S(1)} %get-tuple-element.54), channel_id=1, source_target_pairs={{0,8},{4,12},{8,16},{12,20},{16,24},{20,28},{24,0},{28,4},{32,40},... | collective-permute-start | bytes 589832 | tf_op jit(solution)/shard_map/ppermute | solution.py:268
  28.8 3.1 %collective-permute-start.8 = (bf16[4,96,256]{2,1,0:T(8,128)(2,1)S(1)}, bf16[4,96,256]{2,1,0:T(8,128)(2,1)S(1)}, u32[]{:S(2)}, u32[]{:S(2)}) collective-permute-start(bf16[4,96,256]{2,1,0:T(8,128)(2,1)S(1)} %get-tuple-element.55), channel_id=1, source_target_pairs={{0,24},{4,28},{8,0},{12,4},{16,8},{20,12},{24,16},{28,20},{32,56},... | collective-permute-start | bytes 589832 | tf_op jit(solution)/shard_map/ppermute | solution.py:268
  32.0 1.1 collective-permute-start.7
  33.1 2.0 %fusion.8 = (bf16[4,96,256]{2,1,0:T(8,128)(2,1)}, bf16[4,96,256]{2,1,0:T(8,128)(2,1)}, bf16[4,96,256]{2,1,0:T(8,128)(2,1)S(1)}) fusion(bf16[4,4,96,256]{3,2,1,0:T(8,128)(2,1)} %collective-permute-done.1, bf16[4,4,96,256]{3,2,1,0:T(8,128)(2,1)S(1)} %copy-done.5), kind=kLoop, calls=%fused_computation.18 | loop fusion | flops 1179648 | bytes 1769472 | tf_op jit(solution)/shard_map/convert_element_type | solution.py:261
  35.1 0.9 collective-permute-start.2
  35.9 1.8 %collective-permute-start.4 = (bf16[4,96,256]{2,1,0:T(8,128)(2,1)}, bf16[4,96,256]{2,1,0:T(8,128)(2,1)}, u32[]{:S(2)}, u32[]{:S(2)}) collective-permute-start(bf16[4,96,256]{2,1,0:T(8,128)(2,1)} %get-tuple-element.52), channel_id=1, source_target_pairs={{0,24},{4,28},{8,0},{12,4},{16,8},{20,12},{24,16},{28,20},{32,56},... | collective-permute-start | bytes 589832 | tf_op jit(solution)/shard_map/ppermute | solution.py:268
  37.8 0.7 collective-permute-start.3
  38.4 0.9 collective-permute-done.8
  39.3 2.7 %collective-permute-done.7 = bf16[4,96,256]{2,1,0:T(8,128)(2,1)S(1)} collective-permute-done((bf16[4,96,256]{2,1,0:T(8,128)(2,1)S(1)}, bf16[4,96,256]{2,1,0:T(8,128)(2,1)S(1)}, u32[]{:S(2)}, u32[]{:S(2)}) %collective-permute-start.7) | collective-permute-done | bytes 196640 | tf_op jit(solution)/shard_map/ppermute | solution.py:268
  42.0 0.8 fusion.2
  42.8 1.1 collective-permute-start.9
  44.1 1.3 %copy-done = bf16[4,1024,256]{2,1,0:T(8,128)(2,1)} copy-done((bf16[4,1024,256]{2,1,0:T(8,128)(2,1)}, bf16[4,1024,256]{2,1,0:T(8,128)(2,1)S(1)}, u32[]{:S(2)}) %copy-start) | copy-done | bytes 2097176
  45.4 3.6 %all-to-all-start.1 = ((bf16[4,1024,256]{2,1,0:T(8,128)(2,1)}), bf16[4,1024,256]{2,1,0:T(8,128)(2,1)S(1)}, u32[]{:S(2)}, u32[]{:S(2)}) async-start(bf16[4,1024,256]{2,1,0:T(8,128)(2,1)} %copy-done), calls=%async_computation.1 | async-start | bytes 4194304 | tf_op jit(solution)/shard_map/all_to_all | solution.py:245
  49.0 1.5 %collective-permute-done.3 = bf16[4,96,256]{2,1,0:T(8,128)(2,1)} collective-permute-done((bf16[4,96,256]{2,1,0:T(8,128)(2,1)S(1)}, bf16[4,96,256]{2,1,0:T(8,128)(2,1)}, u32[]{:S(2)}, u32[]{:S(2)}) %collective-permute-start.3) | collective-permute-done | bytes 196640 | tf_op jit(solution)/shard_map/ppermute | solution.py:268
  50.5 1.4 %fusion.6.after_ref = bf16[4,96,256]{2,1,0:T(8,128)(2,1)S(1)} fusion(bf16[4,96,256]{2,1,0:T(8,128)(2,1)} %collective-permute-done.9, bf16[4,96,256]{2,1,0:T(8,128)(2,1)} %collective-permute-done.4, bf16[4,96,256]{2,1,0:T(8,128)(2,1)} %collective-permute-done.3, bf16[4,96,256]{2,1,0:T(8,128)(2,1)} %collective-permute-done.2, ...), kind=kLoop, calls=%fused_computation.8 | loop fusion | flops 1376256 | bytes 1376256 | tf_op jit(solution)/shard_map/convert_element_type | solution.py:273
  52.0 2.1 %collective-permute-start.10 = (bf16[96,256]{1,0:T(8,128)(2,1)S(1)}, bf16[96,256]{1,0:T(8,128)(2,1)S(1)}, u32[]{:S(2)}, u32[]{:S(2)}) collective-permute-start(bf16[96,256]{1,0:T(8,128)(2,1)S(1)} %get-tuple-element.57), channel_id=1, source_target_pairs={{0,64},{4,68},{8,72},{12,76},{16,80},{20,84},{24,88},{28,92},{32,9... | collective-permute-start | bytes 147464 | tf_op jit(solution)/shard_map/ppermute | solution.py:280
  54.1 1.5 %collective-permute-start.12 = (bf16[96,256]{1,0:T(8,128)(2,1)S(1)}, bf16[96,256]{1,0:T(8,128)(2,1)S(1)}, u32[]{:S(2)}, u32[]{:S(2)}) collective-permute-start(bf16[96,256]{1,0:T(8,128)(2,1)S(1)} %get-tuple-element.58), channel_id=1, source_target_pairs={{0,192},{4,196},{8,200},{12,204},{16,208},{20,212},{24,216},{28,22... | collective-permute-start | bytes 147464 | tf_op jit(solution)/shard_map/ppermute | solution.py:280
  55.6 5.0 %collective-permute-start.11 = (bf16[96,256]{1,0:T(8,128)(2,1)S(1)}, bf16[96,256]{1,0:T(8,128)(2,1)S(1)}, u32[]{:S(2)}, u32[]{:S(2)}) collective-permute-start(bf16[96,256]{1,0:T(8,128)(2,1)S(1)} %get-tuple-element.59), channel_id=1, source_target_pairs={{0,128},{4,132},{8,136},{12,140},{16,144},{20,148},{24,152},{28,15... | collective-permute-start | bytes 147464 | tf_op jit(solution)/shard_map/ppermute | solution.py:280
  60.7 1.6 %collective-permute-start.19 = (bf16[768,256]{1,0:T(8,128)(2,1)S(1)}, bf16[768,256]{1,0:T(8,128)(2,1)S(1)}, u32[]{:S(2)}, u32[]{:S(2)}) collective-permute-start(bf16[768,256]{1,0:T(8,128)(2,1)S(1)} %bitcast.44), channel_id=1, source_target_pairs={{0,24},{4,28},{8,0},{12,4},{16,8},{20,12},{24,16},{28,20},{32,56},... | collective-permute-start | bytes 1179656 | tf_op jit(solution)/shard_map/ppermute | solution.py:277
  62.3 0.8 collective-permute-start.18
  63.2 0.8 fusion.18
  64.0 1.4 %collective-permute-start.13 = (bf16[96,256]{1,0:T(8,128)(2,1)S(1)}, bf16[96,256]{1,0:T(8,128)(2,1)S(1)}, u32[]{:S(2)}, u32[]{:S(2)}) collective-permute-start(bf16[96,256]{1,0:T(8,128)(2,1)S(1)} %get-tuple-element.47), channel_id=1, source_target_pairs={{0,32},{4,36},{8,40},{12,44},{16,48},{20,52},{24,56},{28,60},{32,0... | collective-permute-start | bytes 147464 | tf_op jit(solution)/shard_map/ppermute | solution.py:290
  65.4 1.9 %collective-permute-done.13 = bf16[96,256]{1,0:T(8,128)(2,1)S(1)} collective-permute-done((bf16[96,256]{1,0:T(8,128)(2,1)S(1)}, bf16[96,256]{1,0:T(8,128)(2,1)S(1)}, u32[]{:S(2)}, u32[]{:S(2)}) %collective-permute-start.13) | collective-permute-done | bytes 49184 | tf_op jit(solution)/shard_map/ppermute | solution.py:290
  67.2 4.5 %collective-permute-start.14 = (bf16[2,96,256]{2,1,0:T(8,128)(2,1)S(1)}, bf16[2,96,256]{2,1,0:T(8,128)(2,1)S(1)}, u32[]{:S(2)}, u32[]{:S(2)}) collective-permute-start(bf16[2,96,256]{2,1,0:T(8,128)(2,1)S(1)} %pad_maximum_fusion.refs_0_), channel_id=1, source_target_pairs={{0,128},{4,132},{8,136},{12,140},{16,144},{20,148},{24,152},{28,15... | collective-permute-start | bytes 294920 | tf_op jit(solution)/shard_map/ppermute | solution.py:291
  72.3 2.6 %collective-permute-done.14.refs_2_ = bf16[2,96,256]{2,1,0:T(8,128)(2,1)S(1)} collective-permute-done((bf16[2,96,256]{2,1,0:T(8,128)(2,1)S(1)}, bf16[2,96,256]{2,1,0:T(8,128)(2,1)S(1)}, u32[]{:S(2)}, u32[]{:S(2)}) %collective-permute-start.14) | collective-permute-done | bytes 98336 | tf_op jit(solution)/shard_map/ppermute | solution.py:291
  74.8 2.6 %collective-permute-start.15 = (bf16[2,96,256]{2,1,0:T(8,128)(2,1)S(1)}, bf16[2,96,256]{2,1,0:T(8,128)(2,1)}, u32[]{:S(2)}, u32[]{:S(2)}) collective-permute-start(bf16[2,96,256]{2,1,0:T(8,128)(2,1)S(1)} %pad_maximum_fusion.refs_0_), channel_id=1, source_target_pairs={{0,64},{4,68},{8,72},{12,76},{16,80},{20,84},{24,88},{28,92},{32,9... | collective-permute-start | bytes 294920 | tf_op jit(solution)/shard_map/ppermute | solution.py:291
  77.4 2.3 %collective-permute-done.16.refs_3_ = bf16[2,96,256]{2,1,0:T(8,128)(2,1)} collective-permute-done((bf16[2,96,256]{2,1,0:T(8,128)(2,1)S(1)}, bf16[2,96,256]{2,1,0:T(8,128)(2,1)}, u32[]{:S(2)}, u32[]{:S(2)}) %collective-permute-start.16) | collective-permute-done | bytes 98336 | tf_op jit(solution)/shard_map/ppermute | solution.py:291
  79.7 0.9 collective-permute-done.15.refs_1_
  80.6 1.8 %collect.1.refs_0_ = bf16[8,96,256]{2,1,0:T(8,128)(2,1)} custom-call(bf16[2,96,256]{2,1,0:T(8,128)(2,1)} %copy-done.7, bf16[2,96,256]{2,1,0:T(8,128)(2,1)} %collective-permute-done.15.refs_1_, bf16[2,96,256]{2,1,0:T(8,128)(2,1)} %copy-done.10, bf16[2,96,256]{2,1,0:T(8,128)(2,1)} %collective-permute-done.16.refs_3_), custom_call_target="tpu_custom_call" | custom-call | tf_op jit(solution)/shard_map/collect/pallas_call | solution.py:188
  82.5 0.9 collective-permute-done.17.refs_1_
  83.4 5.3 %collective-permute-start.20 = (bf16[768,256]{1,0:T(8,128)(2,1)S(1)}, bf16[768,256]{1,0:T(8,128)(2,1)S(1)}, u32[]{:S(2)}, u32[]{:S(2)}) collective-permute-start(bf16[768,256]{1,0:T(8,128)(2,1)S(1)} %bitcast.47), channel_id=1, source_target_pairs={{0,4},{4,0},{8,12},{12,8},{16,20},{20,16},{24,28},{28,24},{32,36},... | collective-permute-start | bytes 1179656 | tf_op jit(solution)/shard_map/ppermute | solution.py:295
  89.3 4.6 %collective-permute-start.26 = (bf16[8,96,256]{2,1,0:T(8,128)(2,1)}, bf16[8,96,256]{2,1,0:T(8,128)(2,1)S(1)}, u32[]{:S(2)}, u32[]{:S(2)}) collective-permute-start(bf16[8,96,256]{2,1,0:T(8,128)(2,1)} %collect.1.refs_0_), channel_id=1, source_target_pairs={{0,24},{4,28},{8,0},{12,4},{16,8},{20,12},{24,16},{28,20},{32,56},... | collective-permute-start | bytes 1179656 | tf_op jit(solution)/shard_map/ppermute | solution.py:294
  93.9 0.6 collective-permute-start.25
  94.5 0.7 collective-permute-start.24
  95.2 0.9 collective-permute-start.27
  96.1 6.1 %grad_input.1 = bf16[1024,1536]{1,0:T(8,128)(2,1)} custom-call(bf16[4,1024,256]{2,1,0:T(8,128)(2,1)S(1)} %all-to-all-done.1.act_ref, bf16[768,256]{1,0:T(8,128)(2,1)S(1)} %bitcast.48, bf16[768,256]{1,0:T(8,128)(2,1)} %collective-permute-done.17.refs_1_, bf16[768,256]{1,0:T(8,128)(2,1)S(1)} %collective-permute-done.18.refs_2_, ...), custom_call_target="tpu_custom_call" | custom-call | flops 3221225472 | bytes 8388608 | tf_op jit(solution)/shard_map/grad_input/pallas_call | solution.py:163
  102.2 8.3 %collective-permute-done.26.refs_6_ = bf16[8,96,256]{2,1,0:T(8,128)(2,1)S(1)} collective-permute-done((bf16[8,96,256]{2,1,0:T(8,128)(2,1)}, bf16[8,96,256]{2,1,0:T(8,128)(2,1)S(1)}, u32[]{:S(2)}, u32[]{:S(2)}) %collective-permute-start.26) | collective-permute-done | bytes 393248 | tf_op jit(solution)/shard_map/ppermute | solution.py:294
  110.5 4.5 %collective-permute-done.24.refs_2_ = bf16[8,96,256]{2,1,0:T(8,128)(2,1)S(1)} collective-permute-done((bf16[8,96,256]{2,1,0:T(8,128)(2,1)}, bf16[8,96,256]{2,1,0:T(8,128)(2,1)S(1)}, u32[]{:S(2)}, u32[]{:S(2)}) %collective-permute-start.24) | collective-permute-done | bytes 393248 | tf_op jit(solution)/shard_map/ppermute | solution.py:294
  116.0 0.8 collective-permute-done.28.refs_3_
  116.9 0.6 collective-permute-done.29.refs_5_
  117.4 0.6 collective-permute-done.30.refs_7_
  118.0 1.7 %place.1 = bf16[8,4,2,96,256]{4,3,2,1,0:T(8,128)(2,1)} custom-call(bf16[8,96,256]{2,1,0:T(8,128)(2,1)S(1)} %copy-done.1, bf16[8,96,256]{2,1,0:T(8,128)(2,1)S(1)} %collective-permute-done.27.refs_1_, bf16[8,96,256]{2,1,0:T(8,128)(2,1)S(1)} %collective-permute-done.24.refs_2_, bf16[8,96,256]{2,1,0:T(8,128)(2,1)S(1)} %collective-permute-done.28.refs_3_, ...), custom_call_target="tpu_custom_call" | custom-call | tf_op jit(solution)/shard_map/place/pallas_call | solution.py:212
  (55 shorter events, 3.2 us)
Async XLA Ops:
  1.5 14.2 %collective-permute-start = (bf16[96,256]{1,0:T(8,128)(2,1)S(1)}, bf16[96,256]{1,0:T(8,128)(2,1)S(1)}, u32[]{:S(2)}, u32[]{:S(2)}) collective-permute-start(bf16[96,256]{1,0:T(8,128)(2,1)S(1)} %convert.31), channel_id=1, source_target_pairs={{0,0},{1,8},{2,16},{3,24},{4,32},{5,40},{6,48},{7,56},{8,64},{9,72... | collective-permute-start | bytes 147464 | tf_op jit(solution)/shard_map/ppermute | solution.py:251
  15.7 17.4 %collective-permute-start.1 = (bf16[4,4,96,256]{3,2,1,0:T(8,128)(2,1)}, bf16[4,4,96,256]{3,2,1,0:T(8,128)(2,1)}, u32[]{:S(2)}, u32[]{:S(2)}) collective-permute-start(bf16[4,4,96,256]{3,2,1,0:T(8,128)(2,1)} %get-tuple-element.29), channel_id=1, source_target_pairs={{0,4},{4,0},{8,12},{12,8},{16,20},{20,16},{24,28},{28,24},{32,36},... | collective-permute-start | bytes 2359304 | tf_op jit(solution)/shard_map/ppermute | solution.py:259
  15.8 10.7 %collective-permute-start.5 = (bf16[4,4,96,256]{3,2,1,0:T(8,128)(2,1)}, bf16[4,4,96,256]{3,2,1,0:T(8,128)(2,1)S(1)}, u32[]{:S(2)}, u32[]{:S(2)}) collective-permute-start(bf16[4,4,96,256]{3,2,1,0:T(8,128)(2,1)} %get-tuple-element.31.after_ref), channel_id=1, source_target_pairs={{0,4},{4,0},{8,12},{12,8},{16,20},{20,16},{24,28},{28,24},{32,36},... | collective-permute-start | bytes 2359304 | tf_op jit(solution)/shard_map/ppermute | solution.py:259
  16.3 1.1 copy-start.2
  17.4 9.1 %copy-start.4 = (bf16[4,4,96,256]{3,2,1,0:T(8,128)(2,1)S(1)}, bf16[4,4,96,256]{3,2,1,0:T(8,128)(2,1)}, u32[]{:S(2)}) copy-start(bf16[4,4,96,256]{3,2,1,0:T(8,128)(2,1)} %get-tuple-element.30) | copy-start | bytes 2359300
  17.4 15.6 %copy-start.5 = (bf16[4,4,96,256]{3,2,1,0:T(8,128)(2,1)S(1)}, bf16[4,4,96,256]{3,2,1,0:T(8,128)(2,1)}, u32[]{:S(2)}) copy-start(bf16[4,4,96,256]{3,2,1,0:T(8,128)(2,1)} %get-tuple-element.26) | copy-start | bytes 2359300
  18.2 25.7 %copy-start.3 = (bf16[1024,256]{1,0:T(8,128)(2,1)S(1)}, bf16[1024,256]{1,0:T(8,128)(2,1)}, u32[]{:S(2)}) copy-start(bf16[1024,256]{1,0:T(8,128)(2,1)} %get-tuple-element.34.in_ref) | copy-start | bytes 1572868
  18.2 25.7 %all-to-all-start = ((bf16[8,96,256]{2,1,0:T(8,128)(2,1)}), bf16[8,96,256]{2,1,0:T(8,128)(2,1)S(1)}, u32[]{:S(2)}, u32[]{:S(2)}) async-start(bf16[8,96,256]{2,1,0:T(8,128)(2,1)} %spread.3), calls=%async_computation | async-start | bytes 786432 | tf_op jit(solution)/shard_map/all_to_all | solution.py:245
  26.7 11.1 %collective-permute-start.6 = (bf16[4,96,256]{2,1,0:T(8,128)(2,1)S(1)}, bf16[4,96,256]{2,1,0:T(8,128)(2,1)S(1)}, u32[]{:S(2)}, u32[]{:S(2)}) collective-permute-start(bf16[4,96,256]{2,1,0:T(8,128)(2,1)S(1)} %get-tuple-element.54), channel_id=1, source_target_pairs={{0,8},{4,12},{8,16},{12,20},{16,24},{20,28},{24,0},{28,4},{32,40},... | collective-permute-start | bytes 589832 | tf_op jit(solution)/shard_map/ppermute | solution.py:268
  28.8 10.5 %collective-permute-start.8 = (bf16[4,96,256]{2,1,0:T(8,128)(2,1)S(1)}, bf16[4,96,256]{2,1,0:T(8,128)(2,1)S(1)}, u32[]{:S(2)}, u32[]{:S(2)}) collective-permute-start(bf16[4,96,256]{2,1,0:T(8,128)(2,1)S(1)} %get-tuple-element.55), channel_id=1, source_target_pairs={{0,24},{4,28},{8,0},{12,4},{16,8},{20,12},{24,16},{28,20},{32,56},... | collective-permute-start | bytes 589832 | tf_op jit(solution)/shard_map/ppermute | solution.py:268
  32.0 10.0 %collective-permute-start.7 = (bf16[4,96,256]{2,1,0:T(8,128)(2,1)S(1)}, bf16[4,96,256]{2,1,0:T(8,128)(2,1)S(1)}, u32[]{:S(2)}, u32[]{:S(2)}) collective-permute-start(bf16[4,96,256]{2,1,0:T(8,128)(2,1)S(1)} %get-tuple-element.56), channel_id=1, source_target_pairs={{0,16},{4,20},{8,24},{12,28},{16,0},{20,4},{24,8},{28,12},{32,48},... | collective-permute-start | bytes 589832 | tf_op jit(solution)/shard_map/ppermute | solution.py:268
  35.1 13.9 %collective-permute-start.2 = (bf16[4,96,256]{2,1,0:T(8,128)(2,1)}, bf16[4,96,256]{2,1,0:T(8,128)(2,1)}, u32[]{:S(2)}, u32[]{:S(2)}) collective-permute-start(bf16[4,96,256]{2,1,0:T(8,128)(2,1)} %get-tuple-element.51), channel_id=1, source_target_pairs={{0,8},{4,12},{8,16},{12,20},{16,24},{20,28},{24,0},{28,4},{32,40},... | collective-permute-start | bytes 589832 | tf_op jit(solution)/shard_map/ppermute | solution.py:268
  35.9 13.1 %collective-permute-start.4 = (bf16[4,96,256]{2,1,0:T(8,128)(2,1)}, bf16[4,96,256]{2,1,0:T(8,128)(2,1)}, u32[]{:S(2)}, u32[]{:S(2)}) collective-permute-start(bf16[4,96,256]{2,1,0:T(8,128)(2,1)} %get-tuple-element.52), channel_id=1, source_target_pairs={{0,24},{4,28},{8,0},{12,4},{16,8},{20,12},{24,16},{28,20},{32,56},... | collective-permute-start | bytes 589832 | tf_op jit(solution)/shard_map/ppermute | solution.py:268
  37.8 12.7 %collective-permute-start.3 = (bf16[4,96,256]{2,1,0:T(8,128)(2,1)S(1)}, bf16[4,96,256]{2,1,0:T(8,128)(2,1)}, u32[]{:S(2)}, u32[]{:S(2)}) collective-permute-start(bf16[4,96,256]{2,1,0:T(8,128)(2,1)S(1)} %get-tuple-element.53), channel_id=1, source_target_pairs={{0,16},{4,20},{8,24},{12,28},{16,0},{20,4},{24,8},{28,12},{32,48},... | collective-permute-start | bytes 589832 | tf_op jit(solution)/shard_map/ppermute | solution.py:268
  42.8 7.7 %collective-permute-start.9 = (bf16[4,96,256]{2,1,0:T(8,128)(2,1)}, bf16[4,96,256]{2,1,0:T(8,128)(2,1)}, u32[]{:S(2)}, u32[]{:S(2)}) collective-permute-start(bf16[4,96,256]{2,1,0:T(8,128)(2,1)} %fusion.2), channel_id=1, source_target_pairs={{0,32},{4,36},{8,40},{12,44},{16,48},{20,52},{24,56},{28,60},{32,0... | collective-permute-start | bytes 589832 | tf_op jit(solution)/shard_map/ppermute | solution.py:271
  44.1 1.3 %copy-start = (bf16[4,1024,256]{2,1,0:T(8,128)(2,1)}, bf16[4,1024,256]{2,1,0:T(8,128)(2,1)S(1)}, u32[]{:S(2)}) copy-start(bf16[4,1024,256]{2,1,0:T(8,128)(2,1)S(1)} %spread.4) | copy-start | bytes 6291460
  45.4 32.0 %all-to-all-start.1 = ((bf16[4,1024,256]{2,1,0:T(8,128)(2,1)}), bf16[4,1024,256]{2,1,0:T(8,128)(2,1)S(1)}, u32[]{:S(2)}, u32[]{:S(2)}) async-start(bf16[4,1024,256]{2,1,0:T(8,128)(2,1)} %copy-done), calls=%async_computation.1 | async-start | bytes 4194304 | tf_op jit(solution)/shard_map/all_to_all | solution.py:245
  52.0 11.2 %collective-permute-start.10 = (bf16[96,256]{1,0:T(8,128)(2,1)S(1)}, bf16[96,256]{1,0:T(8,128)(2,1)S(1)}, u32[]{:S(2)}, u32[]{:S(2)}) collective-permute-start(bf16[96,256]{1,0:T(8,128)(2,1)S(1)} %get-tuple-element.57), channel_id=1, source_target_pairs={{0,64},{4,68},{8,72},{12,76},{16,80},{20,84},{24,88},{28,92},{32,9... | collective-permute-start | bytes 147464 | tf_op jit(solution)/shard_map/ppermute | solution.py:280
  54.1 9.1 %collective-permute-start.12 = (bf16[96,256]{1,0:T(8,128)(2,1)S(1)}, bf16[96,256]{1,0:T(8,128)(2,1)S(1)}, u32[]{:S(2)}, u32[]{:S(2)}) collective-permute-start(bf16[96,256]{1,0:T(8,128)(2,1)S(1)} %get-tuple-element.58), channel_id=1, source_target_pairs={{0,192},{4,196},{8,200},{12,204},{16,208},{20,212},{24,216},{28,22... | collective-permute-start | bytes 147464 | tf_op jit(solution)/shard_map/ppermute | solution.py:280
  55.6 7.6 %copy-start.6 = (f32[96,256]{1,0:T(8,128)S(1)}, f32[96,256]{1,0:T(8,128)}, u32[]{:S(2)}) copy-start(f32[96,256]{1,0:T(8,128)} %param.9) | copy-start | bytes 294916
  55.6 7.6 %copy-start.8 = (f32[96,256]{1,0:T(8,128)S(1)}, f32[96,256]{1,0:T(8,128)}, u32[]{:S(2)}) copy-start(f32[96,256]{1,0:T(8,128)} %param.10) | copy-start | bytes 294916
  55.6 7.6 %copy-start.9 = (f32[96,256]{1,0:T(8,128)S(1)}, f32[96,256]{1,0:T(8,128)}, u32[]{:S(2)}) copy-start(f32[96,256]{1,0:T(8,128)} %param.11) | copy-start | bytes 294916
  55.6 7.6 %collective-permute-start.11 = (bf16[96,256]{1,0:T(8,128)(2,1)S(1)}, bf16[96,256]{1,0:T(8,128)(2,1)S(1)}, u32[]{:S(2)}, u32[]{:S(2)}) collective-permute-start(bf16[96,256]{1,0:T(8,128)(2,1)S(1)} %get-tuple-element.59), channel_id=1, source_target_pairs={{0,128},{4,132},{8,136},{12,140},{16,144},{20,148},{24,152},{28,15... | collective-permute-start | bytes 147464 | tf_op jit(solution)/shard_map/ppermute | solution.py:280
  60.7 21.8 %collective-permute-start.19 = (bf16[768,256]{1,0:T(8,128)(2,1)S(1)}, bf16[768,256]{1,0:T(8,128)(2,1)S(1)}, u32[]{:S(2)}, u32[]{:S(2)}) collective-permute-start(bf16[768,256]{1,0:T(8,128)(2,1)S(1)} %bitcast.44), channel_id=1, source_target_pairs={{0,24},{4,28},{8,0},{12,4},{16,8},{20,12},{24,16},{28,20},{32,56},... | collective-permute-start | bytes 1179656 | tf_op jit(solution)/shard_map/ppermute | solution.py:277
  62.3 20.1 %collective-permute-start.18 = (bf16[768,256]{1,0:T(8,128)(2,1)S(1)}, bf16[768,256]{1,0:T(8,128)(2,1)S(1)}, u32[]{:S(2)}, u32[]{:S(2)}) collective-permute-start(bf16[768,256]{1,0:T(8,128)(2,1)S(1)} %bitcast.45), channel_id=1, source_target_pairs={{0,16},{4,20},{8,24},{12,28},{16,0},{20,4},{24,8},{28,12},{32,48},... | collective-permute-start | bytes 1179656 | tf_op jit(solution)/shard_map/ppermute | solution.py:277
  63.1 20.3 %collective-permute-start.17 = (bf16[768,256]{1,0:T(8,128)(2,1)S(1)}, bf16[768,256]{1,0:T(8,128)(2,1)}, u32[]{:S(2)}, u32[]{:S(2)}) collective-permute-start(bf16[768,256]{1,0:T(8,128)(2,1)S(1)} %bitcast.46), channel_id=1, source_target_pairs={{0,8},{4,12},{8,16},{12,20},{16,24},{20,28},{24,0},{28,4},{32,40},... | collective-permute-start | bytes 1179656 | tf_op jit(solution)/shard_map/ppermute | solution.py:277
  64.0 3.2 %collective-permute-start.13 = (bf16[96,256]{1,0:T(8,128)(2,1)S(1)}, bf16[96,256]{1,0:T(8,128)(2,1)S(1)}, u32[]{:S(2)}, u32[]{:S(2)}) collective-permute-start(bf16[96,256]{1,0:T(8,128)(2,1)S(1)} %get-tuple-element.47), channel_id=1, source_target_pairs={{0,32},{4,36},{8,40},{12,44},{16,48},{20,52},{24,56},{28,60},{32,0... | collective-permute-start | bytes 147464 | tf_op jit(solution)/shard_map/ppermute | solution.py:290
  67.2 13.4 %copy-start.7 = (bf16[2,96,256]{2,1,0:T(8,128)(2,1)}, bf16[2,96,256]{2,1,0:T(8,128)(2,1)S(1)}, u32[]{:S(2)}) copy-start(bf16[2,96,256]{2,1,0:T(8,128)(2,1)S(1)} %pad_maximum_fusion.refs_0_) | copy-start | bytes 294916
  67.2 7.6 %collective-permute-start.14 = (bf16[2,96,256]{2,1,0:T(8,128)(2,1)S(1)}, bf16[2,96,256]{2,1,0:T(8,128)(2,1)S(1)}, u32[]{:S(2)}, u32[]{:S(2)}) collective-permute-start(bf16[2,96,256]{2,1,0:T(8,128)(2,1)S(1)} %pad_maximum_fusion.refs_0_), channel_id=1, source_target_pairs={{0,128},{4,132},{8,136},{12,140},{16,144},{20,148},{24,152},{28,15... | collective-permute-start | bytes 294920 | tf_op jit(solution)/shard_map/ppermute | solution.py:291
  71.8 7.9 %collective-permute-start.16 = (bf16[2,96,256]{2,1,0:T(8,128)(2,1)S(1)}, bf16[2,96,256]{2,1,0:T(8,128)(2,1)}, u32[]{:S(2)}, u32[]{:S(2)}) collective-permute-start(bf16[2,96,256]{2,1,0:T(8,128)(2,1)S(1)} %pad_maximum_fusion.refs_0_), channel_id=1, source_target_pairs={{0,192},{4,196},{8,200},{12,204},{16,208},{20,212},{24,216},{28,22... | collective-permute-start | bytes 294920 | tf_op jit(solution)/shard_map/ppermute | solution.py:291
  74.8 5.8 %copy-start.10 = (bf16[2,96,256]{2,1,0:T(8,128)(2,1)}, bf16[2,96,256]{2,1,0:T(8,128)(2,1)S(1)}, u32[]{:S(2)}) copy-start(bf16[2,96,256]{2,1,0:T(8,128)(2,1)S(1)} %collective-permute-done.14.refs_2_) | copy-start | bytes 294916
  74.8 5.8 %collective-permute-start.15 = (bf16[2,96,256]{2,1,0:T(8,128)(2,1)S(1)}, bf16[2,96,256]{2,1,0:T(8,128)(2,1)}, u32[]{:S(2)}, u32[]{:S(2)}) collective-permute-start(bf16[2,96,256]{2,1,0:T(8,128)(2,1)S(1)} %pad_maximum_fusion.refs_0_), channel_id=1, source_target_pairs={{0,64},{4,68},{8,72},{12,76},{16,80},{20,84},{24,88},{28,92},{32,9... | collective-permute-start | bytes 294920 | tf_op jit(solution)/shard_map/ppermute | solution.py:291
  82.5 35.6 %copy-start.1 = (bf16[8,96,256]{2,1,0:T(8,128)(2,1)S(1)}, bf16[8,96,256]{2,1,0:T(8,128)(2,1)}, u32[]{:S(2)}) copy-start(bf16[8,96,256]{2,1,0:T(8,128)(2,1)} %collect.1.refs_0_) | copy-start | bytes 1179652
  83.4 10.5 %collective-permute-start.20 = (bf16[768,256]{1,0:T(8,128)(2,1)S(1)}, bf16[768,256]{1,0:T(8,128)(2,1)S(1)}, u32[]{:S(2)}, u32[]{:S(2)}) collective-permute-start(bf16[768,256]{1,0:T(8,128)(2,1)S(1)} %bitcast.47), channel_id=1, source_target_pairs={{0,4},{4,0},{8,12},{12,8},{16,20},{20,16},{24,28},{28,24},{32,36},... | collective-permute-start | bytes 1179656 | tf_op jit(solution)/shard_map/ppermute | solution.py:295
  88.7 5.8 %collective-permute-start.21 = (bf16[768,256]{1,0:T(8,128)(2,1)}, bf16[768,256]{1,0:T(8,128)(2,1)S(1)}, u32[]{:S(2)}, u32[]{:S(2)}) collective-permute-start(bf16[768,256]{1,0:T(8,128)(2,1)} %collective-permute-done.17.refs_1_), channel_id=1, source_target_pairs={{0,4},{4,0},{8,12},{12,8},{16,20},{20,16},{24,28},{28,24},{32,36},... | collective-permute-start | bytes 1179656 | tf_op jit(solution)/shard_map/ppermute | solution.py:295
  88.8 6.4 %collective-permute-start.22 = (bf16[768,256]{1,0:T(8,128)(2,1)S(1)}, bf16[768,256]{1,0:T(8,128)(2,1)S(1)}, u32[]{:S(2)}, u32[]{:S(2)}) collective-permute-start(bf16[768,256]{1,0:T(8,128)(2,1)S(1)} %collective-permute-done.18.refs_2_), channel_id=1, source_target_pairs={{0,4},{4,0},{8,12},{12,8},{16,20},{20,16},{24,28},{28,24},{32,36},... | collective-permute-start | bytes 1179656 | tf_op jit(solution)/shard_map/ppermute | solution.py:295
  89.2 6.9 %collective-permute-start.23 = (bf16[768,256]{1,0:T(8,128)(2,1)S(1)}, bf16[768,256]{1,0:T(8,128)(2,1)S(1)}, u32[]{:S(2)}, u32[]{:S(2)}) collective-permute-start(bf16[768,256]{1,0:T(8,128)(2,1)S(1)} %collective-permute-done.19.refs_3_), channel_id=1, source_target_pairs={{0,4},{4,0},{8,12},{12,8},{16,20},{20,16},{24,28},{28,24},{32,36},... | collective-permute-start | bytes 1179656 | tf_op jit(solution)/shard_map/ppermute | solution.py:295
  89.3 21.3 %collective-permute-start.26 = (bf16[8,96,256]{2,1,0:T(8,128)(2,1)}, bf16[8,96,256]{2,1,0:T(8,128)(2,1)S(1)}, u32[]{:S(2)}, u32[]{:S(2)}) collective-permute-start(bf16[8,96,256]{2,1,0:T(8,128)(2,1)} %collect.1.refs_0_), channel_id=1, source_target_pairs={{0,24},{4,28},{8,0},{12,4},{16,8},{20,12},{24,16},{28,20},{32,56},... | collective-permute-start | bytes 1179656 | tf_op jit(solution)/shard_map/ppermute | solution.py:294
  93.9 16.7 %collective-permute-start.25 = (bf16[8,96,256]{2,1,0:T(8,128)(2,1)}, bf16[8,96,256]{2,1,0:T(8,128)(2,1)S(1)}, u32[]{:S(2)}, u32[]{:S(2)}) collective-permute-start(bf16[8,96,256]{2,1,0:T(8,128)(2,1)} %collect.1.refs_0_), channel_id=1, source_target_pairs={{0,16},{4,20},{8,24},{12,28},{16,0},{20,4},{24,8},{28,12},{32,48},... | collective-permute-start | bytes 1179656 | tf_op jit(solution)/shard_map/ppermute | solution.py:294
  94.5 20.5 %collective-permute-start.24 = (bf16[8,96,256]{2,1,0:T(8,128)(2,1)}, bf16[8,96,256]{2,1,0:T(8,128)(2,1)S(1)}, u32[]{:S(2)}, u32[]{:S(2)}) collective-permute-start(bf16[8,96,256]{2,1,0:T(8,128)(2,1)} %collect.1.refs_0_), channel_id=1, source_target_pairs={{0,8},{4,12},{8,16},{12,20},{16,24},{20,28},{24,0},{28,4},{32,40},... | collective-permute-start | bytes 1179656 | tf_op jit(solution)/shard_map/ppermute | solution.py:294
  95.2 20.9 %collective-permute-start.27 = (bf16[8,96,256]{2,1,0:T(8,128)(2,1)}, bf16[8,96,256]{2,1,0:T(8,128)(2,1)S(1)}, u32[]{:S(2)}, u32[]{:S(2)}) collective-permute-start(bf16[8,96,256]{2,1,0:T(8,128)(2,1)} %collect.1.refs_0_), channel_id=1, source_target_pairs={{0,4},{4,0},{8,12},{12,8},{16,20},{20,16},{24,28},{28,24},{32,36},... | collective-permute-start | bytes 1179656 | tf_op jit(solution)/shard_map/ppermute | solution.py:300
  115.0 1.8 %collective-permute-start.28 = (bf16[8,96,256]{2,1,0:T(8,128)(2,1)S(1)}, bf16[8,96,256]{2,1,0:T(8,128)(2,1)S(1)}, u32[]{:S(2)}, u32[]{:S(2)}) collective-permute-start(bf16[8,96,256]{2,1,0:T(8,128)(2,1)S(1)} %collective-permute-done.24.refs_2_), channel_id=1, source_target_pairs={{0,4},{4,0},{8,12},{12,8},{16,20},{20,16},{24,28},{28,24},{32,36},... | collective-permute-start | bytes 1179656 | tf_op jit(solution)/shard_map/ppermute | solution.py:300
  115.5 1.9 %collective-permute-start.29 = (bf16[8,96,256]{2,1,0:T(8,128)(2,1)S(1)}, bf16[8,96,256]{2,1,0:T(8,128)(2,1)S(1)}, u32[]{:S(2)}, u32[]{:S(2)}) collective-permute-start(bf16[8,96,256]{2,1,0:T(8,128)(2,1)S(1)} %collective-permute-done.25.refs_4_), channel_id=1, source_target_pairs={{0,4},{4,0},{8,12},{12,8},{16,20},{20,16},{24,28},{28,24},{32,36},... | collective-permute-start | bytes 1179656 | tf_op jit(solution)/shard_map/ppermute | solution.py:300
  115.5 2.5 %collective-permute-start.30 = (bf16[8,96,256]{2,1,0:T(8,128)(2,1)S(1)}, bf16[8,96,256]{2,1,0:T(8,128)(2,1)S(1)}, u32[]{:S(2)}, u32[]{:S(2)}) collective-permute-start(bf16[8,96,256]{2,1,0:T(8,128)(2,1)S(1)} %collective-permute-done.26.refs_6_), channel_id=1, source_target_pairs={{0,4},{4,0},{8,12},{12,8},{16,20},{20,16},{24,28},{28,24},{32,36},... | collective-permute-start | bytes 1179656 | tf_op jit(solution)/shard_map/ppermute | solution.py:300

commit v4 on v3

--- a/solution.py
+++ b/solution.py
@@ -72,8 +72,9 @@
 
 
 def term_kernel(pre_hbm, cot_hbm, in_ref, *refs):
-    keeps, sends, act_ref = refs[0:2], refs[2:4], refs[4]
-    pre_ref, cot_ref, held, made, sems = refs[5:]
+    keeps, sends, act_ref, mark_ref = refs[0:2], refs[2:4], refs[4], refs[5]
+    pre_ref, cot_ref, held, made, sems = refs[6:]
+    mark_ref[...] = jnp.zeros_like(mark_ref)
     x, c, z = position()
 
     def fetch(side, j):
@@ -122,8 +123,9 @@
     return pl.pallas_call(
         term_kernel,
         in_specs=[hbm, hbm, hbm],
-        out_specs=[vmem] * 5,
-        out_shape=[out] * 4 + [jax.ShapeDtypeStruct((TOK, HID), BF16)],
+        out_specs=[vmem] * 6,
+        out_shape=[out] * 4
+        + [jax.ShapeDtypeStruct((TOK, HID), BF16), jax.ShapeDtypeStruct((16, 128), BF16)],
         scratch_shapes=[
             pltpu.VMEM((TOK, HID), BF16),
             pltpu.VMEM((TOK, HID), BF16),
@@ -139,7 +141,7 @@
     )(pre_act, grad_hidden, inputs)
 
 
-GI_ROWS = 256
+GI_ROWS = 512
 GI_COLS = D // NT
 
 
@@ -168,9 +170,7 @@
         out_shape=jax.ShapeDtypeStruct((TOK, GI_COLS), BF16),
         compiler_params=pltpu.CompilerParams(vmem_limit_bytes=40 * 2**20),
         cost_estimate=pl.CostEstimate(
-            flops=2 * TOK * GI_COLS * HID * NT,
-            bytes_accessed=2 * (TOK * HID * NT + GI_COLS * HID * NT + TOK * GI_COLS),
-            transcendentals=0,
+            flops=TOK * GI_COLS, bytes_accessed=TOK * GI_COLS, transcendentals=0
         ),
         name="grad_input",
     )(act_all, *mine, *other)
@@ -188,6 +188,7 @@
     return pl.pallas_call(
         collect_kernel,
         out_shape=jax.ShapeDtypeStruct((NZ, OWN, HID), BF16),
+        compiler_params=pltpu.CompilerParams(vmem_limit_bytes=4 * 2**20),
         name="collect",
     )(*pieces)
 
@@ -241,6 +242,23 @@
     )(block, after)
 
 
+def sum_kernel(*refs):
+    *parts, out_ref = refs
+    total = parts[0][...].astype(F32)
+    for part in parts[1:]:
+        total += part[...].astype(F32)
+    out_ref[...] = total.astype(BF16)
+
+
+def add_parts(*parts):
+    return pl.pallas_call(
+        sum_kernel,
+        out_shape=jax.ShapeDtypeStruct(parts[0].shape, BF16),
+        compiler_params=pltpu.CompilerParams(vmem_limit_bytes=8 * 2**20),
+        name="add_parts",
+    )(*parts)
+
+
 def swap_all(blocks, axis, groups=None):
     return lax.all_to_all(
         blocks, axis, split_axis=0, concat_axis=0, axis_index_groups=groups, tiled=True
@@ -249,10 +267,10 @@
 
 def local(inputs, pre_act, grad_hidden, master, moment_one, moment_two):
     w_own = lax.ppermute(master, ("dp", "tensor"), weight_route())
-    *made, act_grad = make_terms(pre_act, grad_hidden, inputs)
+    *made, act_grad, mark = make_terms(pre_act, grad_hidden, inputs)
     keeps, sends = made[:2], made[2:]
     sends[0], sends[1], w_own = tie(sends[0], sends[1], w_own)
-    w_spread = spread(w_own.astype(BF16), NZ, sends[1])
+    w_spread = spread(w_own.astype(BF16), NZ, mark)
 
     sums = [None, None]
     for side in (1, 0):
@@ -261,23 +279,26 @@
             (keeps[side][s].astype(F32) + recv[s].astype(F32)).astype(BF16) for s in range(NX)
         ]
     w_z = swap_all(w_spread, "dp", Z_GROUPS).reshape(HALF, HID)
-    totals = [None, None]
+    parts = [None, None]
     for side in (1, 0):
-        total = sums[side][0].astype(F32)
-        for s in range(1, NX):
-            total += lax.ppermute(sums[side][s], "dp", x_shift(s)).astype(F32)
-        totals[side] = total
-    ahead = totals[1].astype(BF16)
+        parts[side] = [sums[side][0]] + [
+            lax.ppermute(sums[side][s], "dp", x_shift(s)) for s in range(1, NX)
+        ]
+    ahead = add_parts(*parts[1])
     other = lax.ppermute(ahead, "dp", Z_SWAP)
-    act_all = swap_all(spread(act_grad, NT, w_z), "tensor").reshape(NT, TOK, HID)
-    total = (totals[0] + other.astype(F32)).astype(BF16)
-    total, w_z = tie(total, w_z)
-
-    w_z = spread(w_z, 1, total)[0]
-    w_mine = [w_z] + [lax.ppermute(w_z, "dp", x_shift(s)) for s in range(1, NX)]
+    w_next = spread(w_z, 1, ahead)[0]
+    act_all = swap_all(spread(act_grad, NT, w_next), "tensor").reshape(NT, TOK, HID)
+    total = parts[0][0].astype(F32)
+    for part in [*parts[0][1:], other]:
+        total += part.astype(F32)
+    total = total.astype(BF16)
+    w_near = [lax.ppermute(w_next, "dp", x_shift(s)) for s in (1, NX - 1)]
+    w_far = lax.ppermute(spread(w_z, 1, total)[0], "dp", x_shift(2))
+    others = [lax.ppermute(total[j], "dp", z_shift(2 * j)) for j in range(1, NJ)]
+    others[-1], *w_near = tie(others[-1], *w_near)
     grad = total[0].astype(F32)
-    for j in range(1, NJ):
-        grad += lax.ppermute(total[j], "dp", z_shift(2 * j)).astype(F32)
+    for part in others:
+        grad += part.astype(F32)
 
     new_one = 0.9 * moment_one + 0.1 * grad
     new_two = 0.999 * moment_two + 0.001 * grad * grad
@@ -290,14 +311,16 @@
     n_pair = jnp.stack([n_own, lax.ppermute(n_own, "dp", Z_SWAP)])
     n_z = [n_pair] + [lax.ppermute(n_pair, "dp", z_shift(2 * j)) for j in range(1, NJ)]
     n_z[2], act_all = tie(n_z[2], act_all)
-    n_z, *w_mine = tie(collect(n_z), *w_mine)
+    n_z, w_far = tie(collect(n_z), w_far)
     mine = [n_z] + [lax.ppermute(n_z, "dp", x_shift(s)) for s in range(1, NX)]
+    mine[1], w_z, w_far, *w_near = tie(mine[1], w_z, w_far, *w_near)
+    w_mine = [w_z, w_near[0], w_far, w_near[1]]
     w_other = [lax.ppermute(piece, "dp", CORE_SWAP) for piece in w_mine]
     grad_input = make_grad_input(act_all, w_mine, w_other)
-    grad_input, *mine[1:] = tie(grad_input, *mine[1:])
     pieces = []
     for piece in mine:
         pieces += [piece, lax.ppermute(piece, "dp", CORE_SWAP)]
+    grad_input, *pieces = tie(grad_input, *pieces)
     new_weights = make_weights(pieces)
     return (grad_input, new_master, new_one, new_two, new_weights)
 

time: 120 us -> 114 us (0.950)
  starting transfers between devices: 62.1 us -> 58.4 us
  waiting for transfers between devices: 28.4 us -> 25.8 us
    ppermute x4, starting transfers between devices: 5.88 us -> 9.02 us  [local(): w_other = [lax.ppermute(piece, 'dp', CORE_SWAP) for piece in w_mine]]
    ppermute x3, starting transfers between devices: 5.88 us -> 2.76 us  [local(): mine = [n_z] + [lax.ppermute(n_z, 'dp', x_shift(s)) for s in range(1, NX)]]
    ppermute x3, waiting for transfers between devices: 12.8 us -> 9.97 us  [local(): mine = [n_z] + [lax.ppermute(n_z, 'dp', x_shift(s)) for s in range(1, NX)]]
    ppermute x4, waiting for transfers between devices: 1.96 us -> 0.01 us  [local(): pieces += [piece, lax.ppermute(piece, 'dp', CORE_SWAP)]]
    ppermute x3, waiting for transfers between devices: 5.77 us -> 3.9 us  [local(): lax.ppermute(n_pair, 'dp', z_shift(2 * j))]
    ppermute x12, waiting for transfers between devices: 5.98 us -> 7.62 us  [the longest x6 4.57 us: local(): lax.ppermute(sums[side][s], 'dp', x_shift(s))]
    ppermute x3, starting transfers between devices: 7.59 us -> 6.06 us  [local(): lax.ppermute(n_pair, 'dp', z_shift(2 * j))]
    pallas_call x3 -> x4, Pallas kernels: 0.95 us -> 2.44 us  [spread(): pl.pallas_call(spread_kernel, in_specs=[pl.BlockSpec(memory_space=pltpu.V...]
  transfers between devices with their start and end apart: 33 -> 33, of which waited for: 13 -> 9; matrix products, arithmetic and copies ran while one was open for 4% -> 4% of each run, Pallas kernels for 15% -> 16%
where the time goes in v4:
time: 114 us
  starting transfers between devices  58.4 us (51%)
  waiting for transfers between devices  25.8 us (23%)
  Pallas kernels  20.4 us (18%)
  other arithmetic  5.9 us (5%)
  local copies, waits for them, and re-layouts  2.03 us (2%)
    all_to_all x2, starting transfers between devices, swap_all(): lax.all_to_all(blocks, axis, split_axis=0, concat_axis=0, axis_index_grou...  11.9 us
    ppermute x3, waiting for transfers between devices, local(): mine = [n_z] + [lax.ppermute(n_z, 'dp', x_shift(s)) for s in range(1, NX)]  9.97 us
    ppermute x6, starting transfers between devices, local(): lax.ppermute(sums[side][s], 'dp', x_shift(s))  9.66 us
    pallas_call x1, Pallas kernels, make_terms(): pl.pallas_call(term_kernel, in_specs=[hbm, hbm, hbm], out_specs=[vmem] *...  9.22 us
    ppermute x4, starting transfers between devices, local(): w_other = [lax.ppermute(piece, 'dp', CORE_SWAP) for piece in w_mine]  9.02 us
    ppermute x3, starting transfers between devices, local(): lax.ppermute(total[j], 'dp', z_shift(2 * j))  6.64 us
    ppermute x3, starting transfers between devices, local(): lax.ppermute(n_pair, 'dp', z_shift(2 * j))  6.06 us
    pallas_call x1, Pallas kernels, make_grad_input(): pl.pallas_call(input_kernel, grid=(TOK // GI_ROWS,), in_specs=[pl.BlockSp...  5.92 us
  transfers between devices with their start and end apart: 33, of which 9 were waited for; matrix products, arithmetic and copies ran while one was open for 4% of the time, Pallas kernels for 16%

profile of v4, /device:TPU:1, one launch (start us, length us, event | category | flops | bytes accessed | tf_op | source)
XLA Modules:
  0.0 113.5 jit_solution(17058169162171244376)
XLA Ops:
  0.6 0.9 convert.22
  1.5 4.9 %collective-permute-start = (bf16[96,256]{1,0:T(8,128)(2,1)S(1)}, bf16[96,256]{1,0:T(8,128)(2,1)S(1)}, u32[]{:S(2)}, u32[]{:S(2)}) collective-permute-start(bf16[96,256]{1,0:T(8,128)(2,1)S(1)} %convert.22), channel_id=1, source_target_pairs={{0,0},{1,8},{2,16},{3,24},{4,32},{5,40},{6,48},{7,56},{8,64},{9,72... | collective-permute-start | bytes 147464 | tf_op jit(solution)/shard_map/ppermute | solution.py:269
  6.5 9.2 %terms.1 = (bf16[4,4,96,256]{3,2,1,0:T(8,128)(2,1)}, bf16[4,4,96,256]{3,2,1,0:T(8,128)(2,1)}, bf16[4,4,96,256]{3,2,1,0:T(8,128)(2,1)}, bf16[4,4,96,256]{3,2,1,0:...) custom-call(bf16[1024,256]{1,0:T(8,128)(2,1)} %pre_hbm.1, bf16[1024,256]{1,0:T(8,128)(2,1)} %cot_hbm.1, ...), custom_call_target="tpu_custom_call" | custom-call | flops 3221225472 | bytes 15728640 | tf_op jit(solution)/shard_map/terms/pallas_call | solution.py:123
  15.8 0.5 collective-permute-start.1
  16.3 0.7 copy-done.2
  17.0 0.8 spread.4
  17.8 8.2 %all-to-all-start = ((bf16[8,96,256]{2,1,0:T(8,128)(2,1)}), bf16[8,96,256]{2,1,0:T(8,128)(2,1)S(1)}, u32[]{:S(2)}, u32[]{:S(2)}) async-start(bf16[8,96,256]{2,1,0:T(8,128)(2,1)} %spread.4), calls=%async_computation | async-start | bytes 786432 | tf_op jit(solution)/shard_map/all_to_all | solution.py:263
  26.0 1.7 %fusion.11 = (bf16[4,96,256]{2,1,0:T(8,128)(2,1)S(1)}, bf16[4,96,256]{2,1,0:T(8,128)(2,1)S(1)}, bf16[4,96,256]{2,1,0:T(8,128)(2,1)S(1)}, bf16[4,96,256]{2,1,0:T(8,128)(2,1)S(1)}) fusion(bf16[4,4,96,256]{3,2,1,0:T(8,128)(2,1)} %collective-permute-done.5, bf16[4,4,96,256]{3,2,1,0:T(8,128)(2,1)} %get-tuple-element.39), kind=kLoop, calls=%fused_computation.20 | loop fusion | flops 1572864 | bytes 2359296 | tf_op jit(solution)/shard_map/convert_element_type | solution.py:279
  27.7 2.2 %collective-permute-start.6 = (bf16[4,96,256]{2,1,0:T(8,128)(2,1)S(1)}, bf16[4,96,256]{2,1,0:T(8,128)(2,1)S(1)}, u32[]{:S(2)}, u32[]{:S(2)}) collective-permute-start(bf16[4,96,256]{2,1,0:T(8,128)(2,1)S(1)} %get-tuple-element.74), channel_id=1, source_target_pairs={{0,8},{4,12},{8,16},{12,20},{16,24},{20,28},{24,0},{28,4},{32,40},... | collective-permute-start | bytes 589832 | tf_op jit(solution)/shard_map/ppermute | solution.py:285
  29.9 4.2 %collective-permute-start.7 = (bf16[4,96,256]{2,1,0:T(8,128)(2,1)S(1)}, bf16[4,96,256]{2,1,0:T(8,128)(2,1)S(1)}, u32[]{:S(2)}, u32[]{:S(2)}) collective-permute-start(bf16[4,96,256]{2,1,0:T(8,128)(2,1)S(1)} %get-tuple-element.73), channel_id=1, source_target_pairs={{0,16},{4,20},{8,24},{12,28},{16,0},{20,4},{24,8},{28,12},{32,48},... | collective-permute-start | bytes 589832 | tf_op jit(solution)/shard_map/ppermute | solution.py:285
  34.1 0.3 collective-permute-start.8
  34.4 1.0 fusion.5
  35.4 3.0 %collective-permute-start.3 = (bf16[4,96,256]{2,1,0:T(8,128)(2,1)}, bf16[4,96,256]{2,1,0:T(8,128)(2,1)}, u32[]{:S(2)}, u32[]{:S(2)}) collective-permute-start(bf16[4,96,256]{2,1,0:T(8,128)(2,1)} %get-tuple-element.71), channel_id=1, source_target_pairs={{0,16},{4,20},{8,24},{12,28},{16,0},{20,4},{24,8},{28,12},{32,48},... | collective-permute-start | bytes 589832 | tf_op jit(solution)/shard_map/ppermute | solution.py:285
  38.4 4.6 %collective-permute-done.7.refs_2_ = bf16[4,96,256]{2,1,0:T(8,128)(2,1)S(1)} collective-permute-done((bf16[4,96,256]{2,1,0:T(8,128)(2,1)S(1)}, bf16[4,96,256]{2,1,0:T(8,128)(2,1)S(1)}, u32[]{:S(2)}, u32[]{:S(2)}) %collective-permute-start.7) | collective-permute-done | bytes 196640 | tf_op jit(solution)/shard_map/ppermute | solution.py:285
  43.1 1.2 %collective-permute-start.9 = (bf16[4,96,256]{2,1,0:T(8,128)(2,1)S(1)}, bf16[4,96,256]{2,1,0:T(8,128)(2,1)}, u32[]{:S(2)}, u32[]{:S(2)}) collective-permute-start(bf16[4,96,256]{2,1,0:T(8,128)(2,1)S(1)} %add_parts.1.after_ref), channel_id=1, source_target_pairs={{0,32},{4,36},{8,40},{12,44},{16,48},{20,52},{24,56},{28,60},{32,0... | collective-permute-start | bytes 589832 | tf_op jit(solution)/shard_map/ppermute | solution.py:288
  44.3 0.8 spread.5
  45.1 1.8 %collective-permute-start.13 = (bf16[768,256]{1,0:T(8,128)(2,1)}, bf16[768,256]{1,0:T(8,128)(2,1)S(1)}, u32[]{:S(2)}, u32[]{:S(2)}) collective-permute-start(bf16[768,256]{1,0:T(8,128)(2,1)} %bitcast.13.after_ref), channel_id=1, source_target_pairs={{0,8},{4,12},{8,16},{12,20},{16,24},{20,28},{24,0},{28,4},{32,40},... | collective-permute-start | bytes 1179656 | tf_op jit(solution)/shard_map/ppermute | solution.py:295
  47.1 1.3 %copy-done = bf16[4,1024,256]{2,1,0:T(8,128)(2,1)} copy-done((bf16[4,1024,256]{2,1,0:T(8,128)(2,1)}, bf16[4,1024,256]{2,1,0:T(8,128)(2,1)S(1)}, u32[]{:S(2)}) %copy-start) | copy-done | bytes 2097176
  48.4 3.6 %all-to-all-start.1 = ((bf16[4,1024,256]{2,1,0:T(8,128)(2,1)}), bf16[4,1024,256]{2,1,0:T(8,128)(2,1)S(1)}, u32[]{:S(2)}, u32[]{:S(2)}) async-start(bf16[4,1024,256]{2,1,0:T(8,128)(2,1)} %copy-done), calls=%async_computation.1 | async-start | bytes 4194304 | tf_op jit(solution)/shard_map/all_to_all | solution.py:263
  52.0 1.5 %collective-permute-start.14 = (bf16[768,256]{1,0:T(8,128)(2,1)}, bf16[768,256]{1,0:T(8,128)(2,1)S(1)}, u32[]{:S(2)}, u32[]{:S(2)}) collective-permute-start(bf16[768,256]{1,0:T(8,128)(2,1)} %bitcast.13.after_ref), channel_id=1, source_target_pairs={{0,24},{4,28},{8,0},{12,4},{16,8},{20,12},{24,16},{28,20},{32,56},... | collective-permute-start | bytes 1179656 | tf_op jit(solution)/shard_map/ppermute | solution.py:295
  53.6 1.5 %fusion.3.after_ref = bf16[4,96,256]{2,1,0:T(8,128)(2,1)S(1)} fusion(bf16[4,96,256]{2,1,0:T(8,128)(2,1)} %collective-permute-done.9, bf16[4,96,256]{2,1,0:T(8,128)(2,1)} %collective-permute-done.4, bf16[4,96,256]{2,1,0:T(8,128)(2,1)} %collective-permute-done.3, bf16[4,96,256]{2,1,0:T(8,128)(2,1)} %collective-permute-done.2, ...), kind=kLoop, calls=%fused_computation.4 | loop fusion | flops 1376256 | bytes 1376256 | tf_op jit(solution)/shard_map/convert_element_type | solution.py:294
  55.1 2.5 %collective-permute-start.12 = (bf16[96,256]{1,0:T(8,128)(2,1)S(1)}, bf16[96,256]{1,0:T(8,128)(2,1)S(1)}, u32[]{:S(2)}, u32[]{:S(2)}) collective-permute-start(bf16[96,256]{1,0:T(8,128)(2,1)S(1)} %get-tuple-element.77), channel_id=1, source_target_pairs={{0,192},{4,196},{8,200},{12,204},{16,208},{20,212},{24,216},{28,22... | collective-permute-start | bytes 147464 | tf_op jit(solution)/shard_map/ppermute | solution.py:297
  57.6 3.0 %collective-permute-start.11 = (bf16[96,256]{1,0:T(8,128)(2,1)S(1)}, bf16[96,256]{1,0:T(8,128)(2,1)S(1)}, u32[]{:S(2)}, u32[]{:S(2)}) collective-permute-start(bf16[96,256]{1,0:T(8,128)(2,1)S(1)} %get-tuple-element.78), channel_id=1, source_target_pairs={{0,128},{4,132},{8,136},{12,140},{16,144},{20,148},{24,152},{28,15... | collective-permute-start | bytes 147464 | tf_op jit(solution)/shard_map/ppermute | solution.py:297
  60.5 1.2 %collective-permute-start.10 = (bf16[96,256]{1,0:T(8,128)(2,1)S(1)}, bf16[96,256]{1,0:T(8,128)(2,1)S(1)}, u32[]{:S(2)}, u32[]{:S(2)}) collective-permute-start(bf16[96,256]{1,0:T(8,128)(2,1)S(1)} %get-tuple-element.76), channel_id=1, source_target_pairs={{0,64},{4,68},{8,72},{12,76},{16,80},{20,84},{24,88},{28,92},{32,9... | collective-permute-start | bytes 147464 | tf_op jit(solution)/shard_map/ppermute | solution.py:297
  61.7 0.8 spread.7
  62.5 0.8 collective-permute-start.19
  63.3 1.2 %collective-permute-done.11 = bf16[96,256]{1,0:T(8,128)(2,1)S(1)} collective-permute-done((bf16[96,256]{1,0:T(8,128)(2,1)S(1)}, bf16[96,256]{1,0:T(8,128)(2,1)S(1)}, u32[]{:S(2)}, u32[]{:S(2)}) %collective-permute-start.11) | collective-permute-done | bytes 49184 | tf_op jit(solution)/shard_map/ppermute | solution.py:297
  64.5 1.8 %collective-permute-done.10 = bf16[96,256]{1,0:T(8,128)(2,1)S(1)} collective-permute-done((bf16[96,256]{1,0:T(8,128)(2,1)S(1)}, bf16[96,256]{1,0:T(8,128)(2,1)S(1)}, u32[]{:S(2)}, u32[]{:S(2)}) %collective-permute-start.10) | collective-permute-done | bytes 49184 | tf_op jit(solution)/shard_map/ppermute | solution.py:297
  66.4 0.8 fusion.15
  67.1 3.2 %collective-permute-done.15 = bf16[96,256]{1,0:T(8,128)(2,1)S(1)} collective-permute-done((bf16[96,256]{1,0:T(8,128)(2,1)S(1)}, bf16[96,256]{1,0:T(8,128)(2,1)S(1)}, u32[]{:S(2)}, u32[]{:S(2)}) %collective-permute-start.15) | collective-permute-done | bytes 49184 | tf_op jit(solution)/shard_map/ppermute | solution.py:311
  70.4 2.5 %collective-permute-start.16 = (bf16[2,96,256]{2,1,0:T(8,128)(2,1)S(1)}, bf16[2,96,256]{2,1,0:T(8,128)(2,1)S(1)}, u32[]{:S(2)}, u32[]{:S(2)}) collective-permute-start(bf16[2,96,256]{2,1,0:T(8,128)(2,1)S(1)} %pad_maximum_fusion.refs_0_), channel_id=1, source_target_pairs={{0,128},{4,132},{8,136},{12,140},{16,144},{20,148},{24,152},{28,15... | collective-permute-start | bytes 294920 | tf_op jit(solution)/shard_map/ppermute | solution.py:312
  72.9 3.6 %collective-permute-start.18 = (bf16[2,96,256]{2,1,0:T(8,128)(2,1)S(1)}, bf16[2,96,256]{2,1,0:T(8,128)(2,1)}, u32[]{:S(2)}, u32[]{:S(2)}) collective-permute-start(bf16[2,96,256]{2,1,0:T(8,128)(2,1)S(1)} %pad_maximum_fusion.refs_0_), channel_id=1, source_target_pairs={{0,192},{4,196},{8,200},{12,204},{16,208},{20,212},{24,216},{28,22... | collective-permute-start | bytes 294920 | tf_op jit(solution)/shard_map/ppermute | solution.py:312
  76.5 3.0 %collective-permute-done.16.refs_2_ = bf16[2,96,256]{2,1,0:T(8,128)(2,1)S(1)} collective-permute-done((bf16[2,96,256]{2,1,0:T(8,128)(2,1)S(1)}, bf16[2,96,256]{2,1,0:T(8,128)(2,1)S(1)}, u32[]{:S(2)}, u32[]{:S(2)}) %collective-permute-start.16) | collective-permute-done | bytes 98336 | tf_op jit(solution)/shard_map/ppermute | solution.py:312
  79.5 0.9 collective-permute-done.17.refs_1_
  80.4 1.0 collect.1.refs_0_
  81.5 2.2 %collective-permute-start.27 = (bf16[8,96,256]{2,1,0:T(8,128)(2,1)S(1)}, bf16[8,96,256]{2,1,0:T(8,128)(2,1)S(1)}, u32[]{:S(2)}, u32[]{:S(2)}) collective-permute-start(bf16[8,96,256]{2,1,0:T(8,128)(2,1)S(1)} %collect.1.refs_0_), channel_id=1, source_target_pairs={{0,16},{4,20},{8,24},{12,28},{16,0},{20,4},{24,8},{28,12},{32,48},... | collective-permute-start | bytes 1179656 | tf_op jit(solution)/shard_map/ppermute | solution.py:315
  83.6 0.5 collective-permute-start.29
  84.1 10.0 %collective-permute-done.20.refs_2_ = bf16[8,96,256]{2,1,0:T(8,128)(2,1)S(1)} collective-permute-done((bf16[8,96,256]{2,1,0:T(8,128)(2,1)S(1)}, bf16[8,96,256]{2,1,0:T(8,128)(2,1)S(1)}, u32[]{:S(2)}, u32[]{:S(2)}) %collective-permute-start.20) | collective-permute-done | bytes 393248 | tf_op jit(solution)/shard_map/ppermute | solution.py:315
  94.1 8.5 %collective-permute-start.21 = (bf16[768,256]{1,0:T(8,128)(2,1)S(1)}, bf16[768,256]{1,0:T(8,128)(2,1)S(1)}, u32[]{:S(2)}, u32[]{:S(2)}) collective-permute-start(bf16[768,256]{1,0:T(8,128)(2,1)S(1)} %bitcast.44), channel_id=1, source_target_pairs={{0,4},{4,0},{8,12},{12,8},{16,20},{20,16},{24,28},{28,24},{32,36},... | collective-permute-start | bytes 1179656 | tf_op jit(solution)/shard_map/ppermute | solution.py:318
  102.6 0.5 collective-permute-start.23
  103.1 0.5 collective-permute-start.25
  103.6 0.3 collective-permute-done.21.refs_4_
  104.0 0.4 collective-permute-start.26
  104.3 0.8 collective-permute-done.22.refs_5_
  105.1 0.4 collective-permute-start.28
  105.5 0.2 collective-permute-start.30
  105.7 5.9 %grad_input.1 = bf16[1024,1536]{1,0:T(8,128)(2,1)} custom-call(bf16[4,1024,256]{2,1,0:T(8,128)(2,1)S(1)} %all-to-all-done.1.act_ref, bf16[768,256]{1,0:T(8,128)(2,1)S(1)} %bitcast.45, bf16[768,256]{1,0:T(8,128)(2,1)S(1)} %collective-permute-done.13.refs_1_, bf16[768,256]{1,0:T(8,128)(2,1)} %collective-permute-done.19.refs_2_, ...), custom_call_target="tpu_custom_call" | custom-call | flops 1572864 | bytes 1572864 | tf_op jit(solution)/shard_map/grad_input/pallas_call | solution.py:165
  111.6 1.7 %place.1 = bf16[8,4,2,96,256]{4,3,2,1,0:T(8,128)(2,1)} custom-call(bf16[8,96,256]{2,1,0:T(8,128)(2,1)S(1)} %collect.1.refs_0_, bf16[8,96,256]{2,1,0:T(8,128)(2,1)S(1)} %collective-permute-done.25.refs_1_, bf16[8,96,256]{2,1,0:T(8,128)(2,1)S(1)} %collective-permute-done.20.refs_2_, bf16[8,96,256]{2,1,0:T(8,128)(2,1)S(1)} %collective-permute-done.26.refs_3_, ...), custom_call_target="tpu_custom_call" | custom-call | tf_op jit(solution)/shard_map/place/pallas_call | solution.py:213
  (50 shorter events, 0.6 us)
Async XLA Ops:
  1.5 14.2 %collective-permute-start = (bf16[96,256]{1,0:T(8,128)(2,1)S(1)}, bf16[96,256]{1,0:T(8,128)(2,1)S(1)}, u32[]{:S(2)}, u32[]{:S(2)}) collective-permute-start(bf16[96,256]{1,0:T(8,128)(2,1)S(1)} %convert.22), channel_id=1, source_target_pairs={{0,0},{1,8},{2,16},{3,24},{4,32},{5,40},{6,48},{7,56},{8,64},{9,72... | collective-permute-start | bytes 147464 | tf_op jit(solution)/shard_map/ppermute | solution.py:269
  15.7 10.3 %collective-permute-start.5 = (bf16[4,4,96,256]{3,2,1,0:T(8,128)(2,1)}, bf16[4,4,96,256]{3,2,1,0:T(8,128)(2,1)}, u32[]{:S(2)}, u32[]{:S(2)}) collective-permute-start(bf16[4,4,96,256]{3,2,1,0:T(8,128)(2,1)} %get-tuple-element.40), channel_id=1, source_target_pairs={{0,4},{4,0},{8,12},{12,8},{16,20},{20,16},{24,28},{28,24},{32,36},... | collective-permute-start | bytes 2359304 | tf_op jit(solution)/shard_map/ppermute | solution.py:277
  15.8 18.6 %collective-permute-start.1 = (bf16[4,4,96,256]{3,2,1,0:T(8,128)(2,1)}, bf16[4,4,96,256]{3,2,1,0:T(8,128)(2,1)S(1)}, u32[]{:S(2)}, u32[]{:S(2)}) collective-permute-start(bf16[4,4,96,256]{3,2,1,0:T(8,128)(2,1)} %get-tuple-element.38), channel_id=1, source_target_pairs={{0,4},{4,0},{8,12},{12,8},{16,20},{20,16},{24,28},{28,24},{32,36},... | collective-permute-start | bytes 2359304 | tf_op jit(solution)/shard_map/ppermute | solution.py:277
  16.3 0.7 copy-start.2
  17.8 16.6 %copy-start.3 = (bf16[4,4,96,256]{3,2,1,0:T(8,128)(2,1)S(1)}, bf16[4,4,96,256]{3,2,1,0:T(8,128)(2,1)}, u32[]{:S(2)}) copy-start(bf16[4,4,96,256]{3,2,1,0:T(8,128)(2,1)} %get-tuple-element.35) | copy-start | bytes 2359300
  17.8 26.6 %all-to-all-start = ((bf16[8,96,256]{2,1,0:T(8,128)(2,1)}), bf16[8,96,256]{2,1,0:T(8,128)(2,1)S(1)}, u32[]{:S(2)}, u32[]{:S(2)}) async-start(bf16[8,96,256]{2,1,0:T(8,128)(2,1)} %spread.4), calls=%async_computation | async-start | bytes 786432 | tf_op jit(solution)/shard_map/all_to_all | solution.py:263
  27.7 10.7 %collective-permute-start.6 = (bf16[4,96,256]{2,1,0:T(8,128)(2,1)S(1)}, bf16[4,96,256]{2,1,0:T(8,128)(2,1)S(1)}, u32[]{:S(2)}, u32[]{:S(2)}) collective-permute-start(bf16[4,96,256]{2,1,0:T(8,128)(2,1)S(1)} %get-tuple-element.74), channel_id=1, source_target_pairs={{0,8},{4,12},{8,16},{12,20},{16,24},{20,28},{24,0},{28,4},{32,40},... | collective-permute-start | bytes 589832 | tf_op jit(solution)/shard_map/ppermute | solution.py:285
  29.9 13.1 %collective-permute-start.7 = (bf16[4,96,256]{2,1,0:T(8,128)(2,1)S(1)}, bf16[4,96,256]{2,1,0:T(8,128)(2,1)S(1)}, u32[]{:S(2)}, u32[]{:S(2)}) collective-permute-start(bf16[4,96,256]{2,1,0:T(8,128)(2,1)S(1)} %get-tuple-element.73), channel_id=1, source_target_pairs={{0,16},{4,20},{8,24},{12,28},{16,0},{20,4},{24,8},{28,12},{32,48},... | collective-permute-start | bytes 589832 | tf_op jit(solution)/shard_map/ppermute | solution.py:285
  34.1 8.9 %collective-permute-start.8 = (bf16[4,96,256]{2,1,0:T(8,128)(2,1)S(1)}, bf16[4,96,256]{2,1,0:T(8,128)(2,1)S(1)}, u32[]{:S(2)}, u32[]{:S(2)}) collective-permute-start(bf16[4,96,256]{2,1,0:T(8,128)(2,1)S(1)} %get-tuple-element.72), channel_id=1, source_target_pairs={{0,24},{4,28},{8,0},{12,4},{16,8},{20,12},{24,16},{28,20},{32,56},... | collective-permute-start | bytes 589832 | tf_op jit(solution)/shard_map/ppermute | solution.py:285
  34.4 10.7 %copy-start.4 = (bf16[4,4,96,256]{3,2,1,0:T(8,128)(2,1)}, bf16[4,4,96,256]{3,2,1,0:T(8,128)(2,1)S(1)}, u32[]{:S(2)}) copy-start(bf16[4,4,96,256]{3,2,1,0:T(8,128)(2,1)S(1)} %collective-permute-done.1) | copy-start | bytes 2359300
  35.4 16.6 %collective-permute-start.4 = (bf16[4,96,256]{2,1,0:T(8,128)(2,1)S(1)}, bf16[4,96,256]{2,1,0:T(8,128)(2,1)}, u32[]{:S(2)}, u32[]{:S(2)}) collective-permute-start(bf16[4,96,256]{2,1,0:T(8,128)(2,1)S(1)} %get-tuple-element.70), channel_id=1, source_target_pairs={{0,24},{4,28},{8,0},{12,4},{16,8},{20,12},{24,16},{28,20},{32,56},... | collective-permute-start | bytes 589832 | tf_op jit(solution)/shard_map/ppermute | solution.py:285
  35.4 18.1 %collective-permute-start.3 = (bf16[4,96,256]{2,1,0:T(8,128)(2,1)}, bf16[4,96,256]{2,1,0:T(8,128)(2,1)}, u32[]{:S(2)}, u32[]{:S(2)}) collective-permute-start(bf16[4,96,256]{2,1,0:T(8,128)(2,1)} %get-tuple-element.71), channel_id=1, source_target_pairs={{0,16},{4,20},{8,24},{12,28},{16,0},{20,4},{24,8},{28,12},{32,48},... | collective-permute-start | bytes 589832 | tf_op jit(solution)/shard_map/ppermute | solution.py:285
  38.4 15.2 %collective-permute-start.2 = (bf16[4,96,256]{2,1,0:T(8,128)(2,1)}, bf16[4,96,256]{2,1,0:T(8,128)(2,1)}, u32[]{:S(2)}, u32[]{:S(2)}) collective-permute-start(bf16[4,96,256]{2,1,0:T(8,128)(2,1)} %get-tuple-element.69), channel_id=1, source_target_pairs={{0,8},{4,12},{8,16},{12,20},{16,24},{20,28},{24,0},{28,4},{32,40},... | collective-permute-start | bytes 589832 | tf_op jit(solution)/shard_map/ppermute | solution.py:285
  43.1 10.5 %collective-permute-start.9 = (bf16[4,96,256]{2,1,0:T(8,128)(2,1)S(1)}, bf16[4,96,256]{2,1,0:T(8,128)(2,1)}, u32[]{:S(2)}, u32[]{:S(2)}) collective-permute-start(bf16[4,96,256]{2,1,0:T(8,128)(2,1)S(1)} %add_parts.1.after_ref), channel_id=1, source_target_pairs={{0,32},{4,36},{8,40},{12,44},{16,48},{20,52},{24,56},{28,60},{32,0... | collective-permute-start | bytes 589832 | tf_op jit(solution)/shard_map/ppermute | solution.py:288
  44.3 2.6 %copy-start.1 = (bf16[1024,256]{1,0:T(8,128)(2,1)S(1)}, bf16[1024,256]{1,0:T(8,128)(2,1)}, u32[]{:S(2)}) copy-start(bf16[1024,256]{1,0:T(8,128)(2,1)} %get-tuple-element.44.in_ref) | copy-start | bytes 1572868
  45.1 18.2 %collective-permute-start.13 = (bf16[768,256]{1,0:T(8,128)(2,1)}, bf16[768,256]{1,0:T(8,128)(2,1)S(1)}, u32[]{:S(2)}, u32[]{:S(2)}) collective-permute-start(bf16[768,256]{1,0:T(8,128)(2,1)} %bitcast.13.after_ref), channel_id=1, source_target_pairs={{0,8},{4,12},{8,16},{12,20},{16,24},{20,28},{24,0},{28,4},{32,40},... | collective-permute-start | bytes 1179656 | tf_op jit(solution)/shard_map/ppermute | solution.py:295
  47.1 1.3 %copy-start = (bf16[4,1024,256]{2,1,0:T(8,128)(2,1)}, bf16[4,1024,256]{2,1,0:T(8,128)(2,1)S(1)}, u32[]{:S(2)}) copy-start(bf16[4,1024,256]{2,1,0:T(8,128)(2,1)S(1)} %spread.6) | copy-start | bytes 6291460
  48.4 31.1 %all-to-all-start.1 = ((bf16[4,1024,256]{2,1,0:T(8,128)(2,1)}), bf16[4,1024,256]{2,1,0:T(8,128)(2,1)S(1)}, u32[]{:S(2)}, u32[]{:S(2)}) async-start(bf16[4,1024,256]{2,1,0:T(8,128)(2,1)} %copy-done), calls=%async_computation.1 | async-start | bytes 4194304 | tf_op jit(solution)/shard_map/all_to_all | solution.py:263
  52.0 11.3 %collective-permute-start.14 = (bf16[768,256]{1,0:T(8,128)(2,1)}, bf16[768,256]{1,0:T(8,128)(2,1)S(1)}, u32[]{:S(2)}, u32[]{:S(2)}) collective-permute-start(bf16[768,256]{1,0:T(8,128)(2,1)} %bitcast.13.after_ref), channel_id=1, source_target_pairs={{0,24},{4,28},{8,0},{12,4},{16,8},{20,12},{24,16},{28,20},{32,56},... | collective-permute-start | bytes 1179656 | tf_op jit(solution)/shard_map/ppermute | solution.py:295
  55.1 7.4 %collective-permute-start.12 = (bf16[96,256]{1,0:T(8,128)(2,1)S(1)}, bf16[96,256]{1,0:T(8,128)(2,1)S(1)}, u32[]{:S(2)}, u32[]{:S(2)}) collective-permute-start(bf16[96,256]{1,0:T(8,128)(2,1)S(1)} %get-tuple-element.77), channel_id=1, source_target_pairs={{0,192},{4,196},{8,200},{12,204},{16,208},{20,212},{24,216},{28,22... | collective-permute-start | bytes 147464 | tf_op jit(solution)/shard_map/ppermute | solution.py:297
  57.6 7.0 %collective-permute-start.11 = (bf16[96,256]{1,0:T(8,128)(2,1)S(1)}, bf16[96,256]{1,0:T(8,128)(2,1)S(1)}, u32[]{:S(2)}, u32[]{:S(2)}) collective-permute-start(bf16[96,256]{1,0:T(8,128)(2,1)S(1)} %get-tuple-element.78), channel_id=1, source_target_pairs={{0,128},{4,132},{8,136},{12,140},{16,144},{20,148},{24,152},{28,15... | collective-permute-start | bytes 147464 | tf_op jit(solution)/shard_map/ppermute | solution.py:297
  60.5 5.8 %copy-start.5 = (f32[96,256]{1,0:T(8,128)S(1)}, f32[96,256]{1,0:T(8,128)}, u32[]{:S(2)}) copy-start(f32[96,256]{1,0:T(8,128)} %param.9) | copy-start | bytes 294916
  60.5 5.8 %copy-start.6 = (f32[96,256]{1,0:T(8,128)S(1)}, f32[96,256]{1,0:T(8,128)}, u32[]{:S(2)}) copy-start(f32[96,256]{1,0:T(8,128)} %param.10) | copy-start | bytes 294916
  60.5 5.8 %copy-start.7 = (f32[96,256]{1,0:T(8,128)S(1)}, f32[96,256]{1,0:T(8,128)}, u32[]{:S(2)}) copy-start(f32[96,256]{1,0:T(8,128)} %param.11) | copy-start | bytes 294916
  60.5 5.8 %collective-permute-start.10 = (bf16[96,256]{1,0:T(8,128)(2,1)S(1)}, bf16[96,256]{1,0:T(8,128)(2,1)S(1)}, u32[]{:S(2)}, u32[]{:S(2)}) collective-permute-start(bf16[96,256]{1,0:T(8,128)(2,1)S(1)} %get-tuple-element.76), channel_id=1, source_target_pairs={{0,64},{4,68},{8,72},{12,76},{16,80},{20,84},{24,88},{28,92},{32,9... | collective-permute-start | bytes 147464 | tf_op jit(solution)/shard_map/ppermute | solution.py:297
  62.5 18.8 %collective-permute-start.19 = (bf16[768,256]{1,0:T(8,128)(2,1)}, bf16[768,256]{1,0:T(8,128)(2,1)}, u32[]{:S(2)}, u32[]{:S(2)}) collective-permute-start(bf16[768,256]{1,0:T(8,128)(2,1)} %bitcast.16), channel_id=1, source_target_pairs={{0,16},{4,20},{8,24},{12,28},{16,0},{20,4},{24,8},{28,12},{32,48},... | collective-permute-start | bytes 1179656 | tf_op jit(solution)/shard_map/ppermute | solution.py:296
  67.1 3.2 %collective-permute-start.15 = (bf16[96,256]{1,0:T(8,128)(2,1)S(1)}, bf16[96,256]{1,0:T(8,128)(2,1)S(1)}, u32[]{:S(2)}, u32[]{:S(2)}) collective-permute-start(bf16[96,256]{1,0:T(8,128)(2,1)S(1)} %get-tuple-element.65), channel_id=1, source_target_pairs={{0,32},{4,36},{8,40},{12,44},{16,48},{20,52},{24,56},{28,60},{32,0... | collective-permute-start | bytes 147464 | tf_op jit(solution)/shard_map/ppermute | solution.py:311
  70.4 9.1 %collective-permute-start.16 = (bf16[2,96,256]{2,1,0:T(8,128)(2,1)S(1)}, bf16[2,96,256]{2,1,0:T(8,128)(2,1)S(1)}, u32[]{:S(2)}, u32[]{:S(2)}) collective-permute-start(bf16[2,96,256]{2,1,0:T(8,128)(2,1)S(1)} %pad_maximum_fusion.refs_0_), channel_id=1, source_target_pairs={{0,128},{4,132},{8,136},{12,140},{16,144},{20,148},{24,152},{28,15... | collective-permute-start | bytes 294920 | tf_op jit(solution)/shard_map/ppermute | solution.py:312
  72.9 7.5 %collective-permute-start.17 = (bf16[2,96,256]{2,1,0:T(8,128)(2,1)S(1)}, bf16[2,96,256]{2,1,0:T(8,128)(2,1)}, u32[]{:S(2)}, u32[]{:S(2)}) collective-permute-start(bf16[2,96,256]{2,1,0:T(8,128)(2,1)S(1)} %pad_maximum_fusion.refs_0_), channel_id=1, source_target_pairs={{0,64},{4,68},{8,72},{12,76},{16,80},{20,84},{24,88},{28,92},{32,9... | collective-permute-start | bytes 294920 | tf_op jit(solution)/shard_map/ppermute | solution.py:312
  72.9 7.5 %collective-permute-start.18 = (bf16[2,96,256]{2,1,0:T(8,128)(2,1)S(1)}, bf16[2,96,256]{2,1,0:T(8,128)(2,1)}, u32[]{:S(2)}, u32[]{:S(2)}) collective-permute-start(bf16[2,96,256]{2,1,0:T(8,128)(2,1)S(1)} %pad_maximum_fusion.refs_0_), channel_id=1, source_target_pairs={{0,192},{4,196},{8,200},{12,204},{16,208},{20,212},{24,216},{28,22... | collective-permute-start | bytes 294920 | tf_op jit(solution)/shard_map/ppermute | solution.py:312
  81.4 12.7 %collective-permute-start.20 = (bf16[8,96,256]{2,1,0:T(8,128)(2,1)S(1)}, bf16[8,96,256]{2,1,0:T(8,128)(2,1)S(1)}, u32[]{:S(2)}, u32[]{:S(2)}) collective-permute-start(bf16[8,96,256]{2,1,0:T(8,128)(2,1)S(1)} %collect.1.refs_0_), channel_id=1, source_target_pairs={{0,8},{4,12},{8,16},{12,20},{16,24},{20,28},{24,0},{28,4},{32,40},... | collective-permute-start | bytes 1179656 | tf_op jit(solution)/shard_map/ppermute | solution.py:315
  81.5 21.7 %collective-permute-start.27 = (bf16[8,96,256]{2,1,0:T(8,128)(2,1)S(1)}, bf16[8,96,256]{2,1,0:T(8,128)(2,1)S(1)}, u32[]{:S(2)}, u32[]{:S(2)}) collective-permute-start(bf16[8,96,256]{2,1,0:T(8,128)(2,1)S(1)} %collect.1.refs_0_), channel_id=1, source_target_pairs={{0,16},{4,20},{8,24},{12,28},{16,0},{20,4},{24,8},{28,12},{32,48},... | collective-permute-start | bytes 1179656 | tf_op jit(solution)/shard_map/ppermute | solution.py:315
  83.6 19.5 %collective-permute-start.29 = (bf16[8,96,256]{2,1,0:T(8,128)(2,1)S(1)}, bf16[8,96,256]{2,1,0:T(8,128)(2,1)S(1)}, u32[]{:S(2)}, u32[]{:S(2)}) collective-permute-start(bf16[8,96,256]{2,1,0:T(8,128)(2,1)S(1)} %collect.1.refs_0_), channel_id=1, source_target_pairs={{0,24},{4,28},{8,0},{12,4},{16,8},{20,12},{24,16},{28,20},{32,56},... | collective-permute-start | bytes 1179656 | tf_op jit(solution)/shard_map/ppermute | solution.py:315
  94.1 9.9 %collective-permute-start.21 = (bf16[768,256]{1,0:T(8,128)(2,1)S(1)}, bf16[768,256]{1,0:T(8,128)(2,1)S(1)}, u32[]{:S(2)}, u32[]{:S(2)}) collective-permute-start(bf16[768,256]{1,0:T(8,128)(2,1)S(1)} %bitcast.44), channel_id=1, source_target_pairs={{0,4},{4,0},{8,12},{12,8},{16,20},{20,16},{24,28},{28,24},{32,36},... | collective-permute-start | bytes 1179656 | tf_op jit(solution)/shard_map/ppermute | solution.py:318
  102.6 2.5 %collective-permute-start.22 = (bf16[768,256]{1,0:T(8,128)(2,1)S(1)}, bf16[768,256]{1,0:T(8,128)(2,1)S(1)}, u32[]{:S(2)}, u32[]{:S(2)}) collective-permute-start(bf16[768,256]{1,0:T(8,128)(2,1)S(1)} %collective-permute-done.13.refs_1_), channel_id=1, source_target_pairs={{0,4},{4,0},{8,12},{12,8},{16,20},{20,16},{24,28},{28,24},{32,36},... | collective-permute-start | bytes 1179656 | tf_op jit(solution)/shard_map/ppermute | solution.py:318
  102.6 2.8 %collective-permute-start.23 = (bf16[768,256]{1,0:T(8,128)(2,1)}, bf16[768,256]{1,0:T(8,128)(2,1)S(1)}, u32[]{:S(2)}, u32[]{:S(2)}) collective-permute-start(bf16[768,256]{1,0:T(8,128)(2,1)} %collective-permute-done.19.refs_2_), channel_id=1, source_target_pairs={{0,4},{4,0},{8,12},{12,8},{16,20},{20,16},{24,28},{28,24},{32,36},... | collective-permute-start | bytes 1179656 | tf_op jit(solution)/shard_map/ppermute | solution.py:318
  103.1 2.5 %collective-permute-start.24 = (bf16[768,256]{1,0:T(8,128)(2,1)S(1)}, bf16[768,256]{1,0:T(8,128)(2,1)S(1)}, u32[]{:S(2)}, u32[]{:S(2)}) collective-permute-start(bf16[768,256]{1,0:T(8,128)(2,1)S(1)} %collective-permute-done.14.refs_3_), channel_id=1, source_target_pairs={{0,4},{4,0},{8,12},{12,8},{16,20},{20,16},{24,28},{28,24},{32,36},... | collective-permute-start | bytes 1179656 | tf_op jit(solution)/shard_map/ppermute | solution.py:318
  103.1 8.5 %collective-permute-start.25 = (bf16[8,96,256]{2,1,0:T(8,128)(2,1)S(1)}, bf16[8,96,256]{2,1,0:T(8,128)(2,1)S(1)}, u32[]{:S(2)}, u32[]{:S(2)}) collective-permute-start(bf16[8,96,256]{2,1,0:T(8,128)(2,1)S(1)} %collect.1.refs_0_), channel_id=1, source_target_pairs={{0,4},{4,0},{8,12},{12,8},{16,20},{20,16},{24,28},{28,24},{32,36},... | collective-permute-start | bytes 1179656 | tf_op jit(solution)/shard_map/ppermute | solution.py:322
  104.0 7.6 %collective-permute-start.26 = (bf16[8,96,256]{2,1,0:T(8,128)(2,1)S(1)}, bf16[8,96,256]{2,1,0:T(8,128)(2,1)S(1)}, u32[]{:S(2)}, u32[]{:S(2)}) collective-permute-start(bf16[8,96,256]{2,1,0:T(8,128)(2,1)S(1)} %collective-permute-done.20.refs_2_), channel_id=1, source_target_pairs={{0,4},{4,0},{8,12},{12,8},{16,20},{20,16},{24,28},{28,24},{32,36},... | collective-permute-start | bytes 1179656 | tf_op jit(solution)/shard_map/ppermute | solution.py:322
  105.1 6.5 %collective-permute-start.28 = (bf16[8,96,256]{2,1,0:T(8,128)(2,1)S(1)}, bf16[8,96,256]{2,1,0:T(8,128)(2,1)S(1)}, u32[]{:S(2)}, u32[]{:S(2)}) collective-permute-start(bf16[8,96,256]{2,1,0:T(8,128)(2,1)S(1)} %collective-permute-done.27.refs_4_), channel_id=1, source_target_pairs={{0,4},{4,0},{8,12},{12,8},{16,20},{20,16},{24,28},{28,24},{32,36},... | collective-permute-start | bytes 1179656 | tf_op jit(solution)/shard_map/ppermute | solution.py:322
  105.5 6.1 %collective-permute-start.30 = (bf16[8,96,256]{2,1,0:T(8,128)(2,1)S(1)}, bf16[8,96,256]{2,1,0:T(8,128)(2,1)S(1)}, u32[]{:S(2)}, u32[]{:S(2)}) collective-permute-start(bf16[8,96,256]{2,1,0:T(8,128)(2,1)S(1)} %collective-permute-done.29.refs_6_), channel_id=1, source_target_pairs={{0,4},{4,0},{8,12},{12,8},{16,20},{20,16},{24,28},{28,24},{32,36},... | collective-permute-start | bytes 1179656 | tf_op jit(solution)/shard_map/ppermute | solution.py:322

commit v5 on v4

--- a/solution.py
+++ b/solution.py
@@ -72,8 +72,8 @@
 
 
 def term_kernel(pre_hbm, cot_hbm, in_ref, *refs):
-    keeps, sends, act_ref, mark_ref = refs[0:2], refs[2:4], refs[4], refs[5]
-    pre_ref, cot_ref, held, made, sems = refs[6:]
+    keeps, sends, acts_hbm, mark_ref = refs[0:2], refs[2:4], refs[4], refs[5]
+    act_ref, pre_ref, cot_ref, held, made, sems = refs[6:]
     mark_ref[...] = jnp.zeros_like(mark_ref)
     x, c, z = position()
 
@@ -93,6 +93,11 @@
     cot_copy.wait()
     slope = gelu_slope(pre_ref[...].astype(F32))
     act_ref[...] = (cot_ref[...].astype(F32) * slope).astype(BF16)
+    act_copies = [
+        pltpu.make_async_copy(act_ref, acts_hbm.at[t], sems.at[NZ + 2 + t]) for t in range(NT)
+    ]
+    for copy in act_copies:
+        copy.start()
 
     for side in (1, 0):
 
@@ -115,6 +120,9 @@
                 keeps[side][s, j] = made[pl.ds(mine, OWN), :]
                 sends[side][s, j] = made[pl.ds(other, OWN), :]
 
+    for copy in act_copies:
+        copy.wait()
+
 
 def make_terms(pre_act, grad_hidden, inputs):
     out = jax.ShapeDtypeStruct((NX, NJ, OWN, HID), BF16)
@@ -123,15 +131,16 @@
     return pl.pallas_call(
         term_kernel,
         in_specs=[hbm, hbm, hbm],
-        out_specs=[vmem] * 6,
+        out_specs=[vmem] * 4 + [hbm, vmem],
         out_shape=[out] * 4
-        + [jax.ShapeDtypeStruct((TOK, HID), BF16), jax.ShapeDtypeStruct((16, 128), BF16)],
+        + [jax.ShapeDtypeStruct((NT, TOK, HID), BF16), jax.ShapeDtypeStruct((16, 128), BF16)],
         scratch_shapes=[
+            pltpu.VMEM((TOK, HID), BF16),
             pltpu.VMEM((TOK, HID), BF16),
             pltpu.VMEM((TOK, HID), BF16),
             pltpu.VMEM((NZ, TOK, ZROWS), BF16),
             pltpu.VMEM((ZROWS, HID), BF16),
-            pltpu.SemaphoreType.DMA((NZ + 2,)),
+            pltpu.SemaphoreType.DMA((NZ + 2 + NT,)),
         ],
         compiler_params=pltpu.CompilerParams(vmem_limit_bytes=56 * 2**20),
         cost_estimate=pl.CostEstimate(
@@ -267,7 +276,7 @@
 
 def local(inputs, pre_act, grad_hidden, master, moment_one, moment_two):
     w_own = lax.ppermute(master, ("dp", "tensor"), weight_route())
-    *made, act_grad, mark = make_terms(pre_act, grad_hidden, inputs)
+    *made, act_spread, mark = make_terms(pre_act, grad_hidden, inputs)
     keeps, sends = made[:2], made[2:]
     sends[0], sends[1], w_own = tie(sends[0], sends[1], w_own)
     w_spread = spread(w_own.astype(BF16), NZ, mark)
@@ -287,7 +296,8 @@
     ahead = add_parts(*parts[1])
     other = lax.ppermute(ahead, "dp", Z_SWAP)
     w_next = spread(w_z, 1, ahead)[0]
-    act_all = swap_all(spread(act_grad, NT, w_next), "tensor").reshape(NT, TOK, HID)
+    act_spread, w_next = tie(act_spread, w_next)
+    act_all = swap_all(act_spread, "tensor")
     total = parts[0][0].astype(F32)
     for part in [*parts[0][1:], other]:
         total += part.astype(F32)

time: 114 us -> 114 us (level)
  local copies, waits for them, and re-layouts: 2.03 us -> 0.72 us
    ppermute x1, starting transfers between devices: 0.01 us -> 1.63 us  [local(): n_pair = jnp.stack([n_own, lax.ppermute(n_own, 'dp', Z_SWAP)])]
    ppermute x1, waiting for transfers between devices: 3.23 us -> 1.77 us  [local(): n_pair = jnp.stack([n_own, lax.ppermute(n_own, 'dp', Z_SWAP)])]
    unnamed x16 -> x14, local copies, waits for them, and re-layouts: 2.02 us -> 0.71 us
    ppermute x3, starting transfers between devices: 6.64 us -> 7.81 us  [local(): lax.ppermute(total[j], 'dp', z_shift(2 * j))]
    pallas_call x4 -> x3, Pallas kernels: 2.44 us -> 2.32 us  [spread(): pl.pallas_call(spread_kernel, in_specs=[pl.BlockSpec(memory_space=pltpu.V...]
  transfers between devices with their start and end apart: 33 -> 33, of which waited for: 9 -> 11; matrix products, arithmetic and copies ran while one was open for 4% -> 4% of each run, Pallas kernels for 16% -> 17%
where the time goes in v5:
time: 114 us
  starting transfers between devices  59.4 us (52%)
  waiting for transfers between devices  26.4 us (23%)
  Pallas kernels  20.7 us (18%)
  other arithmetic  5.64 us (5%)
    all_to_all x2, starting transfers between devices, swap_all(): lax.all_to_all(blocks, axis, split_axis=0, concat_axis=0, axis_index_grou...  11.9 us
    ppermute x3, waiting for transfers between devices, local(): mine = [n_z] + [lax.ppermute(n_z, 'dp', x_shift(s)) for s in range(1, NX)]  10.8 us
    ppermute x6, starting transfers between devices, local(): lax.ppermute(sums[side][s], 'dp', x_shift(s))  9.66 us
    pallas_call x1, Pallas kernels, make_terms(): pl.pallas_call(term_kernel, in_specs=[hbm, hbm, hbm], out_specs=[vmem] *...  9.62 us
    ppermute x4, starting transfers between devices, local(): w_other = [lax.ppermute(piece, 'dp', CORE_SWAP) for piece in w_mine]  8.21 us
    ppermute x3, starting transfers between devices, local(): lax.ppermute(total[j], 'dp', z_shift(2 * j))  7.81 us
    ppermute x3, starting transfers between devices, local(): lax.ppermute(n_pair, 'dp', z_shift(2 * j))  6.27 us
    pallas_call x1, Pallas kernels, make_grad_input(): pl.pallas_call(input_kernel, grid=(TOK // GI_ROWS,), in_specs=[pl.BlockSp...  5.92 us
  transfers between devices with their start and end apart: 33, of which 11 were waited for; matrix products, arithmetic and copies ran while one was open for 4% of the time, Pallas kernels for 17%

profile of v5, /device:TPU:1, one launch (start us, length us, event | category | flops | bytes accessed | tf_op | source)
XLA Modules:
  0.0 113.7 jit_solution(16449644380775082935)
XLA Ops:
  0.6 0.9 convert.22
  1.5 4.9 %collective-permute-start = (bf16[96,256]{1,0:T(8,128)(2,1)S(1)}, bf16[96,256]{1,0:T(8,128)(2,1)S(1)}, u32[]{:S(2)}, u32[]{:S(2)}) collective-permute-start(bf16[96,256]{1,0:T(8,128)(2,1)S(1)} %convert.22), channel_id=1, source_target_pairs={{0,0},{1,8},{2,16},{3,24},{4,32},{5,40},{6,48},{7,56},{8,64},{9,72... | collective-permute-start | bytes 147464 | tf_op jit(solution)/shard_map/ppermute | solution.py:278
  6.5 9.6 %terms.1 = (bf16[4,4,96,256]{3,2,1,0:T(8,128)(2,1)}, bf16[4,4,96,256]{3,2,1,0:T(8,128)(2,1)}, bf16[4,4,96,256]{3,2,1,0:T(8,128)(2,1)}, bf16[4,4,96,256]{3,2,1,0:...) custom-call(bf16[1024,256]{1,0:T(8,128)(2,1)} %pre_hbm.1, bf16[1024,256]{1,0:T(8,128)(2,1)} %cot_hbm.1, ...), custom_call_target="tpu_custom_call" | custom-call | flops 3221225472 | bytes 15728640 | tf_op jit(solution)/shard_map/terms/pallas_call | solution.py:131
  16.2 0.5 collective-permute-start.1
  16.7 0.7 copy-done
  17.4 0.8 spread.3
  18.2 8.3 %all-to-all-start = ((bf16[8,96,256]{2,1,0:T(8,128)(2,1)}), bf16[8,96,256]{2,1,0:T(8,128)(2,1)S(1)}, u32[]{:S(2)}, u32[]{:S(2)}) async-start(bf16[8,96,256]{2,1,0:T(8,128)(2,1)} %spread.3), calls=%async_computation | async-start | bytes 786432 | tf_op jit(solution)/shard_map/all_to_all | solution.py:272
  26.4 1.4 %fusion.11 = (bf16[4,96,256]{2,1,0:T(8,128)(2,1)S(1)}, bf16[4,96,256]{2,1,0:T(8,128)(2,1)S(1)}, bf16[4,96,256]{2,1,0:T(8,128)(2,1)S(1)}, bf16[4,96,256]{2,1,0:T(8,128)(2,1)S(1)}) fusion(bf16[4,4,96,256]{3,2,1,0:T(8,128)(2,1)} %collective-permute-done.5, bf16[4,4,96,256]{3,2,1,0:T(8,128)(2,1)S(1)} %copy-done.3), kind=kLoop, calls=%fused_computation.20 | loop fusion | flops 1572864 | bytes 2359296 | tf_op jit(solution)/shard_map/convert_element_type | solution.py:288
  27.9 2.2 %collective-permute-start.6 = (bf16[4,96,256]{2,1,0:T(8,128)(2,1)S(1)}, bf16[4,96,256]{2,1,0:T(8,128)(2,1)S(1)}, u32[]{:S(2)}, u32[]{:S(2)}) collective-permute-start(bf16[4,96,256]{2,1,0:T(8,128)(2,1)S(1)} %get-tuple-element.78), channel_id=1, source_target_pairs={{0,8},{4,12},{8,16},{12,20},{16,24},{20,28},{24,0},{28,4},{32,40},... | collective-permute-start | bytes 589832 | tf_op jit(solution)/shard_map/ppermute | solution.py:294
  30.1 4.2 %collective-permute-start.7 = (bf16[4,96,256]{2,1,0:T(8,128)(2,1)S(1)}, bf16[4,96,256]{2,1,0:T(8,128)(2,1)S(1)}, u32[]{:S(2)}, u32[]{:S(2)}) collective-permute-start(bf16[4,96,256]{2,1,0:T(8,128)(2,1)S(1)} %get-tuple-element.77), channel_id=1, source_target_pairs={{0,16},{4,20},{8,24},{12,28},{16,0},{20,4},{24,8},{28,12},{32,48},... | collective-permute-start | bytes 589832 | tf_op jit(solution)/shard_map/ppermute | solution.py:294
  34.6 1.0 fusion.5
  35.6 3.0 %collective-permute-start.3 = (bf16[4,96,256]{2,1,0:T(8,128)(2,1)}, bf16[4,96,256]{2,1,0:T(8,128)(2,1)}, u32[]{:S(2)}, u32[]{:S(2)}) collective-permute-start(bf16[4,96,256]{2,1,0:T(8,128)(2,1)} %get-tuple-element.75), channel_id=1, source_target_pairs={{0,16},{4,20},{8,24},{12,28},{16,0},{20,4},{24,8},{28,12},{32,48},... | collective-permute-start | bytes 589832 | tf_op jit(solution)/shard_map/ppermute | solution.py:294
  38.6 4.6 %collective-permute-done.7.refs_2_ = bf16[4,96,256]{2,1,0:T(8,128)(2,1)S(1)} collective-permute-done((bf16[4,96,256]{2,1,0:T(8,128)(2,1)S(1)}, bf16[4,96,256]{2,1,0:T(8,128)(2,1)S(1)}, u32[]{:S(2)}, u32[]{:S(2)}) %collective-permute-start.7) | collective-permute-done | bytes 196640 | tf_op jit(solution)/shard_map/ppermute | solution.py:294
  43.3 1.2 %collective-permute-start.9 = (bf16[4,96,256]{2,1,0:T(8,128)(2,1)S(1)}, bf16[4,96,256]{2,1,0:T(8,128)(2,1)}, u32[]{:S(2)}, u32[]{:S(2)}) collective-permute-start(bf16[4,96,256]{2,1,0:T(8,128)(2,1)S(1)} %add_parts.1.after_ref), channel_id=1, source_target_pairs={{0,32},{4,36},{8,40},{12,44},{16,48},{20,52},{24,56},{28,60},{32,0... | collective-permute-start | bytes 589832 | tf_op jit(solution)/shard_map/ppermute | solution.py:297
  44.5 0.8 spread.4
  45.3 1.8 %collective-permute-start.13 = (bf16[768,256]{1,0:T(8,128)(2,1)}, bf16[768,256]{1,0:T(8,128)(2,1)S(1)}, u32[]{:S(2)}, u32[]{:S(2)}) collective-permute-start(bf16[768,256]{1,0:T(8,128)(2,1)} %bitcast.13), channel_id=1, source_target_pairs={{0,8},{4,12},{8,16},{12,20},{16,24},{20,28},{24,0},{28,4},{32,40},... | collective-permute-start | bytes 1179656 | tf_op jit(solution)/shard_map/ppermute | solution.py:305
  47.1 3.6 %all-to-all-start.1 = ((bf16[4,1024,256]{2,1,0:T(8,128)(2,1)}), bf16[4,1024,256]{2,1,0:T(8,128)(2,1)S(1)}, u32[]{:S(2)}, u32[]{:S(2)}) async-start(bf16[4,1024,256]{2,1,0:T(8,128)(2,1)} %get-tuple-element.48), calls=%async_computation.1 | async-start | bytes 4194304 | tf_op jit(solution)/shard_map/all_to_all | solution.py:272
  50.7 1.1 collective-permute-start.14
  51.9 0.5 collective-permute-done.2
  52.4 1.5 %fusion.3.after_ref = bf16[4,96,256]{2,1,0:T(8,128)(2,1)S(1)} fusion(bf16[4,96,256]{2,1,0:T(8,128)(2,1)} %collective-permute-done.9, bf16[4,96,256]{2,1,0:T(8,128)(2,1)} %collective-permute-done.4, bf16[4,96,256]{2,1,0:T(8,128)(2,1)} %collective-permute-done.3, bf16[4,96,256]{2,1,0:T(8,128)(2,1)} %collective-permute-done.2, ...), kind=kLoop, calls=%fused_computation.4 | loop fusion | flops 1376256 | bytes 1376256 | tf_op jit(solution)/shard_map/convert_element_type | solution.py:304
  53.9 3.6 %collective-permute-start.12 = (bf16[96,256]{1,0:T(8,128)(2,1)S(1)}, bf16[96,256]{1,0:T(8,128)(2,1)S(1)}, u32[]{:S(2)}, u32[]{:S(2)}) collective-permute-start(bf16[96,256]{1,0:T(8,128)(2,1)S(1)} %get-tuple-element.81), channel_id=1, source_target_pairs={{0,192},{4,196},{8,200},{12,204},{16,208},{20,212},{24,216},{28,22... | collective-permute-start | bytes 147464 | tf_op jit(solution)/shard_map/ppermute | solution.py:307
  57.6 2.1 %collective-permute-start.11 = (bf16[96,256]{1,0:T(8,128)(2,1)S(1)}, bf16[96,256]{1,0:T(8,128)(2,1)S(1)}, u32[]{:S(2)}, u32[]{:S(2)}) collective-permute-start(bf16[96,256]{1,0:T(8,128)(2,1)S(1)} %get-tuple-element.82), channel_id=1, source_target_pairs={{0,128},{4,132},{8,136},{12,140},{16,144},{20,148},{24,152},{28,15... | collective-permute-start | bytes 147464 | tf_op jit(solution)/shard_map/ppermute | solution.py:307
  59.6 2.1 %collective-permute-start.10 = (bf16[96,256]{1,0:T(8,128)(2,1)S(1)}, bf16[96,256]{1,0:T(8,128)(2,1)S(1)}, u32[]{:S(2)}, u32[]{:S(2)}) collective-permute-start(bf16[96,256]{1,0:T(8,128)(2,1)S(1)} %get-tuple-element.80), channel_id=1, source_target_pairs={{0,64},{4,68},{8,72},{12,76},{16,80},{20,84},{24,88},{28,92},{32,9... | collective-permute-start | bytes 147464 | tf_op jit(solution)/shard_map/ppermute | solution.py:307
  61.7 0.8 spread.5
  62.5 1.9 %collective-permute-done.11 = bf16[96,256]{1,0:T(8,128)(2,1)S(1)} collective-permute-done((bf16[96,256]{1,0:T(8,128)(2,1)S(1)}, bf16[96,256]{1,0:T(8,128)(2,1)S(1)}, u32[]{:S(2)}, u32[]{:S(2)}) %collective-permute-start.11) | collective-permute-done | bytes 49184 | tf_op jit(solution)/shard_map/ppermute | solution.py:307
  64.4 1.1 collective-permute-done.10
  65.5 0.8 fusion.15
  66.3 1.6 %collective-permute-start.15 = (bf16[96,256]{1,0:T(8,128)(2,1)S(1)}, bf16[96,256]{1,0:T(8,128)(2,1)S(1)}, u32[]{:S(2)}, u32[]{:S(2)}) collective-permute-start(bf16[96,256]{1,0:T(8,128)(2,1)S(1)} %get-tuple-element.69), channel_id=1, source_target_pairs={{0,32},{4,36},{8,40},{12,44},{16,48},{20,52},{24,56},{28,60},{32,0... | collective-permute-start | bytes 147464 | tf_op jit(solution)/shard_map/ppermute | solution.py:321
  67.9 1.8 %collective-permute-done.15 = bf16[96,256]{1,0:T(8,128)(2,1)S(1)} collective-permute-done((bf16[96,256]{1,0:T(8,128)(2,1)S(1)}, bf16[96,256]{1,0:T(8,128)(2,1)S(1)}, u32[]{:S(2)}, u32[]{:S(2)}) %collective-permute-start.15) | collective-permute-done | bytes 49184 | tf_op jit(solution)/shard_map/ppermute | solution.py:321
  69.7 2.7 %collective-permute-start.16 = (bf16[2,96,256]{2,1,0:T(8,128)(2,1)S(1)}, bf16[2,96,256]{2,1,0:T(8,128)(2,1)S(1)}, u32[]{:S(2)}, u32[]{:S(2)}) collective-permute-start(bf16[2,96,256]{2,1,0:T(8,128)(2,1)S(1)} %pad_maximum_fusion.refs_0_), channel_id=1, source_target_pairs={{0,128},{4,132},{8,136},{12,140},{16,144},{20,148},{24,152},{28,15... | collective-permute-start | bytes 294920 | tf_op jit(solution)/shard_map/ppermute | solution.py:322
  72.4 1.0 collective-permute-start.17
  73.5 2.5 %collective-permute-start.18 = (bf16[2,96,256]{2,1,0:T(8,128)(2,1)S(1)}, bf16[2,96,256]{2,1,0:T(8,128)(2,1)}, u32[]{:S(2)}, u32[]{:S(2)}) collective-permute-start(bf16[2,96,256]{2,1,0:T(8,128)(2,1)S(1)} %pad_maximum_fusion.refs_0_), channel_id=1, source_target_pairs={{0,192},{4,196},{8,200},{12,204},{16,208},{20,212},{24,216},{28,22... | collective-permute-start | bytes 294920 | tf_op jit(solution)/shard_map/ppermute | solution.py:322
  76.0 1.4 %collective-permute-done.16.refs_2_ = bf16[2,96,256]{2,1,0:T(8,128)(2,1)S(1)} collective-permute-done((bf16[2,96,256]{2,1,0:T(8,128)(2,1)S(1)}, bf16[2,96,256]{2,1,0:T(8,128)(2,1)S(1)}, u32[]{:S(2)}, u32[]{:S(2)}) %collective-permute-start.16) | collective-permute-done | bytes 98336 | tf_op jit(solution)/shard_map/ppermute | solution.py:322
  77.4 1.2 %collective-permute-done.17.refs_1_ = bf16[2,96,256]{2,1,0:T(8,128)(2,1)} collective-permute-done((bf16[2,96,256]{2,1,0:T(8,128)(2,1)S(1)}, bf16[2,96,256]{2,1,0:T(8,128)(2,1)}, u32[]{:S(2)}, u32[]{:S(2)}) %collective-permute-start.17) | collective-permute-done | bytes 98336 | tf_op jit(solution)/shard_map/ppermute | solution.py:322
  78.5 2.0 %collective-permute-done.18.refs_3_ = bf16[2,96,256]{2,1,0:T(8,128)(2,1)} collective-permute-done((bf16[2,96,256]{2,1,0:T(8,128)(2,1)S(1)}, bf16[2,96,256]{2,1,0:T(8,128)(2,1)}, u32[]{:S(2)}, u32[]{:S(2)}) %collective-permute-start.18) | collective-permute-done | bytes 98336 | tf_op jit(solution)/shard_map/ppermute | solution.py:322
  80.6 1.0 collect.1.refs_0_
  81.7 1.4 %collective-permute-start.27 = (bf16[8,96,256]{2,1,0:T(8,128)(2,1)S(1)}, bf16[8,96,256]{2,1,0:T(8,128)(2,1)S(1)}, u32[]{:S(2)}, u32[]{:S(2)}) collective-permute-start(bf16[8,96,256]{2,1,0:T(8,128)(2,1)S(1)} %collect.1.refs_0_), channel_id=1, source_target_pairs={{0,16},{4,20},{8,24},{12,28},{16,0},{20,4},{24,8},{28,12},{32,48},... | collective-permute-start | bytes 1179656 | tf_op jit(solution)/shard_map/ppermute | solution.py:325
  83.0 1.3 %collective-permute-start.29 = (bf16[8,96,256]{2,1,0:T(8,128)(2,1)S(1)}, bf16[8,96,256]{2,1,0:T(8,128)(2,1)S(1)}, u32[]{:S(2)}, u32[]{:S(2)}) collective-permute-start(bf16[8,96,256]{2,1,0:T(8,128)(2,1)S(1)} %collect.1.refs_0_), channel_id=1, source_target_pairs={{0,24},{4,28},{8,0},{12,4},{16,8},{20,12},{24,16},{28,20},{32,56},... | collective-permute-start | bytes 1179656 | tf_op jit(solution)/shard_map/ppermute | solution.py:325
  84.3 10.8 %collective-permute-done.20.refs_2_ = bf16[8,96,256]{2,1,0:T(8,128)(2,1)S(1)} collective-permute-done((bf16[8,96,256]{2,1,0:T(8,128)(2,1)S(1)}, bf16[8,96,256]{2,1,0:T(8,128)(2,1)S(1)}, u32[]{:S(2)}, u32[]{:S(2)}) %collective-permute-start.20) | collective-permute-done | bytes 393248 | tf_op jit(solution)/shard_map/ppermute | solution.py:325
  95.1 7.7 %collective-permute-start.21 = (bf16[768,256]{1,0:T(8,128)(2,1)S(1)}, bf16[768,256]{1,0:T(8,128)(2,1)S(1)}, u32[]{:S(2)}, u32[]{:S(2)}) collective-permute-start(bf16[768,256]{1,0:T(8,128)(2,1)S(1)} %bitcast.44), channel_id=1, source_target_pairs={{0,4},{4,0},{8,12},{12,8},{16,20},{20,16},{24,28},{28,24},{32,36},... | collective-permute-start | bytes 1179656 | tf_op jit(solution)/shard_map/ppermute | solution.py:328
  102.8 0.5 collective-permute-start.23
  103.4 0.5 collective-permute-start.25
  103.9 0.3 collective-permute-done.21.refs_4_
  104.2 0.4 collective-permute-start.26
  104.6 0.8 collective-permute-done.22.refs_5_
  105.3 0.4 collective-permute-start.28
  105.9 5.9 %grad_input.1 = bf16[1024,1536]{1,0:T(8,128)(2,1)} custom-call(bf16[4,1024,256]{2,1,0:T(8,128)(2,1)S(1)} %all-to-all-done.1.act_ref, bf16[768,256]{1,0:T(8,128)(2,1)S(1)} %bitcast.45, bf16[768,256]{1,0:T(8,128)(2,1)S(1)} %collective-permute-done.13.refs_1_, bf16[768,256]{1,0:T(8,128)(2,1)} %collective-permute-done.19.refs_2_, ...), custom_call_target="tpu_custom_call" | custom-call | flops 1572864 | bytes 1572864 | tf_op jit(solution)/shard_map/grad_input/pallas_call | solution.py:174
  111.8 1.7 %place.1 = bf16[8,4,2,96,256]{4,3,2,1,0:T(8,128)(2,1)} custom-call(bf16[8,96,256]{2,1,0:T(8,128)(2,1)S(1)} %collect.1.refs_0_, bf16[8,96,256]{2,1,0:T(8,128)(2,1)S(1)} %collective-permute-done.25.refs_1_, bf16[8,96,256]{2,1,0:T(8,128)(2,1)S(1)} %collective-permute-done.20.refs_2_, bf16[8,96,256]{2,1,0:T(8,128)(2,1)S(1)} %collective-permute-done.26.refs_3_, ...), custom_call_target="tpu_custom_call" | custom-call | tf_op jit(solution)/shard_map/place/pallas_call | solution.py:222
  (47 shorter events, 0.9 us)
Async XLA Ops:
  1.5 14.6 %collective-permute-start = (bf16[96,256]{1,0:T(8,128)(2,1)S(1)}, bf16[96,256]{1,0:T(8,128)(2,1)S(1)}, u32[]{:S(2)}, u32[]{:S(2)}) collective-permute-start(bf16[96,256]{1,0:T(8,128)(2,1)S(1)} %convert.22), channel_id=1, source_target_pairs={{0,0},{1,8},{2,16},{3,24},{4,32},{5,40},{6,48},{7,56},{8,64},{9,72... | collective-permute-start | bytes 147464 | tf_op jit(solution)/shard_map/ppermute | solution.py:278
  16.1 10.3 %collective-permute-start.5 = (bf16[4,4,96,256]{3,2,1,0:T(8,128)(2,1)}, bf16[4,4,96,256]{3,2,1,0:T(8,128)(2,1)}, u32[]{:S(2)}, u32[]{:S(2)}) collective-permute-start(bf16[4,4,96,256]{3,2,1,0:T(8,128)(2,1)} %get-tuple-element.42), channel_id=1, source_target_pairs={{0,4},{4,0},{8,12},{12,8},{16,20},{20,16},{24,28},{28,24},{32,36},... | collective-permute-start | bytes 2359304 | tf_op jit(solution)/shard_map/ppermute | solution.py:286
  16.2 18.3 %collective-permute-start.1 = (bf16[4,4,96,256]{3,2,1,0:T(8,128)(2,1)}, bf16[4,4,96,256]{3,2,1,0:T(8,128)(2,1)S(1)}, u32[]{:S(2)}, u32[]{:S(2)}) collective-permute-start(bf16[4,4,96,256]{3,2,1,0:T(8,128)(2,1)} %get-tuple-element.40), channel_id=1, source_target_pairs={{0,4},{4,0},{8,12},{12,8},{16,20},{20,16},{24,28},{28,24},{32,36},... | collective-permute-start | bytes 2359304 | tf_op jit(solution)/shard_map/ppermute | solution.py:286
  16.7 0.7 copy-start
  17.4 9.0 %copy-start.3 = (bf16[4,4,96,256]{3,2,1,0:T(8,128)(2,1)S(1)}, bf16[4,4,96,256]{3,2,1,0:T(8,128)(2,1)}, u32[]{:S(2)}) copy-start(bf16[4,4,96,256]{3,2,1,0:T(8,128)(2,1)} %get-tuple-element.41) | copy-start | bytes 2359300
  18.2 16.4 %copy-start.1 = (bf16[4,4,96,256]{3,2,1,0:T(8,128)(2,1)S(1)}, bf16[4,4,96,256]{3,2,1,0:T(8,128)(2,1)}, u32[]{:S(2)}) copy-start(bf16[4,4,96,256]{3,2,1,0:T(8,128)(2,1)} %get-tuple-element.37) | copy-start | bytes 2359300
  18.2 26.3 %all-to-all-start = ((bf16[8,96,256]{2,1,0:T(8,128)(2,1)}), bf16[8,96,256]{2,1,0:T(8,128)(2,1)S(1)}, u32[]{:S(2)}, u32[]{:S(2)}) async-start(bf16[8,96,256]{2,1,0:T(8,128)(2,1)} %spread.3), calls=%async_computation | async-start | bytes 786432 | tf_op jit(solution)/shard_map/all_to_all | solution.py:272
  27.9 10.7 %collective-permute-start.6 = (bf16[4,96,256]{2,1,0:T(8,128)(2,1)S(1)}, bf16[4,96,256]{2,1,0:T(8,128)(2,1)S(1)}, u32[]{:S(2)}, u32[]{:S(2)}) collective-permute-start(bf16[4,96,256]{2,1,0:T(8,128)(2,1)S(1)} %get-tuple-element.78), channel_id=1, source_target_pairs={{0,8},{4,12},{8,16},{12,20},{16,24},{20,28},{24,0},{28,4},{32,40},... | collective-permute-start | bytes 589832 | tf_op jit(solution)/shard_map/ppermute | solution.py:294
  30.1 13.1 %collective-permute-start.7 = (bf16[4,96,256]{2,1,0:T(8,128)(2,1)S(1)}, bf16[4,96,256]{2,1,0:T(8,128)(2,1)S(1)}, u32[]{:S(2)}, u32[]{:S(2)}) collective-permute-start(bf16[4,96,256]{2,1,0:T(8,128)(2,1)S(1)} %get-tuple-element.77), channel_id=1, source_target_pairs={{0,16},{4,20},{8,24},{12,28},{16,0},{20,4},{24,8},{28,12},{32,48},... | collective-permute-start | bytes 589832 | tf_op jit(solution)/shard_map/ppermute | solution.py:294
  34.3 8.9 %collective-permute-start.8 = (bf16[4,96,256]{2,1,0:T(8,128)(2,1)S(1)}, bf16[4,96,256]{2,1,0:T(8,128)(2,1)S(1)}, u32[]{:S(2)}, u32[]{:S(2)}) collective-permute-start(bf16[4,96,256]{2,1,0:T(8,128)(2,1)S(1)} %get-tuple-element.76), channel_id=1, source_target_pairs={{0,24},{4,28},{8,0},{12,4},{16,8},{20,12},{24,16},{28,20},{32,56},... | collective-permute-start | bytes 589832 | tf_op jit(solution)/shard_map/ppermute | solution.py:294
  34.5 10.7 %copy-start.2 = (bf16[4,4,96,256]{3,2,1,0:T(8,128)(2,1)}, bf16[4,4,96,256]{3,2,1,0:T(8,128)(2,1)S(1)}, u32[]{:S(2)}) copy-start(bf16[4,4,96,256]{3,2,1,0:T(8,128)(2,1)S(1)} %collective-permute-done.1) | copy-start | bytes 2359300
  35.6 15.1 %collective-permute-start.4 = (bf16[4,96,256]{2,1,0:T(8,128)(2,1)S(1)}, bf16[4,96,256]{2,1,0:T(8,128)(2,1)}, u32[]{:S(2)}, u32[]{:S(2)}) collective-permute-start(bf16[4,96,256]{2,1,0:T(8,128)(2,1)S(1)} %get-tuple-element.74), channel_id=1, source_target_pairs={{0,24},{4,28},{8,0},{12,4},{16,8},{20,12},{24,16},{28,20},{32,56},... | collective-permute-start | bytes 589832 | tf_op jit(solution)/shard_map/ppermute | solution.py:294
  35.6 16.3 %collective-permute-start.3 = (bf16[4,96,256]{2,1,0:T(8,128)(2,1)}, bf16[4,96,256]{2,1,0:T(8,128)(2,1)}, u32[]{:S(2)}, u32[]{:S(2)}) collective-permute-start(bf16[4,96,256]{2,1,0:T(8,128)(2,1)} %get-tuple-element.75), channel_id=1, source_target_pairs={{0,16},{4,20},{8,24},{12,28},{16,0},{20,4},{24,8},{28,12},{32,48},... | collective-permute-start | bytes 589832 | tf_op jit(solution)/shard_map/ppermute | solution.py:294
  38.6 13.8 %collective-permute-start.2 = (bf16[4,96,256]{2,1,0:T(8,128)(2,1)}, bf16[4,96,256]{2,1,0:T(8,128)(2,1)}, u32[]{:S(2)}, u32[]{:S(2)}) collective-permute-start(bf16[4,96,256]{2,1,0:T(8,128)(2,1)} %get-tuple-element.73), channel_id=1, source_target_pairs={{0,8},{4,12},{8,16},{12,20},{16,24},{20,28},{24,0},{28,4},{32,40},... | collective-permute-start | bytes 589832 | tf_op jit(solution)/shard_map/ppermute | solution.py:294
  43.3 9.1 %collective-permute-start.9 = (bf16[4,96,256]{2,1,0:T(8,128)(2,1)S(1)}, bf16[4,96,256]{2,1,0:T(8,128)(2,1)}, u32[]{:S(2)}, u32[]{:S(2)}) collective-permute-start(bf16[4,96,256]{2,1,0:T(8,128)(2,1)S(1)} %add_parts.1.after_ref), channel_id=1, source_target_pairs={{0,32},{4,36},{8,40},{12,44},{16,48},{20,52},{24,56},{28,60},{32,0... | collective-permute-start | bytes 589832 | tf_op jit(solution)/shard_map/ppermute | solution.py:297
  45.3 17.2 %collective-permute-start.13 = (bf16[768,256]{1,0:T(8,128)(2,1)}, bf16[768,256]{1,0:T(8,128)(2,1)S(1)}, u32[]{:S(2)}, u32[]{:S(2)}) collective-permute-start(bf16[768,256]{1,0:T(8,128)(2,1)} %bitcast.13), channel_id=1, source_target_pairs={{0,8},{4,12},{8,16},{12,20},{16,24},{20,28},{24,0},{28,4},{32,40},... | collective-permute-start | bytes 1179656 | tf_op jit(solution)/shard_map/ppermute | solution.py:305
  47.1 30.3 %all-to-all-start.1 = ((bf16[4,1024,256]{2,1,0:T(8,128)(2,1)}), bf16[4,1024,256]{2,1,0:T(8,128)(2,1)S(1)}, u32[]{:S(2)}, u32[]{:S(2)}) async-start(bf16[4,1024,256]{2,1,0:T(8,128)(2,1)} %get-tuple-element.48), calls=%async_computation.1 | async-start | bytes 4194304 | tf_op jit(solution)/shard_map/all_to_all | solution.py:272
  50.7 11.8 %collective-permute-start.14 = (bf16[768,256]{1,0:T(8,128)(2,1)}, bf16[768,256]{1,0:T(8,128)(2,1)S(1)}, u32[]{:S(2)}, u32[]{:S(2)}) collective-permute-start(bf16[768,256]{1,0:T(8,128)(2,1)} %bitcast.13), channel_id=1, source_target_pairs={{0,24},{4,28},{8,0},{12,4},{16,8},{20,12},{24,16},{28,20},{32,56},... | collective-permute-start | bytes 1179656 | tf_op jit(solution)/shard_map/ppermute | solution.py:305
  53.9 8.6 %collective-permute-start.12 = (bf16[96,256]{1,0:T(8,128)(2,1)S(1)}, bf16[96,256]{1,0:T(8,128)(2,1)S(1)}, u32[]{:S(2)}, u32[]{:S(2)}) collective-permute-start(bf16[96,256]{1,0:T(8,128)(2,1)S(1)} %get-tuple-element.81), channel_id=1, source_target_pairs={{0,192},{4,196},{8,200},{12,204},{16,208},{20,212},{24,216},{28,22... | collective-permute-start | bytes 147464 | tf_op jit(solution)/shard_map/ppermute | solution.py:307
  57.6 6.9 %collective-permute-start.11 = (bf16[96,256]{1,0:T(8,128)(2,1)S(1)}, bf16[96,256]{1,0:T(8,128)(2,1)S(1)}, u32[]{:S(2)}, u32[]{:S(2)}) collective-permute-start(bf16[96,256]{1,0:T(8,128)(2,1)S(1)} %get-tuple-element.82), channel_id=1, source_target_pairs={{0,128},{4,132},{8,136},{12,140},{16,144},{20,148},{24,152},{28,15... | collective-permute-start | bytes 147464 | tf_op jit(solution)/shard_map/ppermute | solution.py:307
  59.6 5.9 %copy-start.4 = (f32[96,256]{1,0:T(8,128)S(1)}, f32[96,256]{1,0:T(8,128)}, u32[]{:S(2)}) copy-start(f32[96,256]{1,0:T(8,128)} %param.9) | copy-start | bytes 294916
  59.6 5.9 %copy-start.5 = (f32[96,256]{1,0:T(8,128)S(1)}, f32[96,256]{1,0:T(8,128)}, u32[]{:S(2)}) copy-start(f32[96,256]{1,0:T(8,128)} %param.10) | copy-start | bytes 294916
  59.6 5.9 %copy-start.6 = (f32[96,256]{1,0:T(8,128)S(1)}, f32[96,256]{1,0:T(8,128)}, u32[]{:S(2)}) copy-start(f32[96,256]{1,0:T(8,128)} %param.11) | copy-start | bytes 294916
  59.6 5.9 %collective-permute-start.10 = (bf16[96,256]{1,0:T(8,128)(2,1)S(1)}, bf16[96,256]{1,0:T(8,128)(2,1)S(1)}, u32[]{:S(2)}, u32[]{:S(2)}) collective-permute-start(bf16[96,256]{1,0:T(8,128)(2,1)S(1)} %get-tuple-element.80), channel_id=1, source_target_pairs={{0,64},{4,68},{8,72},{12,76},{16,80},{20,84},{24,88},{28,92},{32,9... | collective-permute-start | bytes 147464 | tf_op jit(solution)/shard_map/ppermute | solution.py:307
  62.5 19.1 %collective-permute-start.19 = (bf16[768,256]{1,0:T(8,128)(2,1)}, bf16[768,256]{1,0:T(8,128)(2,1)}, u32[]{:S(2)}, u32[]{:S(2)}) collective-permute-start(bf16[768,256]{1,0:T(8,128)(2,1)} %bitcast.16), channel_id=1, source_target_pairs={{0,16},{4,20},{8,24},{12,28},{16,0},{20,4},{24,8},{28,12},{32,48},... | collective-permute-start | bytes 1179656 | tf_op jit(solution)/shard_map/ppermute | solution.py:306
  66.3 3.4 %collective-permute-start.15 = (bf16[96,256]{1,0:T(8,128)(2,1)S(1)}, bf16[96,256]{1,0:T(8,128)(2,1)S(1)}, u32[]{:S(2)}, u32[]{:S(2)}) collective-permute-start(bf16[96,256]{1,0:T(8,128)(2,1)S(1)} %get-tuple-element.69), channel_id=1, source_target_pairs={{0,32},{4,36},{8,40},{12,44},{16,48},{20,52},{24,56},{28,60},{32,0... | collective-permute-start | bytes 147464 | tf_op jit(solution)/shard_map/ppermute | solution.py:321
  69.7 7.6 %collective-permute-start.16 = (bf16[2,96,256]{2,1,0:T(8,128)(2,1)S(1)}, bf16[2,96,256]{2,1,0:T(8,128)(2,1)S(1)}, u32[]{:S(2)}, u32[]{:S(2)}) collective-permute-start(bf16[2,96,256]{2,1,0:T(8,128)(2,1)S(1)} %pad_maximum_fusion.refs_0_), channel_id=1, source_target_pairs={{0,128},{4,132},{8,136},{12,140},{16,144},{20,148},{24,152},{28,15... | collective-permute-start | bytes 294920 | tf_op jit(solution)/shard_map/ppermute | solution.py:322
  72.4 6.1 %collective-permute-start.17 = (bf16[2,96,256]{2,1,0:T(8,128)(2,1)S(1)}, bf16[2,96,256]{2,1,0:T(8,128)(2,1)}, u32[]{:S(2)}, u32[]{:S(2)}) collective-permute-start(bf16[2,96,256]{2,1,0:T(8,128)(2,1)S(1)} %pad_maximum_fusion.refs_0_), channel_id=1, source_target_pairs={{0,64},{4,68},{8,72},{12,76},{16,80},{20,84},{24,88},{28,92},{32,9... | collective-permute-start | bytes 294920 | tf_op jit(solution)/shard_map/ppermute | solution.py:322
  73.5 7.1 %collective-permute-start.18 = (bf16[2,96,256]{2,1,0:T(8,128)(2,1)S(1)}, bf16[2,96,256]{2,1,0:T(8,128)(2,1)}, u32[]{:S(2)}, u32[]{:S(2)}) collective-permute-start(bf16[2,96,256]{2,1,0:T(8,128)(2,1)S(1)} %pad_maximum_fusion.refs_0_), channel_id=1, source_target_pairs={{0,192},{4,196},{8,200},{12,204},{16,208},{20,212},{24,216},{28,22... | collective-permute-start | bytes 294920 | tf_op jit(solution)/shard_map/ppermute | solution.py:322
  81.6 13.5 %collective-permute-start.20 = (bf16[8,96,256]{2,1,0:T(8,128)(2,1)S(1)}, bf16[8,96,256]{2,1,0:T(8,128)(2,1)S(1)}, u32[]{:S(2)}, u32[]{:S(2)}) collective-permute-start(bf16[8,96,256]{2,1,0:T(8,128)(2,1)S(1)} %collect.1.refs_0_), channel_id=1, source_target_pairs={{0,8},{4,12},{8,16},{12,20},{16,24},{20,28},{24,0},{28,4},{32,40},... | collective-permute-start | bytes 1179656 | tf_op jit(solution)/shard_map/ppermute | solution.py:325
  81.7 21.7 %collective-permute-start.27 = (bf16[8,96,256]{2,1,0:T(8,128)(2,1)S(1)}, bf16[8,96,256]{2,1,0:T(8,128)(2,1)S(1)}, u32[]{:S(2)}, u32[]{:S(2)}) collective-permute-start(bf16[8,96,256]{2,1,0:T(8,128)(2,1)S(1)} %collect.1.refs_0_), channel_id=1, source_target_pairs={{0,16},{4,20},{8,24},{12,28},{16,0},{20,4},{24,8},{28,12},{32,48},... | collective-permute-start | bytes 1179656 | tf_op jit(solution)/shard_map/ppermute | solution.py:325
  83.0 20.3 %collective-permute-start.29 = (bf16[8,96,256]{2,1,0:T(8,128)(2,1)S(1)}, bf16[8,96,256]{2,1,0:T(8,128)(2,1)S(1)}, u32[]{:S(2)}, u32[]{:S(2)}) collective-permute-start(bf16[8,96,256]{2,1,0:T(8,128)(2,1)S(1)} %collect.1.refs_0_), channel_id=1, source_target_pairs={{0,24},{4,28},{8,0},{12,4},{16,8},{20,12},{24,16},{28,20},{32,56},... | collective-permute-start | bytes 1179656 | tf_op jit(solution)/shard_map/ppermute | solution.py:325
  95.1 9.0 %collective-permute-start.21 = (bf16[768,256]{1,0:T(8,128)(2,1)S(1)}, bf16[768,256]{1,0:T(8,128)(2,1)S(1)}, u32[]{:S(2)}, u32[]{:S(2)}) collective-permute-start(bf16[768,256]{1,0:T(8,128)(2,1)S(1)} %bitcast.44), channel_id=1, source_target_pairs={{0,4},{4,0},{8,12},{12,8},{16,20},{20,16},{24,28},{28,24},{32,36},... | collective-permute-start | bytes 1179656 | tf_op jit(solution)/shard_map/ppermute | solution.py:328
  102.8 2.5 %collective-permute-start.22 = (bf16[768,256]{1,0:T(8,128)(2,1)S(1)}, bf16[768,256]{1,0:T(8,128)(2,1)S(1)}, u32[]{:S(2)}, u32[]{:S(2)}) collective-permute-start(bf16[768,256]{1,0:T(8,128)(2,1)S(1)} %collective-permute-done.13.refs_1_), channel_id=1, source_target_pairs={{0,4},{4,0},{8,12},{12,8},{16,20},{20,16},{24,28},{28,24},{32,36},... | collective-permute-start | bytes 1179656 | tf_op jit(solution)/shard_map/ppermute | solution.py:328
  102.8 2.8 %collective-permute-start.23 = (bf16[768,256]{1,0:T(8,128)(2,1)}, bf16[768,256]{1,0:T(8,128)(2,1)S(1)}, u32[]{:S(2)}, u32[]{:S(2)}) collective-permute-start(bf16[768,256]{1,0:T(8,128)(2,1)} %collective-permute-done.19.refs_2_), channel_id=1, source_target_pairs={{0,4},{4,0},{8,12},{12,8},{16,20},{20,16},{24,28},{28,24},{32,36},... | collective-permute-start | bytes 1179656 | tf_op jit(solution)/shard_map/ppermute | solution.py:328
  103.3 2.5 %collective-permute-start.24 = (bf16[768,256]{1,0:T(8,128)(2,1)S(1)}, bf16[768,256]{1,0:T(8,128)(2,1)S(1)}, u32[]{:S(2)}, u32[]{:S(2)}) collective-permute-start(bf16[768,256]{1,0:T(8,128)(2,1)S(1)} %collective-permute-done.14.refs_3_), channel_id=1, source_target_pairs={{0,4},{4,0},{8,12},{12,8},{16,20},{20,16},{24,28},{28,24},{32,36},... | collective-permute-start | bytes 1179656 | tf_op jit(solution)/shard_map/ppermute | solution.py:328
  103.4 8.5 %collective-permute-start.25 = (bf16[8,96,256]{2,1,0:T(8,128)(2,1)S(1)}, bf16[8,96,256]{2,1,0:T(8,128)(2,1)S(1)}, u32[]{:S(2)}, u32[]{:S(2)}) collective-permute-start(bf16[8,96,256]{2,1,0:T(8,128)(2,1)S(1)} %collect.1.refs_0_), channel_id=1, source_target_pairs={{0,4},{4,0},{8,12},{12,8},{16,20},{20,16},{24,28},{28,24},{32,36},... | collective-permute-start | bytes 1179656 | tf_op jit(solution)/shard_map/ppermute | solution.py:332
  104.2 7.6 %collective-permute-start.26 = (bf16[8,96,256]{2,1,0:T(8,128)(2,1)S(1)}, bf16[8,96,256]{2,1,0:T(8,128)(2,1)S(1)}, u32[]{:S(2)}, u32[]{:S(2)}) collective-permute-start(bf16[8,96,256]{2,1,0:T(8,128)(2,1)S(1)} %collective-permute-done.20.refs_2_), channel_id=1, source_target_pairs={{0,4},{4,0},{8,12},{12,8},{16,20},{20,16},{24,28},{28,24},{32,36},... | collective-permute-start | bytes 1179656 | tf_op jit(solution)/shard_map/ppermute | solution.py:332
  105.3 6.5 %collective-permute-start.28 = (bf16[8,96,256]{2,1,0:T(8,128)(2,1)S(1)}, bf16[8,96,256]{2,1,0:T(8,128)(2,1)S(1)}, u32[]{:S(2)}, u32[]{:S(2)}) collective-permute-start(bf16[8,96,256]{2,1,0:T(8,128)(2,1)S(1)} %collective-permute-done.27.refs_4_), channel_id=1, source_target_pairs={{0,4},{4,0},{8,12},{12,8},{16,20},{20,16},{24,28},{28,24},{32,36},... | collective-permute-start | bytes 1179656 | tf_op jit(solution)/shard_map/ppermute | solution.py:332
  105.7 6.1 %collective-permute-start.30 = (bf16[8,96,256]{2,1,0:T(8,128)(2,1)S(1)}, bf16[8,96,256]{2,1,0:T(8,128)(2,1)S(1)}, u32[]{:S(2)}, u32[]{:S(2)}) collective-permute-start(bf16[8,96,256]{2,1,0:T(8,128)(2,1)S(1)} %collective-permute-done.29.refs_6_), channel_id=1, source_target_pairs={{0,4},{4,0},{8,12},{12,8},{16,20},{20,16},{24,28},{28,24},{32,36},... | collective-permute-start | bytes 1179656 | tf_op jit(solution)/shard_map/ppermute | solution.py:332
